TPU v7x, 32 devices: a whole 2x2x4 slice. The times are simulated.
32 devices in a mesh: dp: 32 (over z, y, x, core).
Axes of the slice: x: 2, y: 2, z: 4, core: 2. Of those that a mesh axis runs over, the one named last changes fastest.
Arguments:
- tokens: bfloat16 [16384, 1024], P('dp'), may hold values from -6 to 6
- cotangent: bfloat16 [16384, 1024], P('dp'), may hold values from -16 to 16
- route: int32 [32, 512], P('dp'), may hold values from 0 to 511, as said below
- lengths: int32 [64, 4], P('dp'), may hold values from 1 to 192, 256 in all within a row
- attn_gain: bfloat16 [1024], P('dp'), may hold values from 0.099609375 to 1.8984375
- w_query: bfloat16 [1024, 1024], P('dp'), may hold values from -0.1875 to 0.1875
- key_weight: bfloat16 [1024, 512], P('dp'), may hold values from -0.1875 to 0.1875
- value_weight: bfloat16 [1024, 512], P('dp'), may hold values from -0.1875 to 0.1875
- query_gain: bfloat16 [64], replicated, may hold values from 0.099609375 to 1.8984375
- key_norm_gain: bfloat16 [64], replicated, may hold values from 0.099609375 to 1.8984375
- w_out: bfloat16 [1024, 1024], P('dp'), may hold values from -1 to 1
- ffn_gain: bfloat16 [1024], P('dp'), may hold values from 0.099609375 to 1.8984375
- w_gate: bfloat16 [1024, 4608], P('dp'), may hold values from -0.1875 to 0.1875
- w_up: bfloat16 [1024, 4608], P('dp'), may hold values from -0.1875 to 0.1875
- w_down: bfloat16 [4608, 1024], P('dp'), may hold values from -0.09375 to 0.09375
Outputs:
- output: bfloat16 [16384, 1024], P('dp')
- input_grad: bfloat16 [16384, 1024], P('dp')
- grad_attn_gain: float32 [1024], P('dp')
- grad_query: float32 [1024, 1024], P('dp')
- grad_key: float32 [1024, 512], P('dp')
- grad_value: float32 [1024, 512], P('dp')
- grad_query_gain: float32 [64], replicated
- grad_key_gain: float32 [64], replicated
- grad_out: float32 [1024, 1024], P('dp')
- grad_ffn_gain: float32 [1024], P('dp')
- grad_gate: float32 [1024, 4608], P('dp')
- grad_up: float32 [1024, 4608], P('dp')
- grad_down: float32 [4608, 1024], P('dp')
Inputs may be any that keep to these rules, and one draw needn't show every extreme that they name: Each row of route holds every number from 0 to 511 once.
All inputs are finite; a program needn't handle non-finite values.
Results may differ from a plain program's by a relative error of at most 0.013.
Values may be sent and summed in bfloat16 or wider, within the bound.
No kernel may reach another device: no remote copies, remote signals or barrier semaphores. Data moves between devices by JAX's collectives and lax.ppermute only.
A program may use at most 256 MiB of HBM per device.

v0:
```python
from functools import partial

import jax
import jax.numpy as jnp
from jax import lax
from jax.sharding import PartitionSpec as P

QUERY_HEADS = 16
KEY_VALUE_HEADS = 8
HEAD_SIZE = 64
WINDOW_TOKENS = 256
MICRO = 2


EPS = 1e-05
THETA = 1000000.0
NEGATIVE = -1e30


def tdot(left, right):
    return lax.dot_general(
        left, right, (((0,), (0,)), ((), ())), preferred_element_type=jnp.float32
    )


def ntdot(left, right):
    return lax.dot_general(
        left, right, (((1,), (1,)), ((), ())), preferred_element_type=jnp.float32
    )


def norm_rows(values, gain):
    inverse = lax.rsqrt(jnp.mean(values * values, axis=-1, keepdims=True) + EPS)
    return (values * inverse * gain, inverse)


def norm_back(grad, values, inverse, gain):
    scaled = grad * gain
    grad_values = inverse * scaled - values * inverse * inverse * inverse * jnp.mean(
        scaled * values, axis=-1, keepdims=True
    )
    return (grad_values, grad * values * inverse)


def tables(positions, half_dim):
    steps_index = jnp.arange(half_dim, dtype=jnp.float32)
    inverse_freq = THETA ** (-steps_index / half_dim)
    angles = positions.astype(jnp.float32)[:, None] * inverse_freq[None, :]
    return (jnp.cos(angles), jnp.sin(angles))


def rotate_halves(values, cosine_table, sine_table, direction):
    half_dim = values.shape[-1] // 2
    lower_half = values[..., :half_dim]
    upper_half = values[..., half_dim:]
    return jnp.concatenate(
        [
            lower_half * cosine_table - direction * upper_half * sine_table,
            upper_half * cosine_table + direction * lower_half * sine_table,
        ],
        axis=-1,
    )


def layout(lengths_row, feature_width):
    places = jnp.arange(feature_width, dtype=jnp.int32)
    ends = jnp.cumsum(lengths_row)
    segment = jnp.sum((places[:, None] >= ends[None, :]).astype(jnp.int32), axis=1)
    starts = ends - lengths_row
    picked = segment[:, None] == jnp.arange(lengths_row.shape[0], dtype=jnp.int32)[None, :]
    begins = jnp.sum(jnp.where(picked, starts[None, :], 0), axis=1)
    allowed = (segment[:, None] == segment[None, :]) & (places[None, :] <= places[:, None])
    return (places - begins, allowed)


def masked_scores(allowed, query_block, key_block):
    factor = query_block.shape[-1] ** (-0.5)
    scores = (
        jnp.einsum("qrd,td->rqt", query_block, key_block, preferred_element_type=jnp.float32)
        * factor
    )
    return jnp.where(allowed[None], scores, NEGATIVE)


def attend_forward(allowed, blocks):
    query_block, key_block, value_block = blocks
    scores = masked_scores(allowed, query_block, key_block)
    row_max = jnp.max(scores, axis=-1, keepdims=True)
    exponent = jnp.exp(scores - row_max)
    totals = jnp.sum(exponent, axis=-1, keepdims=True)
    rounded_probs = (exponent / totals).astype(jnp.bfloat16)
    head_mixture = jnp.einsum(
        "rqt,td->qrd", rounded_probs, value_block, preferred_element_type=jnp.float32
    )
    return (head_mixture, (row_max + jnp.log(totals))[..., 0])


def attend_backward(allowed, blocks):
    query_block, key_block, value_block, grad_block, log_totals = blocks
    factor = query_block.shape[-1] ** (-0.5)
    scores = masked_scores(allowed, query_block, key_block)
    probs = jnp.exp(scores - log_totals[..., None])
    rounded_probs = probs.astype(jnp.bfloat16)
    grad_probs = jnp.einsum(
        "qrd,td->rqt", grad_block, value_block, preferred_element_type=jnp.float32
    )
    grad_value = jnp.einsum(
        "rqt,qrd->td", rounded_probs, grad_block, preferred_element_type=jnp.float32
    )
    inner = jnp.sum(probs * grad_probs, axis=-1, keepdims=True)
    grad_scores = (probs * (grad_probs - inner)).astype(jnp.bfloat16)
    grad_query = (
        jnp.einsum("rqt,td->qrd", grad_scores, key_block, preferred_element_type=jnp.float32)
        * factor
    )
    grad_key = (
        jnp.einsum("rqt,qrd->td", grad_scores, query_block, preferred_element_type=jnp.float32)
        * factor
    )
    return (grad_query, grad_key, grad_value)


def run_forward(window_tokens, lengths_row, gathered, query_gain, key_norm_gain):
    attn_gain, w_query, key_weight, value_weight, w_out, ffn_gain, w_gate, w_up, w_down = gathered
    feature_width = window_tokens.shape[0]
    positions, allowed = layout(lengths_row, feature_width)
    cosine_table, sine_table = tables(positions, HEAD_SIZE // 2)
    cosine_table = cosine_table[:, None, :]
    sine_table = sine_table[:, None, :]
    inputs = window_tokens.astype(jnp.float32)
    normed, inverse_one = norm_rows(inputs, attn_gain.astype(jnp.float32))
    normed_low = normed.astype(jnp.bfloat16)
    query_proj = jnp.dot(normed_low, w_query, preferred_element_type=jnp.float32).reshape(
        feature_width, QUERY_HEADS, HEAD_SIZE
    )
    key_projected = jnp.dot(normed_low, key_weight, preferred_element_type=jnp.float32).reshape(
        feature_width, KEY_VALUE_HEADS, HEAD_SIZE
    )
    value_low = (
        jnp.dot(normed_low, value_weight, preferred_element_type=jnp.float32)
        .astype(jnp.bfloat16)
        .reshape(feature_width, KEY_VALUE_HEADS, HEAD_SIZE)
    )
    query_hat, query_inv = norm_rows(query_proj, query_gain.astype(jnp.float32))
    key_hat, key_inv = norm_rows(key_projected, key_norm_gain.astype(jnp.float32))
    query_reduced = rotate_halves(query_hat, cosine_table, sine_table, 1.0).astype(jnp.bfloat16)
    key_low = rotate_halves(key_hat, cosine_table, sine_table, 1.0).astype(jnp.bfloat16)
    heads_of_query = jnp.moveaxis(
        query_reduced.reshape(
            feature_width, KEY_VALUE_HEADS, QUERY_HEADS // KEY_VALUE_HEADS, HEAD_SIZE
        ),
        1,
        0,
    )
    key_heads = jnp.moveaxis(key_low, 1, 0)
    value_heads = jnp.moveaxis(value_low, 1, 0)
    head_mixture, log_totals = lax.map(
        partial(attend_forward, allowed), (heads_of_query, key_heads, value_heads)
    )
    attended = (
        jnp.moveaxis(head_mixture, 0, 1)
        .reshape(feature_width, QUERY_HEADS * HEAD_SIZE)
        .astype(jnp.bfloat16)
    )
    resid = inputs + jnp.dot(attended, w_out, preferred_element_type=jnp.float32)
    normed_two, inverse_two = norm_rows(resid, ffn_gain.astype(jnp.float32))
    ffn_low = normed_two.astype(jnp.bfloat16)
    gate_proj = jnp.dot(ffn_low, w_gate, preferred_element_type=jnp.float32)
    up_proj = jnp.dot(ffn_low, w_up, preferred_element_type=jnp.float32)
    hidden_low = (jax.nn.silu(gate_proj) * up_proj).astype(jnp.bfloat16)
    output = (resid + jnp.dot(hidden_low, w_down, preferred_element_type=jnp.float32)).astype(
        jnp.bfloat16
    )
    saved = (
        inputs,
        inverse_one,
        normed_low,
        query_proj,
        query_inv,
        key_projected,
        key_inv,
        heads_of_query,
        key_heads,
        value_heads,
        log_totals,
        attended,
        resid,
        inverse_two,
        ffn_low,
        gate_proj,
        up_proj,
        hidden_low,
        cosine_table,
        sine_table,
        allowed,
    )
    return (output, saved)


def run_backward(window_grads, saved, gathered, query_gain, key_norm_gain):
    attn_gain, w_query, key_weight, value_weight, w_out, ffn_gain, w_gate, w_up, w_down = gathered
    (
        inputs,
        inverse_one,
        normed_low,
        query_proj,
        query_inv,
        key_projected,
        key_inv,
        heads_of_query,
        key_heads,
        value_heads,
        log_totals,
        attended,
        resid,
        inverse_two,
        ffn_low,
        gate_proj,
        up_proj,
        hidden_low,
        cosine_table,
        sine_table,
        allowed,
    ) = saved
    feature_width = inputs.shape[0]
    grad_rows = window_grads.astype(jnp.float32)
    grad_down = tdot(hidden_low, window_grads)
    grad_hidden = ntdot(window_grads, w_down)
    sigmoid_gate = jax.nn.sigmoid(gate_proj)
    grad_gate_low = (
        grad_hidden * up_proj * sigmoid_gate * (1.0 + gate_proj * (1.0 - sigmoid_gate))
    ).astype(jnp.bfloat16)
    grad_up_low = (grad_hidden * gate_proj * sigmoid_gate).astype(jnp.bfloat16)
    grad_gate = tdot(ffn_low, grad_gate_low)
    grad_up = tdot(ffn_low, grad_up_low)
    grad_normed_two = ntdot(grad_gate_low, w_gate) + ntdot(grad_up_low, w_up)
    grad_resid_part, ffn_rows = norm_back(
        grad_normed_two, resid, inverse_two, ffn_gain.astype(jnp.float32)
    )
    grad_resid = grad_rows + grad_resid_part
    grad_branch_low = grad_resid.astype(jnp.bfloat16)
    grad_out = tdot(attended, grad_branch_low)
    attended_gradient = ntdot(grad_branch_low, w_out).astype(jnp.bfloat16)
    head_gradient = jnp.moveaxis(
        attended_gradient.reshape(
            feature_width, KEY_VALUE_HEADS, QUERY_HEADS // KEY_VALUE_HEADS, HEAD_SIZE
        ),
        1,
        0,
    )
    grad_query_heads, grad_key_heads, value_head_gradient = lax.map(
        partial(attend_backward, allowed),
        (heads_of_query, key_heads, value_heads, head_gradient, log_totals),
    )
    grad_query_rot = jnp.moveaxis(grad_query_heads, 0, 1).reshape(
        feature_width, QUERY_HEADS, HEAD_SIZE
    )
    grad_key_rot = jnp.moveaxis(grad_key_heads, 0, 1)
    grad_value_low = (
        jnp.moveaxis(value_head_gradient, 0, 1)
        .reshape(feature_width, KEY_VALUE_HEADS * HEAD_SIZE)
        .astype(jnp.bfloat16)
    )
    grad_query_hat = rotate_halves(grad_query_rot, cosine_table, sine_table, -1.0)
    grad_key_hat = rotate_halves(grad_key_rot, cosine_table, sine_table, -1.0)
    grad_query_proj, query_rows = norm_back(
        grad_query_hat, query_proj, query_inv, query_gain.astype(jnp.float32)
    )
    key_projection_gradient, key_matrix = norm_back(
        grad_key_hat, key_projected, key_inv, key_norm_gain.astype(jnp.float32)
    )
    grad_query_low = grad_query_proj.reshape(feature_width, QUERY_HEADS * HEAD_SIZE).astype(
        jnp.bfloat16
    )
    key_reduced_gradient = key_projection_gradient.reshape(
        feature_width, KEY_VALUE_HEADS * HEAD_SIZE
    ).astype(jnp.bfloat16)
    grad_query = tdot(normed_low, grad_query_low)
    grad_key = tdot(normed_low, key_reduced_gradient)
    grad_value = tdot(normed_low, grad_value_low)
    grad_normed = (
        ntdot(grad_query_low, w_query)
        + ntdot(key_reduced_gradient, key_weight)
        + ntdot(grad_value_low, value_weight)
    )
    grad_input_part, attn_rows = norm_back(
        grad_normed, inputs, inverse_one, attn_gain.astype(jnp.float32)
    )
    input_grad = (grad_resid + grad_input_part).astype(jnp.bfloat16)
    gradients = (
        jnp.sum(attn_rows, axis=0),
        grad_query,
        grad_key,
        grad_value,
        grad_out,
        jnp.sum(ffn_rows, axis=0),
        grad_gate,
        grad_up,
        grad_down,
    )
    gain_terms = (jnp.sum(query_rows, axis=(0, 1)), jnp.sum(key_matrix, axis=(0, 1)))
    return (input_grad, gradients, gain_terms)


def reduce_each(gradients):
    (
        grad_attn_gain,
        grad_query,
        grad_key,
        grad_value,
        grad_out,
        grad_ffn_gain,
        grad_gate,
        grad_up,
        grad_down,
    ) = gradients
    return (
        lax.psum_scatter(grad_attn_gain, "dp", scatter_dimension=0, tiled=True),
        lax.psum_scatter(grad_query, "dp", scatter_dimension=0, tiled=True),
        lax.psum_scatter(grad_key, "dp", scatter_dimension=0, tiled=True),
        lax.psum_scatter(grad_value, "dp", scatter_dimension=0, tiled=True),
        lax.psum_scatter(grad_out, "dp", scatter_dimension=0, tiled=True),
        lax.psum_scatter(grad_ffn_gain, "dp", scatter_dimension=0, tiled=True),
        lax.psum_scatter(grad_gate, "dp", scatter_dimension=0, tiled=True),
        lax.psum_scatter(grad_up, "dp", scatter_dimension=0, tiled=True),
        lax.psum_scatter(grad_down, "dp", scatter_dimension=0, tiled=True),
    )


def gather_all(attn_gain, w_query, key_weight, value_weight, w_out, ffn_gain, w_gate, w_up, w_down):
    return (
        lax.all_gather(attn_gain, "dp", axis=0, tiled=True),
        lax.all_gather(w_query, "dp", axis=0, tiled=True),
        lax.all_gather(key_weight, "dp", axis=0, tiled=True),
        lax.all_gather(value_weight, "dp", axis=0, tiled=True),
        lax.all_gather(w_out, "dp", axis=0, tiled=True),
        lax.all_gather(ffn_gain, "dp", axis=0, tiled=True),
        lax.all_gather(w_gate, "dp", axis=0, tiled=True),
        lax.all_gather(w_up, "dp", axis=0, tiled=True),
        lax.all_gather(w_down, "dp", axis=0, tiled=True),
    )


def add_tuples(running, fresh):
    if running is None:
        return fresh
    return tuple((earlier + later for earlier, later in zip(running, fresh)))


def per_device(
    tokens,
    cotangent,
    route,
    lengths,
    attn_gain,
    w_query,
    key_weight,
    value_weight,
    query_gain,
    key_norm_gain,
    w_out,
    ffn_gain,
    w_gate,
    w_up,
    w_down,
):
    feature_width = WINDOW_TOKENS
    orders = route[0]
    row_count = orders.shape[0]
    inverse = (
        jnp.zeros((row_count,), jnp.int32).at[orders].set(jnp.arange(row_count, dtype=jnp.int32))
    )
    sent_tokens = tokens[orders]
    sent_grads = cotangent[orders]
    owned_sums = None
    gain_sums = None
    outputs = []
    input_grads = []
    for micro_step in range(MICRO):
        lower_row = micro_step * feature_width
        window_tokens, window_grads = (
            lax.all_to_all(
                sent_tokens[lower_row : lower_row + feature_width],
                "dp",
                split_axis=0,
                concat_axis=0,
                tiled=True,
            ),
            lax.all_to_all(
                sent_grads[lower_row : lower_row + feature_width],
                "dp",
                split_axis=0,
                concat_axis=0,
                tiled=True,
            ),
        )
        gathered = gather_all(
            attn_gain, w_query, key_weight, value_weight, w_out, ffn_gain, w_gate, w_up, w_down
        )
        output, saved = run_forward(
            window_tokens, lengths[micro_step], gathered, query_gain, key_norm_gain
        )
        gathered = (
            lax.all_gather(attn_gain, "dp", axis=0, tiled=True),
            lax.all_gather(w_query, "dp", axis=0, tiled=True),
            lax.all_gather(key_weight, "dp", axis=0, tiled=True),
            lax.all_gather(value_weight, "dp", axis=0, tiled=True),
            lax.all_gather(w_out, "dp", axis=0, tiled=True),
            lax.all_gather(ffn_gain, "dp", axis=0, tiled=True),
            lax.all_gather(w_gate, "dp", axis=0, tiled=True),
            lax.all_gather(w_up, "dp", axis=0, tiled=True),
            lax.all_gather(w_down, "dp", axis=0, tiled=True),
        )
        input_grad, gradients, gain_terms = run_backward(
            window_grads, saved, gathered, query_gain, key_norm_gain
        )
        returned_out, returned_grad = (
            lax.all_to_all(output, "dp", split_axis=0, concat_axis=0, tiled=True),
            lax.all_to_all(input_grad, "dp", split_axis=0, concat_axis=0, tiled=True),
        )
        outputs.append(returned_out)
        input_grads.append(returned_grad)
        gain_sums = add_tuples(gain_sums, gain_terms)
        owned_sums = add_tuples(owned_sums, reduce_each(gradients))
    query_total, key_total = lax.psum((gain_sums[0], gain_sums[1]), "dp")
    output_rows = jnp.concatenate(outputs, axis=0)[inverse]
    grad_rows = jnp.concatenate(input_grads, axis=0)[inverse]
    return (
        output_rows,
        grad_rows,
        owned_sums[0],
        owned_sums[1],
        owned_sums[2],
        owned_sums[3],
        query_total,
        key_total,
        owned_sums[4],
        owned_sums[5],
        owned_sums[6],
        owned_sums[7],
        owned_sums[8],
    )


def solution(mesh):
    in_specs = (
        P("dp", None),
        P("dp", None),
        P("dp", None),
        P("dp", None),
        P("dp"),
        P("dp", None),
        P("dp", None),
        P("dp", None),
        P(),
        P(),
        P("dp", None),
        P("dp"),
        P("dp", None),
        P("dp", None),
        P("dp", None),
    )
    out_specs = (
        P("dp", None),
        P("dp", None),
        P("dp"),
        P("dp", None),
        P("dp", None),
        P("dp", None),
        P(),
        P(),
        P("dp", None),
        P("dp"),
        P("dp", None),
        P("dp", None),
        P("dp", None),
    )
    return jax.shard_map(
        per_device, mesh=mesh, in_specs=in_specs, out_specs=out_specs, check_vma=False
    )
```

profile of v0, /device:TPU:0, one launch (start us, length us, event | category | flops | bytes accessed | tf_op | source)
XLA Modules:
  0.0 1898.8 jit_solution(6431474581215042951)
XLA Ops:
  12.4 2.1 gather_fusion
  15.6 7.3 all-to-all-start.2
  24.5 14.5 all-to-all-done.2
  38.9 3.1 all-to-all-start
  43.2 40.8 %all-reduce.5 = (bf16[1024]{0:T(1024)(128)(2,1)S(1)}, bf16[1024]{0:T(1024)(128)(2,1)S(1)}) all-reduce(bf16[1024]{0:T(1024)(128)(2,1)S(1)} %dynamic-update-slice, bf16[1024]{0:T(1024)(128)(2,1)S(1)} %dynamic-update-slice.1), channel_id=1, replica_groups=mesh['dp'=32] {'dp'}, use_global_device_ids=true, to_apply=%add | all-reduce | flops 2048 | bytes 8192
  85.1 2.8 gather_fusion.2
  88.8 2.2 slice_bitcast_fusion.1
  91.3 4.8 all-to-all-start.4
  99.6 28.1 %all-gather.10.cloned.1.call-done = bf16[1024,512]{1,0:T(8,128)(2,1)} async-done(((bf16[32,512]{1,0:T(8,128)(2,1)}), bf16[1024,512]{1,0:T(8,128)(2,1)}) %all-gather.10.cloned.1.call-update) | async-done | bytes 1048592 | tf_op jit(solution)/shard_map/all_gather | solution.py:334
  127.7 2.3 copy.79
  141.2 44.8 %all-gather.12.cloned.1.call-done = bf16[1024,1024]{1,0:T(8,128)(2,1)} async-done(((bf16[32,1024]{1,0:T(8,128)(2,1)}), bf16[1024,1024]{1,0:T(8,128)(2,1)}) %all-gather.12.cloned.1.call-update) | async-done | bytes 2097168 | tf_op jit(solution)/shard_map/all_gather | solution.py:333
  185.9 3.9 copy.80
  189.9 2.6 multiply_reduce_fusion.13
  195.2 11.9 while.56
  207.2 36.8 %all-gather.14.cloned.1.call-done = bf16[1024,1024]{1,0:T(8,128)(2,1)} async-done(((bf16[32,1024]{1,0:T(8,128)(2,1)}), bf16[1024,1024]{1,0:T(8,128)(2,1)}) %all-gather.14.cloned.1.call-update) | async-done | bytes 2097168 | tf_op jit(solution)/shard_map/all_gather | solution.py:336
  244.0 3.3 multiply_reduce_fusion.12
  248.5 28.5 %while.57 = (s32[]{:T(128)}, bf16[8,256,2,64]{1,3,2,0:T(8,128)(2,1)}, f32[8,2,256]{2,1,0:T(2,128)}, bf16[8,256,64]{1,2,0:T(8,128)(2,1)}, bf16[8,256,64]{1,2,0:T(...) while((s32[]{:T(128)}, bf16[8,256,2,64]{1,3,2,0:T(8,128)(2,1)}, ...), condition=%wide.region_20.21_spmd.clone, body=%wide.region_17.20_spmd.clone.sunk | while | flops 34799104 | bytes 1985633 | solution.py:157
  277.1 2.8 multiply_reduce_fusion.10
  280.7 47.0 %all-gather.16.cloned.1.call-done = bf16[1024,4608]{1,0:T(8,128)(2,1)} async-done(((bf16[32,4608]{1,0:T(8,128)(2,1)}), bf16[1024,4608]{1,0:T(8,128)(2,1)}) %all-gather.16.cloned.1.call-update) | async-done | bytes 9437200 | tf_op jit(solution)/shard_map/all_gather | solution.py:338
  327.7 8.0 fusion.197
  335.6 75.5 %all-gather.18.cloned.1.call-done = bf16[1024,4608]{1,0:T(8,128)(2,1)} async-done(((bf16[32,4608]{1,0:T(8,128)(2,1)}), bf16[1024,4608]{1,0:T(8,128)(2,1)}) %all-gather.18.cloned.1.call-update) | async-done | bytes 9437200 | tf_op jit(solution)/shard_map/all_gather | solution.py:339
  411.1 7.9 fusion.198
  419.0 3.3 all-to-all-start.6
  422.8 77.2 %all-gather.20.cloned.1.call-done = bf16[4608,1024]{1,0:T(8,128)(2,1)} async-done(((bf16[144,1024]{1,0:T(8,128)(2,1)}), bf16[4608,1024]{1,0:T(8,128)(2,1)}) %all-gather.20.cloned.1.call-update) | async-done | bytes 9437200 | tf_op jit(solution)/shard_map/all_gather | solution.py:340
  499.9 10.0 multiply_convert_fusion.4
  509.9 6.9 fusion.201
  516.9 6.2 multiply_reduce_fusion.3
  523.1 2.2 subtract_add_fusion.1
  526.9 2.1 copy.82
  531.0 60.0 %while.58 = (s32[]{:T(128)}, f32[8,256,2,64]{1,3,2,0:T(8,128)}, f32[8,256,64]{1,2,0:T(8,128)}, bf16[8,256,64]{1,2,0:T(8,128)(2,1)S(1)}, bf16[8,256,64]{1,2,0:T(8...) while((s32[]{:T(128)}, f32[8,256,2,64]{1,3,2,0:T(8,128)}, ...), condition=%wide.region_26.27_spmd.clone, body=%wide.region_24.26_spmd.clone.sunk | while | flops 85310976 | bytes 4702329 | solution.py:251
  591.0 8.7 fusion.199
  599.7 7.9 fusion.200
  607.6 10.0 multiply_convert_fusion.2
  617.6 7.2 fusion.203
  624.8 6.1 multiply_reduce_fusion.2
  633.9 2.1 copy.83
  636.9 59.6 %while.59 = (s32[]{:T(128)}, f32[8,256,2,64]{1,3,2,0:T(8,128)S(1)}, f32[8,256,64]{1,2,0:T(8,128)}, bf16[8,256,64]{1,2,0:T(8,128)(2,1)}, bf16[8,256,64]{1,2,0:T(8...) while((s32[]{:T(128)}, f32[8,256,2,64]{1,3,2,0:T(8,128)S(1)}, ...), condition=%wide.region_33.34_spmd.clone, body=%wide.region_31.33_spmd.clone.sunk | while | flops 85310976 | bytes 4702329 | solution.py:251
  712.5 2.8 convolution_add_fusion.4
  718.4 2.7 convolution_add_fusion.3
  722.1 9.7 fusion.205
  731.9 12.1 convolution_add_fusion.2
  744.1 9.8 fusion.206
  753.9 12.3 convolution_add_fusion.1
  766.5 10.9 fusion.149
  777.4 12.6 convolution_add_fusion
  790.0 8.2 fusion.116
  798.2 3.4 all-to-all-start.3
  801.6 1.9 fusion.204
  808.9 7.1 fusion.117
  817.8 4.4 all-to-all-start.1
  822.3 2.9 fusion.132
  827.0 11.5 all-to-all-done.1
  838.4 19.3 %all_to_all.90 = bf16[32,8,1024]{2,1,0:T(8,128)(2,1)S(1)} all-to-all(bf16[32,8,1024]{2,1,0:T(8,128)(2,1)} %get-tuple-element.416), channel_id=1, replica_groups=mesh['dp'=32] {'dp'}, dimensions={0} | all-to-all | bytes 1048576 | tf_op jit(solution)/shard_map/all_to_all | solution.py:419
  857.7 3.1 all-to-all-start.5
  860.8 2.6 scatter_custom_fusion
  863.5 41.0 %all-reduce.4 = (f32[1024]{0:T(1024)S(1)}, f32[64]{0:T(128)}, f32[64]{0:T(128)}, f32[1024]{0:T(1024)S(1)}) all-reduce(f32[1024]{0:T(1024)S(1)} %add.327, f32[64]{0:T(128)S(1)} %add.320, f32[64]{0:T(128)S(1)} %add.321, f32[1024]{0:T(1024)S(1)} %add.332), channel_id=11, replica_groups=mesh['dp'=32] {'dp'}, use_global_device_ids=true, to_apply=%region_38.39.clone | all-reduce | flops 2176 | bytes 17408
  906.9 2.8 gather_fusion.1
  909.8 2.8 gather_fusion.3
  912.6 65.6 %reduce-scatter.12.cloned.1.call-done = f32[32,512]{1,0:T(8,128)} async-done(((f32[1024,512]{1,0:T(8,128)}), f32[32,512]{1,0:T(8,128)}) %reduce-scatter.12.cloned.1.call-update) | async-done | bytes 65552 | tf_op jit(solution)/shard_map/reduce_scatter | solution.py:321
  978.1 139.6 %reduce-scatter.8.cloned.1.call-done = f32[32,1024]{1,0:T(8,128)} async-done(((f32[1024,1024]{1,0:T(8,128)}), f32[32,1024]{1,0:T(8,128)}) %reduce-scatter.8.cloned.1.call-update) | async-done | bytes 131088 | tf_op jit(solution)/shard_map/reduce_scatter | solution.py:319
  1117.7 139.6 %reduce-scatter.14.cloned.1.call-done = f32[32,1024]{1,0:T(8,128)} async-done(((f32[1024,1024]{1,0:T(8,128)}), f32[32,1024]{1,0:T(8,128)}) %reduce-scatter.14.cloned.1.call-update) | async-done | bytes 131088 | tf_op jit(solution)/shard_map/reduce_scatter | solution.py:322
  1257.3 209.5 %reduce-scatter.16.cloned.1.call-done = f32[32,4608]{1,0:T(8,128)} async-done(((f32[1024,4608]{1,0:T(8,128)}), f32[32,4608]{1,0:T(8,128)}) %reduce-scatter.16.cloned.1.call-update) | async-done | bytes 589840 | tf_op jit(solution)/shard_map/reduce_scatter | solution.py:324
  1466.8 212.5 %reduce-scatter.18.cloned.1.call-done = f32[32,4608]{1,0:T(8,128)} async-done(((f32[1024,4608]{1,0:T(8,128)}), f32[32,4608]{1,0:T(8,128)}) %reduce-scatter.18.cloned.1.call-update) | async-done | bytes 589840 | tf_op jit(solution)/shard_map/reduce_scatter | solution.py:325
  1679.4 212.4 %reduce-scatter.20.cloned.1.call-done = f32[144,1024]{1,0:T(8,128)} async-done(((f32[4608,1024]{1,0:T(8,128)}), f32[144,1024]{1,0:T(8,128)}) %reduce-scatter.20.cloned.1.call-update) | async-done | bytes 589840 | tf_op jit(solution)/shard_map/reduce_scatter | solution.py:326
  (524 shorter events, 229.1 us)
Async XLA Ops:
  7.2 89.8 %all-gather.8.cloned.1.call-start = ((), (), s32[]{:S(2)}) async-start(), calls=%async_computation.15 | async-start | bytes 1081344 | tf_op jit(solution)/shard_map/all_gather | solution.py:335
  7.9 119.8 %all-gather.10.cloned.1.call-start = ((), (), s32[]{:S(2)}) async-start(), calls=%async_computation.16 | async-start | bytes 1081344 | tf_op jit(solution)/shard_map/all_gather | solution.py:334
  8.7 177.3 %all-gather.12.cloned.1.call-start = ((), (), s32[]{:S(2)}) async-start(), calls=%async_computation.17 | async-start | bytes 2162688 | tf_op jit(solution)/shard_map/all_gather | solution.py:333
  9.4 234.6 %all-gather.14.cloned.1.call-start = ((), (), s32[]{:S(2)}) async-start(), calls=%async_computation.18 | async-start | bytes 2162688 | tf_op jit(solution)/shard_map/all_gather | solution.py:336
  10.0 317.7 %all-gather.16.cloned.1.call-start = ((), (), s32[]{:S(2)}) async-start(), calls=%async_computation.19 | async-start | bytes 9732096 | tf_op jit(solution)/shard_map/all_gather | solution.py:338
  10.6 400.5 %all-gather.18.cloned.1.call-start = ((), (), s32[]{:S(2)}) async-start(), calls=%async_computation.20 | async-start | bytes 9732096 | tf_op jit(solution)/shard_map/all_gather | solution.py:339
  12.4 11.2 copy-start.83
  14.5 28.2 %copy-start.86 = (bf16[32]{0:T(256)(128)(2,1)S(1)}, bf16[32]{0:T(256)(128)(2,1)}, u32[]{:S(2)}) copy-start(bf16[32]{0:T(256)(128)(2,1)} %param.27) | copy-start | bytes 196
  14.5 28.4 %copy-start.87 = (bf16[32]{0:T(256)(128)(2,1)S(1)}, bf16[32]{0:T(256)(128)(2,1)}, u32[]{:S(2)}) copy-start(bf16[32]{0:T(256)(128)(2,1)} %param.34) | copy-start | bytes 196
  14.5 69.5 %copy-start.88 = (bf16[64]{0:T(256)(128)(2,1)S(1)}, bf16[64]{0:T(256)(128)(2,1)}, u32[]{:S(2)}) copy-start(bf16[64]{0:T(256)(128)(2,1)} %param.32) | copy-start | bytes 388
  14.5 70.0 %copy-start.89 = (bf16[64]{0:T(256)(128)(2,1)S(1)}, bf16[64]{0:T(256)(128)(2,1)}, u32[]{:S(2)}) copy-start(bf16[64]{0:T(256)(128)(2,1)} %param.31) | copy-start | bytes 388
  14.6 70.5 %copy-start.2 = (bf16[512,1024]{1,0:T(8,128)(2,1)S(1)}, bf16[512,1024]{1,0:T(8,128)(2,1)}, u32[]{:S(2)}) copy-start(bf16[512,1024]{1,0:T(8,128)(2,1)} %param.24) | copy-start | bytes 3145732
  15.6 23.3 %all-to-all-start.2 = ((bf16[32,8,1024]{2,1,0:T(8,128)(2,1)}), bf16[32,8,1024]{2,1,0:T(8,128)(2,1)S(1)}, u32[]{:S(2)}, u32[]{:S(2)}) async-start(bf16[32,8,1024]{2,1,0:T(8,128)(2,1)} %get-tuple-element.404), calls=%async_computation.2 | async-start | bytes 1048576 | tf_op jit(solution)/shard_map/all_to_all | solution.py:382
  22.9 477.0 %all-gather.20.cloned.1.call-start = ((), (), s32[]{:S(2)}) async-start(), calls=%async_computation.21 | async-start | bytes 9732096 | tf_op jit(solution)/shard_map/all_gather | solution.py:340
  24.4 63.4 %copy-start.31 = (bf16[8,256,2,64]{1,3,2,0:T(8,128)(2,1)}, bf16[8,256,2,64]{1,3,2,0:T(8,128)(2,1)S(1)}, u32[]{:S(2)}) copy-start(bf16[8,256,2,64]{1,3,2,0:T(8,128)(2,1)S(1)} %fusion.195) | copy-start | bytes 1572868
  38.9 153.6 %copy-start.6 = (bf16[32,8,1024]{2,1,0:T(8,128)(2,1)}, bf16[32,8,1024]{2,1,0:T(8,128)(2,1)S(1)}, u32[]{:S(2)}) copy-start(bf16[32,8,1024]{2,1,0:T(8,128)(2,1)S(1)} %all-to-all-done.2) | copy-start | bytes 1572868
  38.9 52.4 %all-to-all-start = ((bf16[32,8,1024]{2,1,0:T(8,128)(2,1)}), bf16[32,8,1024]{2,1,0:T(8,128)(2,1)S(1)}, u32[]{:S(2)}, u32[]{:S(2)}) async-start(bf16[32,8,1024]{2,1,0:T(8,128)(2,1)} %get-tuple-element.403), calls=%async_computation | async-start | bytes 1048576 | tf_op jit(solution)/shard_map/all_to_all | solution.py:382
  91.3 38.7 %copy-start.72 = (f32[256]{0:T(256)}, f32[256]{0:T(256)S(1)}, u32[]{:S(2)}) copy-start(f32[256]{0:T(256)S(1)} %rsqrt.78) | copy-start | bytes 3076
  91.3 152.6 %copy-start.4 = (bf16[32,8,1024]{2,1,0:T(8,128)(2,1)}, bf16[32,8,1024]{2,1,0:T(8,128)(2,1)S(1)}, u32[]{:S(2)}) copy-start(bf16[32,8,1024]{2,1,0:T(8,128)(2,1)S(1)} %all-to-all-done) | copy-start | bytes 1572868
  91.3 327.6 %all-to-all-start.4 = ((bf16[32,8,1024]{2,1,0:T(8,128)(2,1)}), bf16[32,8,1024]{2,1,0:T(8,128)(2,1)}, u32[]{:S(2)}, u32[]{:S(2)}) async-start(bf16[32,8,1024]{2,1,0:T(8,128)(2,1)} %get-tuple-element.399), calls=%async_computation.4 | async-start | bytes 1048576 | tf_op jit(solution)/shard_map/all_to_all | solution.py:389
  98.7 36.2 %copy-start.44 = (bf16[1024,512]{1,0:T(8,128)(2,1)S(1)}, bf16[1024,512]{1,0:T(8,128)(2,1)}, u32[]{:S(2)}) copy-start(bf16[1024,512]{1,0:T(8,128)(2,1)} %all-gather.8.cloned.1.call-done) | copy-start | bytes 3145732
  131.8 8.7 copy-start.36
  134.2 55.6 %copy-start.38 = (f32[256,8,64]{0,2,1:T(8,128)}, f32[256,8,64]{0,2,1:T(8,128)S(1)}, u32[]{:S(2)}) copy-start(f32[256,8,64]{0,2,1:T(8,128)S(1)} %get-tuple-element.449) | copy-start | bytes 1572868
  207.1 41.4 %copy-start.33 = (bf16[8,256,2,64]{1,3,2,0:T(8,128)(2,1)}, bf16[8,256,2,64]{1,3,2,0:T(8,128)(2,1)S(1)}, u32[]{:S(2)}) copy-start(bf16[8,256,2,64]{1,3,2,0:T(8,128)(2,1)S(1)} %get-tuple-element.197) | copy-start | bytes 1572868
  207.1 41.3 %copy-start.60 = (bf16[8,256,64]{1,2,0:T(8,128)(2,1)}, bf16[8,256,64]{1,2,0:T(8,128)(2,1)S(1)}, u32[]{:S(2)}) copy-start(bf16[8,256,64]{1,2,0:T(8,128)(2,1)S(1)} %get-tuple-element.845) | copy-start | bytes 786436
  207.2 41.3 %copy-start.69 = (f32[8,2,256]{2,1,0:T(2,128)}, f32[8,2,256]{2,1,0:T(2,128)S(1)}, u32[]{:S(2)}) copy-start(f32[8,2,256]{2,1,0:T(2,128)S(1)} %get-tuple-element.743) | copy-start | bytes 49156
  207.2 41.3 %copy-start.46 = (bf16[8,256,2,64]{1,3,2,0:T(8,128)(2,1)}, bf16[8,256,2,64]{1,3,2,0:T(8,128)(2,1)S(1)}, u32[]{:S(2)}) copy-start(bf16[8,256,2,64]{1,3,2,0:T(8,128)(2,1)S(1)} %get-tuple-element.840) | copy-start | bytes 1572868
  248.5 28.6 %copy-start.3 = (bf16[1024,1024]{1,0:T(8,128)(2,1)S(1)}, bf16[1024,1024]{1,0:T(8,128)(2,1)}, u32[]{:S(2)}) copy-start(bf16[1024,1024]{1,0:T(8,128)(2,1)} %all-gather.14.cloned.1.call-done) | copy-start | bytes 6291460
  248.5 28.6 %copy-start.7 = (bf16[32,8,1024]{2,1,0:T(8,128)(2,1)S(1)}, bf16[32,8,1024]{2,1,0:T(8,128)(2,1)}, u32[]{:S(2)}) copy-start(bf16[32,8,1024]{2,1,0:T(8,128)(2,1)} %copy-done.6) | copy-start | bytes 1572868
  280.6 130.4 %copy-start.18 = (bf16[256,1024]{1,0:T(8,128)(2,1)}, bf16[256,1024]{1,0:T(8,128)(2,1)S(1)}, u32[]{:S(2)}) copy-start(bf16[256,1024]{1,0:T(8,128)(2,1)S(1)} %multiply_convert_fusion.9) | copy-start | bytes 1572868
  419.0 188.6 %all-to-all-start.6 = ((bf16[32,8,1024]{2,1,0:T(8,128)(2,1)}), bf16[32,8,1024]{2,1,0:T(8,128)(2,1)}, u32[]{:S(2)}, u32[]{:S(2)}) async-start(bf16[32,8,1024]{2,1,0:T(8,128)(2,1)} %get-tuple-element.400), calls=%async_computation.6 | async-start | bytes 1048576 | tf_op jit(solution)/shard_map/all_to_all | solution.py:389
  422.3 490.2 %reduce-scatter.10.cloned.1.call-start = ((), (), s32[]{:S(2)}) async-start(), calls=%async_computation.23 | async-start | bytes 2162688 | tf_op jit(solution)/shard_map/reduce_scatter | solution.py:320
  509.9 7.0 copy-start.26
  591.0 8.7 copy-start.9
  617.6 7.2 copy-start.51
  617.6 7.2 copy-start.49
  617.6 7.2 copy-start.29
  617.6 7.2 copy-start.76
  636.9 62.4 %copy-start.37 = (f32[256,8,64]{0,2,1:T(8,128)S(1)}, f32[256,8,64]{0,2,1:T(8,128)}, u32[]{:S(2)}) copy-start(f32[256,8,64]{0,2,1:T(8,128)} %copy-done.36) | copy-start | bytes 1572868
  636.9 62.4 %copy-start.39 = (f32[256,8,64]{0,2,1:T(8,128)S(1)}, f32[256,8,64]{0,2,1:T(8,128)}, u32[]{:S(2)}) copy-start(f32[256,8,64]{0,2,1:T(8,128)} %copy-done.38) | copy-start | bytes 1572868
  636.9 62.4 %copy-start.80 = (f32[64]{0:T(128)S(1)}, f32[64]{0:T(128)}, u32[]{:S(2)}) copy-start(f32[64]{0:T(128)} %convert_element_type.257) | copy-start | bytes 772
  704.1 274.0 %reduce-scatter.12.cloned.1.call-start = ((), (), s32[]{:S(2)}) async-start(), calls=%async_computation.24 | async-start | bytes 2162688 | tf_op jit(solution)/shard_map/reduce_scatter | solution.py:321
  706.7 411.0 %reduce-scatter.8.cloned.1.call-start = ((), (), s32[]{:S(2)}) async-start(), calls=%async_computation.22 | async-start | bytes 4325376 | tf_op jit(solution)/shard_map/reduce_scatter | solution.py:319
  715.4 542.0 %reduce-scatter.14.cloned.1.call-start = ((), (), s32[]{:S(2)}) async-start(), calls=%async_computation.25 | async-start | bytes 4325376 | tf_op jit(solution)/shard_map/reduce_scatter | solution.py:322
  721.1 10.7 copy-start.10
  721.1 745.7 %reduce-scatter.16.cloned.1.call-start = ((), (), s32[]{:S(2)}) async-start(), calls=%async_computation.26 | async-start | bytes 19464192 | tf_op jit(solution)/shard_map/reduce_scatter | solution.py:324
  722.1 9.7 copy-start.52
  744.0 935.4 %reduce-scatter.18.cloned.1.call-start = ((), (), s32[]{:S(2)}) async-start(), calls=%async_computation.27 | async-start | bytes 19464192 | tf_op jit(solution)/shard_map/reduce_scatter | solution.py:325
  744.1 9.8 copy-start.50
  766.2 1125.6 %reduce-scatter.20.cloned.1.call-start = ((), (), s32[]{:S(2)}) async-start(), calls=%async_computation.28 | async-start | bytes 19464192 | tf_op jit(solution)/shard_map/reduce_scatter | solution.py:326
  766.5 10.9 copy-start.35
  790.0 11.6 copy-start.11
  798.2 19.6 %all-to-all-start.3 = ((bf16[32,8,1024]{2,1,0:T(8,128)(2,1)}), bf16[32,8,1024]{2,1,0:T(8,128)(2,1)}, u32[]{:S(2)}, u32[]{:S(2)}) async-start(bf16[32,8,1024]{2,1,0:T(8,128)(2,1)} %fusion.116), calls=%async_computation.3 | async-start | bytes 1048576 | tf_op jit(solution)/shard_map/all_to_all | solution.py:418
  808.9 13.3 copy-start.73
  808.9 13.3 copy-start.74
  816.0 9.2 copy-start.14
  816.0 9.2 copy-start.17
  817.8 20.6 %all-to-all-start.1 = ((bf16[32,8,1024]{2,1,0:T(8,128)(2,1)}), bf16[32,8,1024]{2,1,0:T(8,128)(2,1)}, u32[]{:S(2)}, u32[]{:S(2)}) async-start(bf16[32,8,1024]{2,1,0:T(8,128)(2,1)} %fusion.117), calls=%async_computation.1 | async-start | bytes 1048576 | tf_op jit(solution)/shard_map/all_to_all | solution.py:418
  825.2 38.2 %copy-start.84 = (f32[64]{0:T(128)S(1)}, f32[64]{0:T(128)}, u32[]{:S(2)}) copy-start(f32[64]{0:T(128)} %get-tuple-element.301) | copy-start | bytes 772
  825.2 38.2 %copy-start.85 = (f32[64]{0:T(128)S(1)}, f32[64]{0:T(128)}, u32[]{:S(2)}) copy-start(f32[64]{0:T(128)} %get-tuple-element.434) | copy-start | bytes 772
  825.2 38.3 %copy-start.81 = (f32[1024]{0:T(1024)S(1)}, f32[1024]{0:T(1024)}, u32[]{:S(2)}) copy-start(f32[1024]{0:T(1024)} %get-tuple-element.289) | copy-start | bytes 12292
  825.2 38.3 %copy-start.82 = (f32[1024]{0:T(1024)S(1)}, f32[1024]{0:T(1024)}, u32[]{:S(2)}) copy-start(f32[1024]{0:T(1024)} %get-tuple-element.287) | copy-start | bytes 12292
  857.7 52.0 %all-to-all-start.5 = ((bf16[32,8,1024]{2,1,0:T(8,128)(2,1)}), bf16[32,8,1024]{2,1,0:T(8,128)(2,1)S(1)}, u32[]{:S(2)}, u32[]{:S(2)}) async-start(bf16[32,8,1024]{2,1,0:T(8,128)(2,1)} %get-tuple-element.415), calls=%async_computation.5 | async-start | bytes 1048576 | tf_op jit(solution)/shard_map/all_to_all | solution.py:419
  909.7 982.1 %copy-start.1 = (bf16[512,1024]{1,0:T(8,128)(2,1)S(1)}, bf16[512,1024]{1,0:T(8,128)(2,1)}, u32[]{:S(2)}) copy-start(bf16[512,1024]{1,0:T(8,128)(2,1)} %param.23) | copy-start | bytes 3145732
  (47 other events, 145.3 us)
Sparse Core Ops, SparseCore 0:
  10.9 58.6 all-gather.7
  72.5 55.1 all-gather.9
  130.6 55.3 all-gather.11
  188.6 55.2 all-gather.13
  246.7 80.9 all-gather.15
  330.4 80.6 all-gather.17
  414.0 85.8 all-gather.19
  704.2 136.6 reduce-scatter.9
  843.8 134.2 reduce-scatter.11
  980.8 136.8 reduce-scatter.7
  1120.6 136.7 reduce-scatter.13
  1264.2 202.6 reduce-scatter.15
  1473.8 205.5 reduce-scatter.17
  1686.2 205.5 reduce-scatter.19
where the time goes:
time: 1910 us; the launch traced here: 1900 us
  waiting for transfers between devices  1320 us (69%)
  matrix products  342 us (18%)
  blocking collectives  101 us (5%)
  local copies, waits for them, and re-layouts  50 us (3%)
  other arithmetic  37.6 us (2%)
  starting transfers between devices  30.7 us (2%)
    reduce_scatter x1, waiting for transfers between devices, reduce_each(): lax.psum_scatter(grad_up, 'dp', scatter_dimension=0, tiled=True)  213 us
    reduce_scatter x1, waiting for transfers between devices, reduce_each(): lax.psum_scatter(grad_down, 'dp', scatter_dimension=0, tiled=True)  212 us
    reduce_scatter x1, waiting for transfers between devices, reduce_each(): lax.psum_scatter(grad_gate, 'dp', scatter_dimension=0, tiled=True)  210 us
    reduce_scatter x1, waiting for transfers between devices, reduce_each(): lax.psum_scatter(grad_out, 'dp', scatter_dimension=0, tiled=True)  140 us
    reduce_scatter x1, waiting for transfers between devices, reduce_each(): lax.psum_scatter(grad_query, 'dp', scatter_dimension=0, tiled=True)  140 us
    unnamed x2, blocking collectives  81.8 us
    dot_general x14, matrix products, tdot(): lax.dot_general(left, right, (((0,), (0,)), ((), ())), preferred_element_...  80.6 us
    all_gather x1, waiting for transfers between devices, gather_all(): lax.all_gather(w_down, 'dp', axis=0, tiled=True)  77.2 us
  transfers between devices with their start and end apart: 21, of which 15 were waited for; matrix products, arithmetic and copies ran while one was open for 17% of the time, Pallas kernels for 0%

commit v1 on v0

v1 whole, which is shorter than its diff:
```python
from functools import partial

import jax
import jax.numpy as jnp
from jax import lax
from jax.experimental import pallas as pl
from jax.experimental.pallas import tpu as pltpu
from jax.sharding import PartitionSpec as P

QUERY_HEADS = 16
KEY_VALUE_HEADS = 8
HEAD_SIZE = 64
WINDOW_TOKENS = 256
MICRO = 2


EPS = 1e-05
THETA = 1000000.0
NEGATIVE = -1e30


def tdot(left, right):
    return lax.dot_general(
        left, right, (((0,), (0,)), ((), ())), preferred_element_type=jnp.float32
    )


def ntdot(left, right):
    return lax.dot_general(
        left, right, (((1,), (1,)), ((), ())), preferred_element_type=jnp.float32
    )


def norm_rows(values, gain):
    inverse = lax.rsqrt(jnp.mean(values * values, axis=-1, keepdims=True) + EPS)
    return (values * inverse * gain, inverse)


def norm_back(grad, values, inverse, gain):
    scaled = grad * gain
    grad_values = inverse * scaled - values * inverse * inverse * inverse * jnp.mean(
        scaled * values, axis=-1, keepdims=True
    )
    return (grad_values, grad * values * inverse)


def tables(positions, half_dim):
    steps_index = jnp.arange(half_dim, dtype=jnp.float32)
    inverse_freq = THETA ** (-steps_index / half_dim)
    angles = positions.astype(jnp.float32)[:, None] * inverse_freq[None, :]
    return (jnp.cos(angles), jnp.sin(angles))


def rotate_halves(values, cosine_table, sine_table, direction):
    half_dim = values.shape[-1] // 2
    lower_half = values[..., :half_dim]
    upper_half = values[..., half_dim:]
    return jnp.concatenate(
        [
            lower_half * cosine_table - direction * upper_half * sine_table,
            upper_half * cosine_table + direction * lower_half * sine_table,
        ],
        axis=-1,
    )


def layout(lengths_row, feature_width):
    places = jnp.arange(feature_width, dtype=jnp.int32)
    ends = jnp.cumsum(lengths_row)
    segment = jnp.sum((places[:, None] >= ends[None, :]).astype(jnp.int32), axis=1)
    starts = ends - lengths_row
    picked = segment[:, None] == jnp.arange(lengths_row.shape[0], dtype=jnp.int32)[None, :]
    begins = jnp.sum(jnp.where(picked, starts[None, :], 0), axis=1)
    allowed = (segment[:, None] == segment[None, :]) & (places[None, :] <= places[:, None])
    return (places - begins, allowed)


def masked_scores(allowed, query_block, key_block):
    factor = query_block.shape[-1] ** (-0.5)
    scores = (
        jnp.einsum("qrd,td->rqt", query_block, key_block, preferred_element_type=jnp.float32)
        * factor
    )
    return jnp.where(allowed[None], scores, NEGATIVE)


def attend_forward(allowed, blocks):
    query_block, key_block, value_block = blocks
    scores = masked_scores(allowed, query_block, key_block)
    row_max = jnp.max(scores, axis=-1, keepdims=True)
    exponent = jnp.exp(scores - row_max)
    totals = jnp.sum(exponent, axis=-1, keepdims=True)
    rounded_probs = (exponent / totals).astype(jnp.bfloat16)
    head_mixture = jnp.einsum(
        "rqt,td->qrd", rounded_probs, value_block, preferred_element_type=jnp.float32
    )
    return (head_mixture, (row_max + jnp.log(totals))[..., 0])


def attend_backward(allowed, blocks):
    query_block, key_block, value_block, grad_block, log_totals = blocks
    factor = query_block.shape[-1] ** (-0.5)
    scores = masked_scores(allowed, query_block, key_block)
    probs = jnp.exp(scores - log_totals[..., None])
    rounded_probs = probs.astype(jnp.bfloat16)
    grad_probs = jnp.einsum(
        "qrd,td->rqt", grad_block, value_block, preferred_element_type=jnp.float32
    )
    grad_value = jnp.einsum(
        "rqt,qrd->td", rounded_probs, grad_block, preferred_element_type=jnp.float32
    )
    inner = jnp.sum(probs * grad_probs, axis=-1, keepdims=True)
    grad_scores = (probs * (grad_probs - inner)).astype(jnp.bfloat16)
    grad_query = (
        jnp.einsum("rqt,td->qrd", grad_scores, key_block, preferred_element_type=jnp.float32)
        * factor
    )
    grad_key = (
        jnp.einsum("rqt,qrd->td", grad_scores, query_block, preferred_element_type=jnp.float32)
        * factor
    )
    return (grad_query, grad_key, grad_value)


def hop(values, bit, count):
    return lax.ppermute(values, "dp", [(i, i ^ (1 << bit)) for i in range(count)])


def owner_select(place, order, count, width):
    share = width // count
    bits = len(order)
    column = jnp.arange(width, dtype=jnp.int32)
    block = column // share
    mask = jnp.zeros_like(block)
    for at, bit in enumerate(order):
        mask = mask | (((block >> (bits - 1 - at)) & 1) << bit)
    feature = (place ^ mask) * share + column % share
    return (jnp.arange(width, dtype=jnp.int32)[:, None] == feature[None, :]).astype(jnp.bfloat16)


def select_rows(select, values):
    return lax.dot_general(
        select, values, (((0,), (1,)), ((), ())), preferred_element_type=jnp.float32
    ).astype(jnp.bfloat16)


def scatter_rest(kept, received, order, count):
    for bit in order:
        half = kept.shape[0] // 2
        sent = (kept[half:].astype(jnp.float32) + received[half:].astype(jnp.float32)).astype(jnp.bfloat16)
        kept = (kept[:half].astype(jnp.float32) + received[:half].astype(jnp.float32)).astype(jnp.bfloat16)
        received = hop(sent, bit, count)
    return kept.astype(jnp.float32) + received.astype(jnp.float32)


def product_scatter(parts, right, order, count):
    dot = lambda left: jnp.dot(left, right, preferred_element_type=jnp.float32)
    quarter = parts[0].shape[0]
    first = jnp.concatenate([dot(parts[2]).astype(jnp.bfloat16), dot(parts[3]).astype(jnp.bfloat16)], axis=0)
    got = hop(first, order[0], count)
    second = (dot(parts[1]) + got[quarter:].astype(jnp.float32)).astype(jnp.bfloat16)
    received = hop(second, order[1], count)
    kept = (dot(parts[0]) + got[:quarter].astype(jnp.float32)).astype(jnp.bfloat16)
    return scatter_rest(kept, received, order[2:], count)


def quarters(values):
    rows = values.shape[0] // 4
    return [values[i * rows : (i + 1) * rows] for i in range(4)]


def forward_kernel(n2_ref, gate_ref, up_ref, gp_ref, up_out_ref, hid_ref):
    n2 = n2_ref[...]
    gate = jnp.dot(n2, gate_ref[...], preferred_element_type=jnp.float32)
    up = jnp.dot(n2, up_ref[...], preferred_element_type=jnp.float32)
    hidden = gate * jax.nn.sigmoid(gate) * up
    gp_ref[...] = gate.astype(jnp.bfloat16)
    up_out_ref[...] = up.astype(jnp.bfloat16)
    hid_ref[...] = hidden.T.astype(jnp.bfloat16)


def ffn_forward(normed, weight):
    rows, width = normed.shape
    hidden = weight.shape[1] // 2
    tile = 512
    steps = hidden // tile
    shape = jax.ShapeDtypeStruct((rows, hidden), jnp.bfloat16)
    return pl.pallas_call(
        forward_kernel,
        grid=(steps,),
        in_specs=[
            pl.BlockSpec((rows, width), lambda j: (0, 0)),
            pl.BlockSpec((width, tile), lambda j: (0, j)),
            pl.BlockSpec((width, tile), lambda j: (0, j + steps)),
        ],
        out_specs=[
            pl.BlockSpec((rows, tile), lambda j: (0, j)),
            pl.BlockSpec((rows, tile), lambda j: (0, j)),
            pl.BlockSpec((tile, rows), lambda j: (j, 0)),
        ],
        out_shape=[shape, shape, jax.ShapeDtypeStruct((hidden, rows), jnp.bfloat16)],
        compiler_params=pltpu.CompilerParams(vmem_limit_bytes=48 << 20),
        cost_estimate=pl.CostEstimate(
            flops=4 * rows * width * hidden, bytes_accessed=4 * width * hidden + 6 * rows * hidden, transcendentals=rows * hidden
        ),
    )(normed, weight, weight)


def backward_kernel(gp_ref, up_ref, dy_ref, h1_ref, gate_ref, upw_ref, down_ref, dg_ref, du_ref, y_ref, dn_ref, acc_y, acc_n):
    j = pl.program_id(0)

    @pl.when(j == 0)
    def _():
        acc_y[...] = h1_ref[...]
        acc_n[...] = jnp.zeros_like(acc_n)

    gate = gp_ref[...].astype(jnp.float32)
    up = up_ref[...].astype(jnp.float32)
    down = down_ref[...]
    dhid = lax.dot_general(dy_ref[...], down, (((1,), (1,)), ((), ())), preferred_element_type=jnp.float32)
    sig = jax.nn.sigmoid(gate)
    silu = gate * sig
    dgate = (dhid * up * (sig + silu * (1.0 - sig))).astype(jnp.bfloat16)
    dup = (dhid * silu).astype(jnp.bfloat16)
    dg_ref[...] = dgate
    du_ref[...] = dup
    acc_y[...] += jnp.dot((silu * up).astype(jnp.bfloat16), down, preferred_element_type=jnp.float32)
    acc_n[...] += ntdot(dgate, gate_ref[...]) + ntdot(dup, upw_ref[...])

    @pl.when(j == pl.num_programs(0) - 1)
    def _():
        y_ref[...] = acc_y[...].astype(jnp.bfloat16)
        dn_ref[...] = acc_n[...]


def ffn_backward(gate, up, grads, resid, weight, down):
    rows, hidden = gate.shape
    width = grads.shape[1]
    tile = 512
    steps = hidden // tile
    shape = jax.ShapeDtypeStruct((rows, hidden), jnp.bfloat16)
    whole = pl.BlockSpec((rows, width), lambda j: (0, 0))
    cut = pl.BlockSpec((rows, tile), lambda j: (0, j))
    return pl.pallas_call(
        backward_kernel,
        grid=(steps,),
        in_specs=[
            cut,
            cut,
            whole,
            whole,
            pl.BlockSpec((width, tile), lambda j: (0, j)),
            pl.BlockSpec((width, tile), lambda j: (0, j + steps)),
            pl.BlockSpec((tile, width), lambda j: (j, 0)),
        ],
        out_specs=[cut, cut, whole, whole],
        out_shape=[
            shape,
            shape,
            jax.ShapeDtypeStruct((rows, width), jnp.bfloat16),
            jax.ShapeDtypeStruct((rows, width), jnp.float32),
        ],
        scratch_shapes=[pltpu.VMEM((rows, width), jnp.float32), pltpu.VMEM((rows, width), jnp.float32)],
        compiler_params=pltpu.CompilerParams(vmem_limit_bytes=56 << 20),
        cost_estimate=pl.CostEstimate(
            flops=8 * rows * width * hidden, bytes_accessed=6 * width * hidden + 8 * rows * hidden, transcendentals=rows * hidden
        ),
    )(gate, up, grads, resid, weight, weight, down)


def gather(values):
    return lax.all_gather(values, "dp", axis=0, tiled=True)


def per_device(
    tokens,
    cotangent,
    route,
    lengths,
    attn_gain,
    w_query,
    key_weight,
    value_weight,
    query_gain,
    key_norm_gain,
    w_out,
    ffn_gain,
    w_gate,
    w_up,
    w_down,
):
    f32 = jnp.float32
    low = jnp.bfloat16
    count = lax.axis_size("dp")
    levels = count.bit_length() - 1
    place = lax.axis_index("dp")
    window = WINDOW_TOKENS
    share = window // count
    width = tokens.shape[1]
    share_width = width // count
    q_width = QUERY_HEADS * HEAD_SIZE
    k_width = KEY_VALUE_HEADS * HEAD_SIZE
    rows = MICRO * window
    plain = list(range(levels))
    turned = [0, 2, 1] + list(range(3, levels))

    orders = route[0].reshape(MICRO, count, share).transpose(1, 0, 2).reshape(rows)
    deal = (orders[:, None] == jnp.arange(rows, dtype=jnp.int32)[None, :]).astype(low)

    def exchange(values):
        return lax.all_to_all(values, "dp", split_axis=0, concat_axis=0, tiled=True)

    def to_windows(values):
        sent = jnp.dot(deal, values, preferred_element_type=f32).astype(low)
        got = exchange(sent).reshape(count, MICRO, share, width)
        return got.transpose(1, 0, 2, 3).reshape(rows, width)

    def from_windows(values):
        sent = values.reshape(MICRO, count, share, width).transpose(1, 0, 2, 3).reshape(rows, width)
        return tdot(deal, exchange(sent)).astype(low)

    gains = jnp.pad(jnp.stack([attn_gain, ffn_gain], axis=1), ((0, 0), (0, 126)))
    attn_all = gather(jnp.concatenate([w_query, key_weight, value_weight, w_out, gains], axis=1))
    gate_up_all = gather(jnp.concatenate([w_gate, w_up], axis=1))
    down_all = gather(w_down)
    qkv_all = attn_all[:, : q_width + 2 * k_width]
    out_all = attn_all[:, q_width + 2 * k_width : q_width + 2 * k_width + width]
    gain_columns = attn_all[:, q_width + 2 * k_width + width :].astype(f32)
    attn_gain_all = gain_columns[:, 0]
    ffn_gain_all = gain_columns[:, 1]

    window_tokens = to_windows(tokens)
    window_grads = to_windows(cotangent)

    inputs = window_tokens.astype(f32)
    normed, inverse_one = norm_rows(inputs, attn_gain_all)
    normed_low = normed.astype(low)
    proj = jnp.dot(normed_low, qkv_all, preferred_element_type=f32)
    q_gain = query_gain.astype(f32)
    k_gain = key_norm_gain.astype(f32)
    query_proj = proj[:, :q_width].reshape(rows, QUERY_HEADS, HEAD_SIZE)
    key_proj = proj[:, q_width : q_width + k_width].reshape(rows, KEY_VALUE_HEADS, HEAD_SIZE)
    value_low = proj[:, q_width + k_width :].astype(low).reshape(rows, KEY_VALUE_HEADS, HEAD_SIZE)
    layouts = [layout(lengths[m], window) for m in range(MICRO)]
    positions = jnp.concatenate([l[0] for l in layouts])
    cosine_table, sine_table = tables(positions, HEAD_SIZE // 2)
    cosine_table = cosine_table[:, None, :]
    sine_table = sine_table[:, None, :]
    query_hat, query_inv = norm_rows(query_proj, q_gain)
    key_hat, key_inv = norm_rows(key_proj, k_gain)
    query_low = rotate_halves(query_hat, cosine_table, sine_table, 1.0).astype(low)
    key_low = rotate_halves(key_hat, cosine_table, sine_table, 1.0).astype(low)
    group = QUERY_HEADS // KEY_VALUE_HEADS

    def heads(values, per):
        return jnp.moveaxis(values.reshape(MICRO, window, KEY_VALUE_HEADS, per, HEAD_SIZE), 2, 1)

    q_heads = heads(query_low, group)
    k_heads = heads(key_low, 1)[:, :, :, 0]
    v_heads = heads(value_low, 1)[:, :, :, 0]
    mixtures = []
    logs = []
    for m in range(MICRO):
        mixture, log_totals = lax.map(partial(attend_forward, layouts[m][1]), (q_heads[m], k_heads[m], v_heads[m]))
        mixtures.append(jnp.moveaxis(mixture, 0, 1).reshape(window, q_width).astype(low))
        logs.append(log_totals)
    attended = jnp.concatenate(mixtures, axis=0)
    resid = inputs + jnp.dot(attended, out_all, preferred_element_type=f32)
    normed_two, inverse_two = norm_rows(resid, ffn_gain_all)
    ffn_low = normed_two.astype(low)

    gate_proj, up_proj, hidden_t = ffn_forward(ffn_low, gate_up_all)
    hid_blocks = hidden_t.reshape(-1, 2, 2, 2, w_down.shape[0], rows)

    down_parts = []
    bit_c = place & 1
    bit_x = (place >> 1) & 1
    for flip_c in (0, 1):
        for flip_x in (0, 1):
            part = lax.dynamic_index_in_dim(hid_blocks, bit_c ^ flip_c, 3, False)
            part = lax.dynamic_index_in_dim(part, bit_x ^ flip_x, 2, False)
            down_parts.append(part.reshape(-1, rows))
    dot_down = lambda left: jnp.dot(left, window_grads, preferred_element_type=f32)
    quarter = down_parts[0].shape[0]
    first = jnp.concatenate([dot_down(down_parts[2]).astype(low), dot_down(down_parts[3]).astype(low)], axis=0)
    got = hop(first, 0, count)
    second = (dot_down(down_parts[1]) + got[quarter:].astype(f32)).astype(low)
    received = hop(second, 1, count)
    kept = (dot_down(down_parts[0]) + got[:quarter].astype(f32)).astype(low)
    for bit in range(2, levels):
        shape = (-1, 2, w_down.shape[0], width)
        mine = (place >> bit) & 1
        kept = kept.reshape(shape)
        received = received.reshape(shape)
        both = lambda at: (
            lax.dynamic_index_in_dim(kept, at, 1, False).astype(f32)
            + lax.dynamic_index_in_dim(received, at, 1, False).astype(f32)
        ).astype(low)
        sent = both(1 - mine)
        kept = both(mine)
        received = hop(sent, bit, count)
    grad_down = (kept.astype(f32) + received.astype(f32)).reshape(w_down.shape)

    grad_gate_low, grad_up_low, output, grad_normed_two = ffn_backward(
        gate_proj, up_proj, window_grads, resid, gate_up_all, down_all
    )
    output_rows = from_windows(output)

    select_plain = owner_select(place, plain, count, width)
    select_turned = owner_select(place, turned, count, width)
    grad_gate = product_scatter(quarters(select_rows(select_turned, ffn_low)), grad_gate_low, turned, count)
    ffn_plain = quarters(select_rows(select_plain, ffn_low))
    grad_up = product_scatter(ffn_plain, grad_up_low, plain, count)

    grad_resid_part, ffn_rows = norm_back(grad_normed_two, resid, inverse_two, ffn_gain_all)
    grad_resid = window_grads.astype(f32) + grad_resid_part
    branch_low = grad_resid.astype(low)
    att_gradient = ntdot(branch_low, out_all).astype(low)
    grad_out = product_scatter(quarters(select_rows(select_turned, attended)), branch_low, turned, count)
    head_gradient = heads(att_gradient, group)
    back_parts = [
        lax.map(
            partial(attend_backward, layouts[m][1]),
            (q_heads[m], k_heads[m], v_heads[m], head_gradient[m], logs[m]),
        )
        for m in range(MICRO)
    ]

    def join(at, per):
        return jnp.concatenate([jnp.moveaxis(b[at], 0, 1).reshape(window, per, HEAD_SIZE) for b in back_parts], axis=0)

    dq_rot = join(0, QUERY_HEADS)
    dk_rot = join(1, KEY_VALUE_HEADS)
    dv_low = join(2, KEY_VALUE_HEADS).reshape(rows, k_width).astype(low)
    dq_hat = rotate_halves(dq_rot, cosine_table, sine_table, -1.0)
    dk_hat = rotate_halves(dk_rot, cosine_table, sine_table, -1.0)
    dq_proj, query_rows = norm_back(dq_hat, query_proj, query_inv, q_gain)
    dk_proj, key_rows = norm_back(dk_hat, key_proj, key_inv, k_gain)
    dqkv = jnp.concatenate(
        [dq_proj.reshape(rows, q_width).astype(low), dk_proj.reshape(rows, k_width).astype(low), dv_low], axis=1
    )
    grad_qkv = product_scatter(quarters(select_rows(select_plain, normed_low)), dqkv, plain, count)
    grad_normed = ntdot(dqkv, qkv_all)
    grad_input_part, attn_rows = norm_back(grad_normed, inputs, inverse_one, attn_gain_all)
    input_grad = (grad_resid + grad_input_part).astype(low)
    grad_rows = from_windows(input_grad)

    small = jnp.concatenate(
        [
            jnp.sum(attn_rows, axis=0),
            jnp.sum(ffn_rows, axis=0),
            jnp.sum(query_rows, axis=(0, 1)),
            jnp.sum(key_rows, axis=(0, 1)),
        ]
    ).reshape(-1, 128)
    for bit in range(levels):
        small = small + hop(small, bit, count)
    small = small.reshape(-1)
    own = lambda start: lax.dynamic_slice(small, (start + place * share_width,), (share_width,))
    return (
        output_rows,
        grad_rows,
        own(0),
        grad_qkv[:, :q_width],
        grad_qkv[:, q_width : q_width + k_width],
        grad_qkv[:, q_width + k_width :],
        small[2 * width : 2 * width + HEAD_SIZE],
        small[2 * width + HEAD_SIZE :],
        grad_out,
        own(width),
        grad_gate,
        grad_up,
        grad_down,
    )


def solution(mesh):
    in_specs = (
        P("dp", None),
        P("dp", None),
        P("dp", None),
        P("dp", None),
        P("dp"),
        P("dp", None),
        P("dp", None),
        P("dp", None),
        P(),
        P(),
        P("dp", None),
        P("dp"),
        P("dp", None),
        P("dp", None),
        P("dp", None),
    )
    out_specs = (
        P("dp", None),
        P("dp", None),
        P("dp"),
        P("dp", None),
        P("dp", None),
        P("dp", None),
        P(),
        P(),
        P("dp", None),
        P("dp"),
        P("dp", None),
        P("dp", None),
        P("dp", None),
    )
    return jax.shard_map(
        per_device, mesh=mesh, in_specs=in_specs, out_specs=out_specs, check_vma=False
    )
```

time: 1910 us -> 879 us (0.46)
  waiting for transfers between devices: 1320 us -> 361 us
  matrix products: 342 us -> 235 us
  blocking collectives: 101 us -> 0 us
  Pallas kernels: 0 us -> 49.4 us
  other arithmetic: 37.6 us -> 70.8 us
  local copies, waits for them, and re-layouts: 50 us -> 83.1 us
  starting transfers between devices: 30.7 us -> 52.7 us
    reduce_scatter x7 -> x0, waiting for transfers between devices: 979 us -> none  [the longest x1 213 us: reduce_each(): lax.psum_scatter(grad_up, 'dp', scatter_dimension=0, tiled=True)]
    all_gather x7 -> x3, waiting for transfers between devices: 309 us -> 98.7 us  [gather(): return lax.all_gather(values, 'dp', axis=0, tiled=True)]
    ppermute x0 -> x30, waiting for transfers between devices: none -> 192 us  [hop(): return lax.ppermute(values, 'dp', [(i, i ^ 1 << bit) for i in range(count)])]
    unnamed x2 -> x0, blocking collectives: 81.8 us -> none
    dot_general x14 -> x2, matrix products: 80.6 us -> 4.82 us  [tdot(): lax.dot_general(left, right, (((0,), (0,)), ((), ())), preferred_element_...]
    pallas_call x0 -> x2, Pallas kernels: none -> 49.4 us  [the longest x1 32 us: ffn_backward(): pl.pallas_call(backward_kernel, grid=(steps,), in_specs=[cut, cut, whole,...]
    dot_general x14 -> x2, matrix products: 59.5 us -> 10.3 us  [ntdot(): lax.dot_general(left, right, (((1,), (1,)), ((), ())), preferred_element_...]
    all_to_all x7 -> x4, waiting for transfers between devices: 27.8 us -> 69.6 us  [exchange(): return lax.all_to_all(values, 'dp', split_axis=0, concat_axis=0, tiled=True)]
  transfers between devices with their start and end apart: 21 -> 37, of which waited for: 15 -> 19; matrix products, arithmetic and copies ran while one was open for 17% -> 20% of each run, Pallas kernels for 0% -> 2%
where the time goes in v1:
time: 879 us; the launch traced here: 869 us
  waiting for transfers between devices  361 us (41%)
  matrix products  235 us (27%)
  local copies, waits for them, and re-layouts  83.1 us (9%)
  other arithmetic  70.8 us (8%)
  starting transfers between devices  52.7 us (6%)
  Pallas kernels  49.4 us (6%)
  between operations  15.3 us (2%)
    ppermute x30, waiting for transfers between devices, hop(): return lax.ppermute(values, 'dp', [(i, i ^ 1 << bit) for i in range(count)])  192 us
    all_gather x3, waiting for transfers between devices, gather(): return lax.all_gather(values, 'dp', axis=0, tiled=True)  98.7 us
    all_to_all x4, waiting for transfers between devices, exchange(): return lax.all_to_all(values, 'dp', split_axis=0, concat_axis=0, tiled=True)  69.6 us
    dot_general x16, matrix products, product_scatter(): dot = lambda left: jnp.dot(left, right, preferred_element_type=jnp.float32)  44.4 us
    dot_general x32, matrix products, masked_scores(): jnp.einsum('qrd,td->rqt', query_block, key_block, preferred_element_type=...  37.4 us
    ppermute x30, starting transfers between devices, hop(): return lax.ppermute(values, 'dp', [(i, i ^ 1 << bit) for i in range(count)])  34.4 us
    pallas_call x1, Pallas kernels, ffn_backward(): pl.pallas_call(backward_kernel, grid=(steps,), in_specs=[cut, cut, whole,...  32 us
    dot_general x16, matrix products, attend_backward(): jnp.einsum('rqt,qrd->td', grad_scores, query_block, preferred_element_typ...  26.8 us
  transfers between devices with their start and end apart: 37, of which 19 were waited for; matrix products, arithmetic and copies ran while one was open for 20% of the time, Pallas kernels for 2%

profile of v1, /device:TPU:0, one launch (start us, length us, event | category | flops | bytes accessed | tf_op | source)
XLA Modules:
  0.0 868.8 jit_solution(8164642927783278824)
XLA Ops:
  17.2 7.3 all-to-all-start
  32.3 30.9 %all-to-all-done = bf16[32,16,1024]{2,1,0:T(8,128)(2,1)S(1)} async-done(((bf16[32,16,1024]{2,1,0:T(8,128)(2,1)}), bf16[32,16,1024]{2,1,0:T(8,128)(2,1)S(1)}, u32[]{:S(2)}, u32[]{:S(2)}) %all-to-all-start) | async-done | bytes 1048608 | tf_op jit(solution)/shard_map/all_to_all | solution.py:311
  63.1 3.6 all-to-all-start.1
  71.7 38.7 %all-to-all-done.1 = bf16[32,16,1024]{2,1,0:T(8,128)(2,1)} async-done(((bf16[32,16,1024]{2,1,0:T(8,128)(2,1)}), bf16[32,16,1024]{2,1,0:T(8,128)(2,1)}, u32[]{:S(2)}, u32[]{:S(2)}) %all-to-all-start.1) | async-done | bytes 1048608 | tf_op jit(solution)/shard_map/all_to_all | solution.py:311
  110.4 2.3 copy.224
  115.0 4.9 fusion.107
  143.3 23.3 %while.56 = (s32[]{:T(128)}, bf16[8,256,2,64]{1,3,2,0:T(8,128)(2,1)S(1)}, f32[8,2,256]{2,1,0:T(2,128)}, bf16[8,256,64]{1,2,0:T(8,128)(2,1)}, bf16[8,256,64]{1,2,...) while((s32[]{:T(128)}, ...), condition=%wide.region_12.13_spmd.clone, body=%wide.region_9.12_spmd.clone.sunk | while | flops 34799104 | bytes 1986133 | solution.py:364
  167.4 23.8 %while.57 = (s32[]{:T(128)}, bf16[8,256,2,64]{1,3,2,0:T(8,128)(2,1)S(1)}, f32[8,2,256]{2,1,0:T(2,128)}, bf16[8,256,64]{1,2,0:T(8,128)(2,1)}, bf16[8,256,64]{1,2,...) while((s32[]{:T(128)}, ...), condition=%wide.region_16.17_spmd.clone, body=%wide.region_13.16_spmd.clone.sunk | while | flops 34799104 | bytes 1986133 | solution.py:364
  191.2 3.2 multiply_reduce_fusion.6
  194.4 2.3 fusion.144
  199.9 2.3 fusion.138
  202.2 35.0 %all-gather.6.cloned.1.call-done.gate_ref.up_ref.upw_ref = bf16[1024,9216]{1,0:T(8,128)(2,1)} async-done(((bf16[32,9216]{1,0:T(8,128)(2,1)}), bf16[1024,9216]{1,0:T(8,128)(2,1)}) %all-gather.6.cloned.1.call-update) | async-done | bytes 18874384 | tf_op jit(solution)/shard_map/all_gather | solution.py:272
  237.2 17.4 %shard_map.246 = (bf16[512,4608]{1,0:T(8,128)(2,1)S(1)}, bf16[512,4608]{1,0:T(8,128)(2,1)}, bf16[4608,512]{1,0:T(8,128)(2,1)}) custom-call(bf16[512,1024]{1,0:T(8,128)(2,1)S(1)} %multiply_convert_fusion.2.n2_ref, bf16[1024,9216]{1,0:T(8,128)(2,1)} %all-gather.6.cloned.1.call-done.gate_ref.up_ref.upw_ref, ...), custom_call_target="tpu_custom_call" | custom-call | flops 9663676416 | bytes 33030144 | tf_op jit(solution)/shard_map/pallas_call | solution.py:188
  256.7 63.7 %all-gather.8.cloned.1.call-done.down_ref = bf16[4608,1024]{1,0:T(8,128)(2,1)} async-done(((bf16[144,1024]{1,0:T(8,128)(2,1)}), bf16[4608,1024]{1,0:T(8,128)(2,1)}) %all-gather.8.cloned.1.call-update) | async-done | bytes 9437200 | tf_op jit(solution)/shard_map/all_gather | solution.py:272
  320.4 32.0 %shard_map.247 = (bf16[512,4608]{1,0:T(8,128)(2,1)}, bf16[512,4608]{1,0:T(8,128)(2,1)}, bf16[512,1024]{1,0:T(8,128)(2,1)}, f32[512,1024]{1,0:T(8,128)}) custom-call(bf16[512,4608]{1,0:T(8,128)(2,1)} %copy-done.2, bf16[512,4608]{1,0:T(8,128)(2,1)} %get-tuple-element.207.up_ref, bf16[512,1024]{1,0:T(8,128)(2,1)} %bitcast.454, f32[512,1024]{1,0:T(8,128)} %copy-done.3, ...), custom_call_target="tpu_custom_call" | custom-call | flops 19327352832 | bytes 47185920 | tf_op jit(solution)/shard_map/pallas_call | solution.py:244
  352.4 5.3 convolution_convert_fusion
  357.7 2.8 convolution_convert_fusion.1
  360.5 2.9 convolution_convert_fusion.2
  363.4 4.0 convolution_convert_fusion.3
  372.4 2.9 fusion.132
  378.0 2.3 fusion.243
  383.1 64.9 %while.58 = (s32[]{:T(128)}, f32[8,256,2,64]{1,3,2,0:T(8,128)}, f32[8,256,64]{1,2,0:T(8,128)}, bf16[8,256,64]{1,2,0:T(8,128)(2,1)}, bf16[8,256,64]{1,2,0:T(8,128...) while((s32[]{:T(128)}, f32[8,256,2,64]{1,3,2,0:T(8,128)}, ...), condition=%wide.region_21.22_spmd.clone, body=%wide.region_19.21_spmd.clone.sunk | while | flops 85310976 | bytes 4702321 | solution.py:422
  452.1 60.1 %while.59 = (s32[]{:T(128)}, f32[8,256,2,64]{1,3,2,0:T(8,128)}, f32[8,256,64]{1,2,0:T(8,128)}, bf16[8,256,64]{1,2,0:T(8,128)(2,1)S(1)}, bf16[8,256,64]{1,2,0:T(8...) while((s32[]{:T(128)}, f32[8,256,2,64]{1,3,2,0:T(8,128)}, ...), condition=%wide.region_24.25_spmd.clone, body=%wide.region_22.24_spmd.clone.sunk | while | flops 85310976 | bytes 4702321 | solution.py:422
  512.3 2.4 multiply_subtract_fusion
  518.2 2.9 copy.232
  521.1 3.1 copy.227
  528.2 2.6 copy.238
  534.1 4.8 multiply_reduce_fusion.2
  549.6 2.9 pad_maximum_fusion.2
  553.7 2.5 pad_maximum_fusion.1
  558.0 7.4 fusion.121
  565.8 3.3 pad_maximum_fusion.5
  570.7 2.3 collective-permute-done.1
  574.5 2.9 add_convert_fusion.14
  578.4 3.5 all-to-all-start.3
  583.7 4.1 pad_maximum_fusion
  587.8 11.8 %collective-permute-done.3 = f32[17,128]{1,0:T(8,128)S(1)} collective-permute-done((f32[17,128]{1,0:T(8,128)S(1)}, f32[17,128]{1,0:T(8,128)S(1)}, u32[]{:S(2)}, u32[]{:S(2)}) %collective-permute-start.3) | collective-permute-done | bytes 8736 | tf_op jit(solution)/shard_map/ppermute | solution.py:126
  599.6 4.6 collective-permute-start.4
  607.3 3.5 fusion.251
  613.6 5.4 collective-permute-done.11
  621.1 3.0 add_convert_fusion.12
  624.4 3.4 collective-permute-done.12
  629.3 3.8 all-to-all-start.2
  633.1 2.7 collective-permute-start.14
  635.9 2.7 add_convert_fusion.13
  638.5 19.1 %collective-permute-done.6 = bf16[256,2048]{1,0:T(8,128)(2,1)S(1)} collective-permute-done((bf16[256,2048]{1,0:T(8,128)(2,1)}, bf16[256,2048]{1,0:T(8,128)(2,1)S(1)}, u32[]{:S(2)}, u32[]{:S(2)}) %collective-permute-start.6) | collective-permute-done | bytes 1048608 | tf_op jit(solution)/shard_map/ppermute | solution.py:126
  659.6 2.3 collective-permute-done.14
  662.6 3.0 convolution_convert_fusion.8
  665.6 4.8 collective-permute-done.7
  673.7 4.2 collective-permute-done.8
  680.0 5.7 add_convert_fusion.1
  686.9 5.0 add_convert_fusion.2
  695.2 3.5 add_convert_fusion.4
  699.6 3.1 add_convert_fusion.3
  702.7 3.1 add_convert_fusion.5
  705.8 34.2 %collective-permute-done.26 = bf16[1152,1024]{1,0:T(8,128)(2,1)S(1)} collective-permute-done((bf16[1152,1024]{1,0:T(8,128)(2,1)S(1)}, bf16[1152,1024]{1,0:T(8,128)(2,1)S(1)}, u32[]{:S(2)}, u32[]{:S(2)}) %collective-permute-start.26) | collective-permute-done | bytes 2359328 | tf_op jit(solution)/shard_map/ppermute | solution.py:126
  742.2 43.0 %collective-permute-done.21 = bf16[256,4608]{1,0:T(8,128)(2,1)S(1)} collective-permute-done((bf16[256,4608]{1,0:T(8,128)(2,1)S(1)}, bf16[256,4608]{1,0:T(8,128)(2,1)S(1)}, u32[]{:S(2)}, u32[]{:S(2)}) %collective-permute-start.21) | collective-permute-done | bytes 2359328 | tf_op jit(solution)/shard_map/ppermute | solution.py:126
  785.8 2.2 collective-permute-start.22
  790.1 18.0 %collective-permute-done.22 = bf16[128,4608]{1,0:T(8,128)(2,1)S(1)} collective-permute-done((bf16[128,4608]{1,0:T(8,128)(2,1)S(1)}, bf16[128,4608]{1,0:T(8,128)(2,1)S(1)}, u32[]{:S(2)}, u32[]{:S(2)}) %collective-permute-start.22) | collective-permute-done | bytes 1179680 | tf_op jit(solution)/shard_map/ppermute | solution.py:126
  808.3 2.8 collective-permute-start.23
  814.4 18.5 %collective-permute-done.23 = bf16[64,4608]{1,0:T(8,128)(2,1)S(1)} collective-permute-done((bf16[64,4608]{1,0:T(8,128)(2,1)S(1)}, bf16[64,4608]{1,0:T(8,128)(2,1)S(1)}, u32[]{:S(2)}, u32[]{:S(2)}) %collective-permute-start.23) | collective-permute-done | bytes 589856 | tf_op jit(solution)/shard_map/ppermute | solution.py:126
  833.1 9.8 %collective-permute-done.18 = bf16[64,4608]{1,0:T(8,128)(2,1)S(1)} collective-permute-done((bf16[64,4608]{1,0:T(8,128)(2,1)S(1)}, bf16[64,4608]{1,0:T(8,128)(2,1)S(1)}, u32[]{:S(2)}, u32[]{:S(2)}) %collective-permute-start.18) | collective-permute-done | bytes 589856 | tf_op jit(solution)/shard_map/ppermute | solution.py:126
  843.7 11.9 %collective-permute-done.24 = bf16[32,4608]{1,0:T(8,128)(2,1)S(1)} collective-permute-done((bf16[32,4608]{1,0:T(8,128)(2,1)S(1)}, bf16[32,4608]{1,0:T(8,128)(2,1)S(1)}, u32[]{:S(2)}, u32[]{:S(2)}) %collective-permute-start.24) | collective-permute-done | bytes 294944 | tf_op jit(solution)/shard_map/ppermute | solution.py:126
  856.5 3.7 collective-permute-done.19
  (605 shorter events, 305.2 us)
Async XLA Ops:
  7.2 8.3 copy-start
  7.2 105.5 %all-gather.4.cloned.1.call-start = ((), (), s32[]{:S(2)}) async-start(), calls=%async_computation.4 | async-start | bytes 6758400 | tf_op jit(solution)/shard_map/all_gather | solution.py:272
  12.0 225.2 %all-gather.6.cloned.1.call-start = ((), (), s32[]{:S(2)}) async-start(), calls=%async_computation.5 | async-start | bytes 19464192 | tf_op jit(solution)/shard_map/all_gather | solution.py:272
  15.4 15.1 %copy-start.70 = (s32[512]{0:T(512)}, s32[512]{0:T(512)S(1)}, u32[]{:S(2)}) copy-start(s32[512]{0:T(512)S(1)} %eq.47) | copy-start | bytes 6148
  17.2 10.4 %copy-start.75 = (bf16[64]{0:T(256)(128)(2,1)S(1)}, bf16[64]{0:T(256)(128)(2,1)}, u32[]{:S(2)}) copy-start(bf16[64]{0:T(256)(128)(2,1)} %param.31) | copy-start | bytes 388
  17.2 11.0 %copy-start.65 = (s32[2,4]{1,0:T(2,128)S(1)}, s32[2,4]{1,0:T(2,128)}, u32[]{:S(2)}) copy-start(s32[2,4]{1,0:T(2,128)} %param.26) | copy-start | bytes 100
  17.2 11.3 %copy-start.76 = (bf16[64]{0:T(256)(128)(2,1)S(1)}, bf16[64]{0:T(256)(128)(2,1)}, u32[]{:S(2)}) copy-start(bf16[64]{0:T(256)(128)(2,1)} %param.32) | copy-start | bytes 388
  17.2 13.3 %copy-start.77 = (bf16[512,1024]{1,0:T(8,128)(2,1)S(1)}, bf16[512,1024]{1,0:T(8,128)(2,1)}, u32[]{:S(2)}) copy-start(bf16[512,1024]{1,0:T(8,128)(2,1)} %param.24) | copy-start | bytes 3145732
  17.2 45.9 %all-to-all-start = ((bf16[32,16,1024]{2,1,0:T(8,128)(2,1)}), bf16[32,16,1024]{2,1,0:T(8,128)(2,1)S(1)}, u32[]{:S(2)}, u32[]{:S(2)}) async-start(bf16[32,16,1024]{2,1,0:T(8,128)(2,1)} %bitcast.1), calls=%async_computation | async-start | bytes 2097152 | tf_op jit(solution)/shard_map/all_to_all | solution.py:311
  24.5 295.9 %all-gather.8.cloned.1.call-start = ((), (), s32[]{:S(2)}) async-start(), calls=%async_computation.6 | async-start | bytes 9732096 | tf_op jit(solution)/shard_map/all_gather | solution.py:272
  63.1 47.3 %all-to-all-start.1 = ((bf16[32,16,1024]{2,1,0:T(8,128)(2,1)}), bf16[32,16,1024]{2,1,0:T(8,128)(2,1)}, u32[]{:S(2)}, u32[]{:S(2)}) async-start(bf16[32,16,1024]{2,1,0:T(8,128)(2,1)} %bitcast.28), calls=%async_computation.1 | async-start | bytes 2097152 | tf_op jit(solution)/shard_map/all_to_all | solution.py:311
  69.6 44.6 %copy-start.7 = (f32[2,32,8,1024]{3,2,1,0:T(8,128)}, f32[2,32,8,1024]{3,2,1,0:T(8,128)S(1)}, u32[]{:S(2)}) copy-start(f32[2,32,8,1024]{3,2,1,0:T(8,128)S(1)} %copy.215) | copy-start | bytes 6291460
  71.7 43.3 %copy-start.60 = (f32[512]{0:T(512)}, f32[512]{0:T(512)S(1)}, u32[]{:S(2)}) copy-start(f32[512]{0:T(512)S(1)} %rsqrt.36) | copy-start | bytes 6148
  143.3 24.2 %copy-start.29 = (bf16[8,256,2,64]{1,3,2,0:T(8,128)(2,1)S(1)}, bf16[8,256,2,64]{1,3,2,0:T(8,128)(2,1)}, u32[]{:S(2)}) copy-start(bf16[8,256,2,64]{1,3,2,0:T(8,128)(2,1)} %copy-done.28) | copy-start | bytes 1572868
  167.4 23.8 %copy-start.8 = (f32[2,32,8,1024]{3,2,1,0:T(8,128)S(1)}, f32[2,32,8,1024]{3,2,1,0:T(8,128)}, u32[]{:S(2)}) copy-start(f32[2,32,8,1024]{3,2,1,0:T(8,128)} %copy-done.7) | copy-start | bytes 6291460
  198.3 162.2 %copy-start.79 = (bf16[1024,512]{1,0:T(8,128)(2,1)}, bf16[1024,512]{1,0:T(8,128)(2,1)S(1)}, u32[]{:S(2)}) copy-start(bf16[1024,512]{1,0:T(8,128)(2,1)S(1)} %fusion.135) | copy-start | bytes 3145732
  199.9 157.8 %copy-start.81 = (bf16[1024,512]{1,0:T(8,128)(2,1)}, bf16[1024,512]{1,0:T(8,128)(2,1)S(1)}, u32[]{:S(2)}) copy-start(bf16[1024,512]{1,0:T(8,128)(2,1)S(1)} %fusion.141) | copy-start | bytes 3145732
  552.6 127.4 %collective-permute-start.25 = (bf16[2304,1024]{1,0:T(8,128)(2,1)}, bf16[2304,1024]{1,0:T(8,128)(2,1)}, u32[]{:S(2)}, u32[]{:S(2)}) collective-permute-start(bf16[2304,1024]{1,0:T(8,128)(2,1)} %pad_maximum_fusion.2), channel_id=1, source_target_pairs={{0,1},{1,0},{2,3},{3,2},{4,5},{5,4},{6,7},{7,6},{8,9},{9,8},{10,11... | collective-permute-start | bytes 14155784 | tf_op jit(solution)/shard_map/ppermute | solution.py:126
  556.2 130.7 %collective-permute-start.20 = (bf16[512,4608]{1,0:T(8,128)(2,1)}, bf16[512,4608]{1,0:T(8,128)(2,1)}, u32[]{:S(2)}, u32[]{:S(2)}) collective-permute-start(bf16[512,4608]{1,0:T(8,128)(2,1)} %pad_maximum_fusion.1), channel_id=1, source_target_pairs={{0,1},{1,0},{2,3},{3,2},{4,5},{5,4},{6,7},{7,6},{8,9},{9,8},{10,11... | collective-permute-start | bytes 14155784 | tf_op jit(solution)/shard_map/ppermute | solution.py:126
  557.6 46.7 %collective-permute-start.10 = (bf16[512,1024]{1,0:T(8,128)(2,1)}, bf16[512,1024]{1,0:T(8,128)(2,1)}, u32[]{:S(2)}, u32[]{:S(2)}) collective-permute-start(bf16[512,1024]{1,0:T(8,128)(2,1)} %pad_maximum_fusion.9), channel_id=1, source_target_pairs={{0,1},{1,0},{2,3},{3,2},{4,5},{5,4},{6,7},{7,6},{8,9},{9,8},{10,11... | collective-permute-start | bytes 3145736 | tf_op jit(solution)/shard_map/ppermute | solution.py:126
  565.4 9.1 %copy-start.9 = (f32[2,32,8,1024]{3,2,1,0:T(8,128)S(1)}, f32[2,32,8,1024]{3,2,1,0:T(8,128)}, u32[]{:S(2)}) copy-start(f32[2,32,8,1024]{3,2,1,0:T(8,128)} %copy-done.7) | copy-start | bytes 6291460
  565.4 9.1 %copy-start.11 = (f32[512,1024]{1,0:T(8,128)S(1)}, f32[512,1024]{1,0:T(8,128)}, u32[]{:S(2)}) copy-start(f32[512,1024]{1,0:T(8,128)} %get-tuple-element.209) | copy-start | bytes 6291460
  565.4 9.1 %copy-start.59 = (f32[512]{0:T(512)S(1)}, f32[512]{0:T(512)}, u32[]{:S(2)}) copy-start(f32[512]{0:T(512)} %copy-done.58) | copy-start | bytes 6148
  565.4 3.8 collective-permute-start
  569.1 52.0 %collective-permute-start.5 = (bf16[512,2048]{1,0:T(8,128)(2,1)}, bf16[512,2048]{1,0:T(8,128)(2,1)}, u32[]{:S(2)}, u32[]{:S(2)}) collective-permute-start(bf16[512,2048]{1,0:T(8,128)(2,1)} %pad_maximum_fusion.5), channel_id=1, source_target_pairs={{0,1},{1,0},{2,3},{3,2},{4,5},{5,4},{6,7},{7,6},{8,9},{9,8},{10,11... | collective-permute-start | bytes 6291464 | tf_op jit(solution)/shard_map/ppermute | solution.py:126
  569.2 3.7 collective-permute-start.1
  572.9 9.0 %collective-permute-start.2 = (f32[17,128]{1,0:T(8,128)S(1)}, f32[17,128]{1,0:T(8,128)S(1)}, u32[]{:S(2)}, u32[]{:S(2)}) collective-permute-start(f32[17,128]{1,0:T(8,128)S(1)} %fusion.285), channel_id=1, source_target_pairs={{0,4},{1,5},{2,6},{3,7},{4,0},{5,1},{6,2},{7,3},{8,12},{9,13},{10,... | collective-permute-start | bytes 26120 | tf_op jit(solution)/shard_map/ppermute | solution.py:126
  578.4 50.8 %all-to-all-start.3 = ((bf16[32,16,1024]{2,1,0:T(8,128)(2,1)}), bf16[32,16,1024]{2,1,0:T(8,128)(2,1)}, u32[]{:S(2)}, u32[]{:S(2)}) async-start(bf16[32,16,1024]{2,1,0:T(8,128)(2,1)} %bitcast.368), calls=%async_computation.3 | async-start | bytes 2097152 | tf_op jit(solution)/shard_map/all_to_all | solution.py:311
  582.0 22.3 %copy-start.19 = (bf16[512,1024]{1,0:T(8,128)(2,1)S(1)}, bf16[512,1024]{1,0:T(8,128)(2,1)}, u32[]{:S(2)}) copy-start(bf16[512,1024]{1,0:T(8,128)(2,1)} %copy-done.18) | copy-start | bytes 3145732
  582.0 22.2 %copy-start.54 = (bf16[1024,512]{1,0:T(8,128)(2,1)S(1)}, bf16[1024,512]{1,0:T(8,128)(2,1)}, u32[]{:S(2)}) copy-start(bf16[1024,512]{1,0:T(8,128)(2,1)} %fusion.144) | copy-start | bytes 3145732
  582.0 17.6 %collective-permute-start.3 = (f32[17,128]{1,0:T(8,128)S(1)}, f32[17,128]{1,0:T(8,128)S(1)}, u32[]{:S(2)}, u32[]{:S(2)}) collective-permute-start(f32[17,128]{1,0:T(8,128)S(1)} %add.397), channel_id=1, source_target_pairs={{0,8},{1,9},{2,10},{3,11},{4,12},{5,13},{6,14},{7,15},{8,0},{9,1},... | collective-permute-start | bytes 26120 | tf_op jit(solution)/shard_map/ppermute | solution.py:126
  587.8 19.5 %copy-start.35 = (bf16[4,2,1,1,144,512]{5,4,3,2,1,0:T(8,128)(2,1)S(1)}, bf16[4,2,1,1,144,512]{5,4,3,2,1,0:T(8,128)(2,1)}, u32[]{:S(2)}) copy-start(bf16[4,2,1,1,144,512]{5,4,3,2,1,0:T(8,128)(2,1)} %get-tuple-element.392) | copy-start | bytes 3538948
  599.6 12.3 %collective-permute-start.4 = (f32[17,128]{1,0:T(8,128)S(1)}, f32[17,128]{1,0:T(8,128)S(1)}, u32[]{:S(2)}, u32[]{:S(2)}) collective-permute-start(f32[17,128]{1,0:T(8,128)S(1)} %add.398), channel_id=1, source_target_pairs={{0,16},{1,17},{2,18},{3,19},{4,20},{5,21},{6,22},{7,23},{8,24},{9,... | collective-permute-start | bytes 26120 | tf_op jit(solution)/shard_map/ppermute | solution.py:126
  605.7 13.3 %collective-permute-start.11 = (bf16[256,1024]{1,0:T(8,128)(2,1)S(1)}, bf16[256,1024]{1,0:T(8,128)(2,1)S(1)}, u32[]{:S(2)}, u32[]{:S(2)}) collective-permute-start(bf16[256,1024]{1,0:T(8,128)(2,1)S(1)} %add_convert_fusion.21), channel_id=1, source_target_pairs={{0,4},{1,5},{2,6},{3,7},{4,0},{5,1},{6,2},{7,3},{8,12},{9,13},{10,... | collective-permute-start | bytes 1572872 | tf_op jit(solution)/shard_map/ppermute | solution.py:126
  611.9 9.2 %copy-start.40 = (bf16[512,1024]{1,0:T(8,128)(2,1)S(1)}, bf16[512,1024]{1,0:T(8,128)(2,1)}, u32[]{:S(2)}) copy-start(bf16[512,1024]{1,0:T(8,128)(2,1)} %copy-done.39) | copy-start | bytes 3145732
  611.9 9.2 %copy-start.47 = (bf16[512,512]{1,0:T(8,128)(2,1)S(1)}, bf16[512,512]{1,0:T(8,128)(2,1)}, u32[]{:S(2)}) copy-start(bf16[512,512]{1,0:T(8,128)(2,1)} %copy.239) | copy-start | bytes 1572868
  611.9 9.2 %copy-start.49 = (bf16[512,512]{1,0:T(8,128)(2,1)S(1)}, bf16[512,512]{1,0:T(8,128)(2,1)}, u32[]{:S(2)}) copy-start(bf16[512,512]{1,0:T(8,128)(2,1)} %copy-done.48) | copy-start | bytes 1572868
  611.9 83.3 %collective-permute-start.15 = (bf16[512,4608]{1,0:T(8,128)(2,1)}, bf16[512,4608]{1,0:T(8,128)(2,1)}, u32[]{:S(2)}, u32[]{:S(2)}) collective-permute-start(bf16[512,4608]{1,0:T(8,128)(2,1)} %pad_maximum_fusion), channel_id=1, source_target_pairs={{0,1},{1,0},{2,3},{3,2},{4,5},{5,4},{6,7},{7,6},{8,9},{9,8},{10,11... | collective-permute-start | bytes 14155784 | tf_op jit(solution)/shard_map/ppermute | solution.py:126
  619.2 8.6 collective-permute-start.12
  624.1 33.5 %collective-permute-start.6 = (bf16[256,2048]{1,0:T(8,128)(2,1)}, bf16[256,2048]{1,0:T(8,128)(2,1)S(1)}, u32[]{:S(2)}, u32[]{:S(2)}) collective-permute-start(bf16[256,2048]{1,0:T(8,128)(2,1)} %add_convert_fusion.12), channel_id=1, source_target_pairs={{0,2},{1,3},{2,0},{3,1},{4,6},{5,7},{6,4},{7,5},{8,10},{9,11},{10,... | collective-permute-start | bytes 3145736 | tf_op jit(solution)/shard_map/ppermute | solution.py:126
  627.9 5.2 collective-permute-start.13
  629.3 42.7 %all-to-all-start.2 = ((bf16[32,16,1024]{2,1,0:T(8,128)(2,1)}), bf16[32,16,1024]{2,1,0:T(8,128)(2,1)S(1)}, u32[]{:S(2)}, u32[]{:S(2)}) async-start(bf16[32,16,1024]{2,1,0:T(8,128)(2,1)} %bitcast.369), calls=%async_computation.2 | async-start | bytes 2097152 | tf_op jit(solution)/shard_map/all_to_all | solution.py:311
  633.1 28.8 %collective-permute-start.14 = (bf16[32,1024]{1,0:T(8,128)(2,1)S(1)}, bf16[32,1024]{1,0:T(8,128)(2,1)S(1)}, u32[]{:S(2)}, u32[]{:S(2)}) collective-permute-start(bf16[32,1024]{1,0:T(8,128)(2,1)S(1)} %add_convert_fusion.39), channel_id=1, source_target_pairs={{0,16},{1,17},{2,18},{3,19},{4,20},{5,21},{6,22},{7,23},{8,24},{9,... | collective-permute-start | bytes 196616 | tf_op jit(solution)/shard_map/ppermute | solution.py:126
  638.5 24.1 %copy-start.71 = (s32[512]{0:T(512)S(1)}, s32[512]{0:T(512)}, u32[]{:S(2)}) copy-start(s32[512]{0:T(512)} %copy-done.70) | copy-start | bytes 6148
  658.0 12.4 %collective-permute-start.7 = (bf16[128,2048]{1,0:T(8,128)(2,1)S(1)}, bf16[128,2048]{1,0:T(8,128)(2,1)S(1)}, u32[]{:S(2)}, u32[]{:S(2)}) collective-permute-start(bf16[128,2048]{1,0:T(8,128)(2,1)S(1)} %get-tuple-element.410), channel_id=1, source_target_pairs={{0,4},{1,5},{2,6},{3,7},{4,0},{5,1},{6,2},{7,3},{8,12},{9,13},{10,... | collective-permute-start | bytes 1572872 | tf_op jit(solution)/shard_map/ppermute | solution.py:126
  670.4 9.5 %copy-start.20 = (bf16[4,2,1,1,144,512]{5,4,3,2,1,0:T(8,128)(2,1)S(1)}, bf16[4,2,1,1,144,512]{5,4,3,2,1,0:T(8,128)(2,1)}, u32[]{:S(2)}) copy-start(bf16[4,2,1,1,144,512]{5,4,3,2,1,0:T(8,128)(2,1)} %get-tuple-element.391) | copy-start | bytes 3538948
  671.3 6.7 collective-permute-start.8
  678.9 14.0 %collective-permute-start.9 = (bf16[32,2048]{1,0:T(8,128)(2,1)S(1)}, bf16[32,2048]{1,0:T(8,128)(2,1)S(1)}, u32[]{:S(2)}, u32[]{:S(2)}) collective-permute-start(bf16[32,2048]{1,0:T(8,128)(2,1)S(1)} %add_convert_fusion.37), channel_id=1, source_target_pairs={{0,16},{1,17},{2,18},{3,19},{4,20},{5,21},{6,22},{7,23},{8,24},{9,... | collective-permute-start | bytes 393224 | tf_op jit(solution)/shard_map/ppermute | solution.py:126
  685.7 9.5 %slice-start.5 = ((s8[4718592]{0:T(1024)(128)(4,1)}), s8[4194304]{0:T(1024)(128)(4,1)S(1)}, s32[]{:S(2)}) async-start(s8[4718592]{0:T(1024)(128)(4,1)} %bitcast.501), calls=%async_computation.12 | async-start | bytes 8388608
  685.7 9.5 %slice-start.6 = ((s8[4718592]{0:T(1024)(128)(4,1)}), s8[524288]{0:T(1024)(128)(4,1)S(1)}, s32[]{:S(2)}) async-start(s8[4718592]{0:T(1024)(128)(4,1)} %bitcast.501), calls=%async_computation.13 | async-start | bytes 1048576
  685.7 9.5 %copy-start.80 = (bf16[1024,512]{1,0:T(8,128)(2,1)S(1)}, bf16[1024,512]{1,0:T(8,128)(2,1)}, u32[]{:S(2)}) copy-start(bf16[1024,512]{1,0:T(8,128)(2,1)} %copy-done.79) | copy-start | bytes 3145732
  685.7 54.2 %collective-permute-start.26 = (bf16[1152,1024]{1,0:T(8,128)(2,1)S(1)}, bf16[1152,1024]{1,0:T(8,128)(2,1)S(1)}, u32[]{:S(2)}, u32[]{:S(2)}) collective-permute-start(bf16[1152,1024]{1,0:T(8,128)(2,1)S(1)} %get-tuple-element.390), channel_id=1, source_target_pairs={{0,2},{1,3},{2,0},{3,1},{4,6},{5,7},{6,4},{7,5},{8,10},{9,11},{10,... | collective-permute-start | bytes 7077896 | tf_op jit(solution)/shard_map/ppermute | solution.py:126
  692.0 93.2 %collective-permute-start.21 = (bf16[256,4608]{1,0:T(8,128)(2,1)S(1)}, bf16[256,4608]{1,0:T(8,128)(2,1)S(1)}, u32[]{:S(2)}, u32[]{:S(2)}) collective-permute-start(bf16[256,4608]{1,0:T(8,128)(2,1)S(1)} %add_convert_fusion.2), channel_id=1, source_target_pairs={{0,2},{1,3},{2,0},{3,1},{4,6},{5,7},{6,4},{7,5},{8,10},{9,11},{10,... | collective-permute-start | bytes 7077896 | tf_op jit(solution)/shard_map/ppermute | solution.py:126
  698.7 89.2 %collective-permute-start.16 = (bf16[256,4608]{1,0:T(8,128)(2,1)S(1)}, bf16[256,4608]{1,0:T(8,128)(2,1)S(1)}, u32[]{:S(2)}, u32[]{:S(2)}) collective-permute-start(bf16[256,4608]{1,0:T(8,128)(2,1)S(1)} %add_convert_fusion.4), channel_id=1, source_target_pairs={{0,4},{1,5},{2,6},{3,7},{4,0},{5,1},{6,2},{7,3},{8,12},{9,13},{10,... | collective-permute-start | bytes 7077896 | tf_op jit(solution)/shard_map/ppermute | solution.py:126
  741.1 47.8 %collective-permute-start.27 = (bf16[4,144,1024]{2,1,0:T(8,128)(2,1)S(1)}, bf16[4,144,1024]{2,1,0:T(8,128)(2,1)S(1)}, u32[]{:S(2)}, u32[]{:S(2)}) collective-permute-start(bf16[4,144,1024]{2,1,0:T(8,128)(2,1)S(1)} %get-tuple-element.388), channel_id=1, source_target_pairs={{0,4},{1,5},{2,6},{3,7},{4,0},{5,1},{6,2},{7,3},{8,12},{9,13},{10,... | collective-permute-start | bytes 3538952 | tf_op jit(solution)/shard_map/ppermute | solution.py:126
  785.8 22.3 %collective-permute-start.22 = (bf16[128,4608]{1,0:T(8,128)(2,1)S(1)}, bf16[128,4608]{1,0:T(8,128)(2,1)S(1)}, u32[]{:S(2)}, u32[]{:S(2)}) collective-permute-start(bf16[128,4608]{1,0:T(8,128)(2,1)S(1)} %get-tuple-element.396), channel_id=1, source_target_pairs={{0,4},{1,5},{2,6},{3,7},{4,0},{5,1},{6,2},{7,3},{8,12},{9,13},{10,... | collective-permute-start | bytes 3538952 | tf_op jit(solution)/shard_map/ppermute | solution.py:126
  788.5 22.6 %collective-permute-start.17 = (bf16[128,4608]{1,0:T(8,128)(2,1)S(1)}, bf16[128,4608]{1,0:T(8,128)(2,1)S(1)}, u32[]{:S(2)}, u32[]{:S(2)}) collective-permute-start(bf16[128,4608]{1,0:T(8,128)(2,1)S(1)} %get-tuple-element.398), channel_id=1, source_target_pairs={{0,2},{1,3},{2,0},{3,1},{4,6},{5,7},{6,4},{7,5},{8,10},{9,11},{10,... | collective-permute-start | bytes 3538952 | tf_op jit(solution)/shard_map/ppermute | solution.py:126
  789.4 23.4 %collective-permute-start.28 = (bf16[2,144,1024]{2,1,0:T(8,128)(2,1)S(1)}, bf16[2,144,1024]{2,1,0:T(8,128)(2,1)S(1)}, u32[]{:S(2)}, u32[]{:S(2)}) collective-permute-start(bf16[2,144,1024]{2,1,0:T(8,128)(2,1)S(1)} %get-tuple-element.400), channel_id=1, source_target_pairs={{0,8},{1,9},{2,10},{3,11},{4,12},{5,13},{6,14},{7,15},{8,0},{9,1},... | collective-permute-start | bytes 1769480 | tf_op jit(solution)/shard_map/ppermute | solution.py:126
  808.3 24.5 %collective-permute-start.23 = (bf16[64,4608]{1,0:T(8,128)(2,1)S(1)}, bf16[64,4608]{1,0:T(8,128)(2,1)S(1)}, u32[]{:S(2)}, u32[]{:S(2)}) collective-permute-start(bf16[64,4608]{1,0:T(8,128)(2,1)S(1)} %get-tuple-element.402), channel_id=1, source_target_pairs={{0,8},{1,9},{2,10},{3,11},{4,12},{5,13},{6,14},{7,15},{8,0},{9,1},... | collective-permute-start | bytes 1769480 | tf_op jit(solution)/shard_map/ppermute | solution.py:126
  811.4 31.4 %collective-permute-start.18 = (bf16[64,4608]{1,0:T(8,128)(2,1)S(1)}, bf16[64,4608]{1,0:T(8,128)(2,1)S(1)}, u32[]{:S(2)}, u32[]{:S(2)}) collective-permute-start(bf16[64,4608]{1,0:T(8,128)(2,1)S(1)} %get-tuple-element.404), channel_id=1, source_target_pairs={{0,8},{1,9},{2,10},{3,11},{4,12},{5,13},{6,14},{7,15},{8,0},{9,1},... | collective-permute-start | bytes 1769480 | tf_op jit(solution)/shard_map/ppermute | solution.py:126
  812.8 48.2 %collective-permute-start.29 = (bf16[1,144,1024]{2,1,0:T(8,128)(2,1)S(1)}, bf16[1,144,1024]{2,1,0:T(8,128)(2,1)S(1)}, u32[]{:S(2)}, u32[]{:S(2)}) collective-permute-start(bf16[1,144,1024]{2,1,0:T(8,128)(2,1)S(1)} %fusion.151), channel_id=1, source_target_pairs={{0,16},{1,17},{2,18},{3,19},{4,20},{5,21},{6,22},{7,23},{8,24},{9,... | collective-permute-start | bytes 884744 | tf_op jit(solution)/shard_map/ppermute | solution.py:126
  833.0 22.6 %collective-permute-start.24 = (bf16[32,4608]{1,0:T(8,128)(2,1)S(1)}, bf16[32,4608]{1,0:T(8,128)(2,1)S(1)}, u32[]{:S(2)}, u32[]{:S(2)}) collective-permute-start(bf16[32,4608]{1,0:T(8,128)(2,1)S(1)} %add_convert_fusion.26), channel_id=1, source_target_pairs={{0,16},{1,17},{2,18},{3,19},{4,20},{5,21},{6,22},{7,23},{8,24},{9,... | collective-permute-start | bytes 884744 | tf_op jit(solution)/shard_map/ppermute | solution.py:126
  842.8 19.2 %copy-start.1 = (bf16[512,1024]{1,0:T(8,128)(2,1)S(1)}, bf16[512,1024]{1,0:T(8,128)(2,1)}, u32[]{:S(2)}) copy-start(bf16[512,1024]{1,0:T(8,128)(2,1)} %param.23) | copy-start | bytes 3145732
  842.9 17.2 %collective-permute-start.19 = (bf16[32,4608]{1,0:T(8,128)(2,1)S(1)}, bf16[32,4608]{1,0:T(8,128)(2,1)S(1)}, u32[]{:S(2)}, u32[]{:S(2)}) collective-permute-start(bf16[32,4608]{1,0:T(8,128)(2,1)S(1)} %add_convert_fusion.28), channel_id=1, source_target_pairs={{0,16},{1,17},{2,18},{3,19},{4,20},{5,21},{6,22},{7,23},{8,24},{9,... | collective-permute-start | bytes 884744 | tf_op jit(solution)/shard_map/ppermute | solution.py:126
  (66 other events, 198.4 us)
Sparse Core Ops, SparseCore 0:
  12.2 97.5 all-gather.3
  113.3 123.8 all-gather.5
  240.1 80.2 all-gather.7

commit v2 on v1

v2 whole, which is shorter than its diff:
```python
import jax
import jax.numpy as jnp
from jax import lax
from jax.experimental import pallas as pl
from jax.experimental.pallas import tpu as pltpu
from jax.sharding import PartitionSpec as P

QUERY_HEADS = 16
KEY_VALUE_HEADS = 8
HEAD_SIZE = 64
WINDOW_TOKENS = 256
MICRO = 2


EPS = 1e-05
THETA = 1000000.0
NEGATIVE = -1e30


def tdot(left, right):
    return lax.dot_general(
        left, right, (((0,), (0,)), ((), ())), preferred_element_type=jnp.float32
    )


def ntdot(left, right):
    return lax.dot_general(
        left, right, (((1,), (1,)), ((), ())), preferred_element_type=jnp.float32
    )


def norm_rows(values, gain):
    inverse = lax.rsqrt(jnp.mean(values * values, axis=-1, keepdims=True) + EPS)
    return (values * inverse * gain, inverse)


def norm_back(grad, values, inverse, gain):
    scaled = grad * gain
    grad_values = inverse * scaled - values * inverse * inverse * inverse * jnp.mean(
        scaled * values, axis=-1, keepdims=True
    )
    return (grad_values, grad * values * inverse)


def tables(positions, half_dim):
    steps_index = jnp.arange(half_dim, dtype=jnp.float32)
    inverse_freq = THETA ** (-steps_index / half_dim)
    angles = positions.astype(jnp.float32)[:, None] * inverse_freq[None, :]
    return (jnp.cos(angles), jnp.sin(angles))


def layout(lengths_row, feature_width):
    places = jnp.arange(feature_width, dtype=jnp.int32)
    ends = jnp.cumsum(lengths_row)
    segment = jnp.sum((places[:, None] >= ends[None, :]).astype(jnp.int32), axis=1)
    starts = ends - lengths_row
    picked = segment[:, None] == jnp.arange(lengths_row.shape[0], dtype=jnp.int32)[None, :]
    begins = jnp.sum(jnp.where(picked, starts[None, :], 0), axis=1)
    allowed = (segment[:, None] == segment[None, :]) & (places[None, :] <= places[:, None])
    return (places - begins, allowed)


CHUNKS = 32
FLOOR = pl.CostEstimate(flops=0, bytes_accessed=1 << 16, transcendentals=0)
ANYWHERE = pl.BlockSpec(memory_space=pltpu.HBM)
F32 = jnp.float32
LOW = jnp.bfloat16


def label(body):
    parts = [p for p in body.__qualname__.split('.') if not p.startswith('<') and p != 'body']
    return '_'.join(parts).lower()


def run(body, operands, in_specs, out_shape, out_specs, grid=(1,), scratch=(), deps=(), vmem=60, aliases=None, carry=()):
    deps = tuple(deps)
    carry = tuple(carry)
    inputs = len(operands)
    skipped = inputs + len(deps) + len(carry)
    single = not isinstance(out_shape, (list, tuple))
    out_shape = [out_shape] if single else list(out_shape)
    out_specs = [out_specs] if single else list(out_specs)
    outputs = len(out_shape)

    def wrapped(*refs):
        body(*refs[:inputs], *refs[skipped : skipped + outputs], *refs[skipped + outputs + len(carry) :])

    aliases = dict(aliases or {})
    for i in range(len(carry)):
        aliases[inputs + len(deps) + i] = outputs + i
    outs = pl.pallas_call(
        wrapped,
        grid=grid,
        in_specs=list(in_specs) + [ANYWHERE] * (len(deps) + len(carry)),
        out_specs=out_specs + [ANYWHERE] * len(carry),
        out_shape=out_shape + [jax.ShapeDtypeStruct(c.shape, c.dtype) for c in carry],
        scratch_shapes=list(scratch),
        input_output_aliases=aliases,
        compiler_params=pltpu.CompilerParams(vmem_limit_bytes=vmem << 20),
        cost_estimate=FLOOR,
        name=label(body),
    )(*operands, *deps, *carry)
    own = outs[0] if single else outs[:outputs]
    return (own, list(outs[outputs:])) if carry else own


def hop(values, bit, count):
    return lax.ppermute(values, "dp", [(i, i ^ (1 << bit)) for i in range(count)])


def position_masks(order, count):
    bits = len(order)
    position = jnp.arange(count, dtype=jnp.int32)
    mask = jnp.zeros_like(position)
    for at, bit in enumerate(order):
        mask = mask | (((position >> (bits - 1 - at)) & 1) << bit)
    return mask


def owner_select(place, order, count, width):
    share = width // count
    column = jnp.arange(width, dtype=jnp.int32)
    feature = (place ^ jnp.repeat(position_masks(order, count), share)) * share + column % share
    return (jnp.arange(width, dtype=jnp.int32)[:, None] == feature[None, :]).astype(LOW)


def select_rows(selects, values, deps=()):
    rows, width = values[0].shape

    def body(*refs):
        count = len(values)
        for i in range(count):
            refs[2 * count][i] = lax.dot_general(
                refs[i][...], refs[count + i][...], (((0,), (1,)), ((), ())), preferred_element_type=F32
            ).astype(LOW)

    whole = lambda a: pl.BlockSpec(a.shape, lambda i: (0, 0))
    operands = [*selects, *values]
    return run(
        body,
        operands,
        [whole(a) for a in operands],
        jax.ShapeDtypeStruct((len(values), width, rows), LOW),
        pl.BlockSpec((len(values), width, rows), lambda i: (0, 0, 0)),
        deps=deps,
    )


def order_blocks(blocks, place, order):
    count, share, tokens = blocks.shape
    rest = order[1:-2]

    def mask_of(t):
        mask = 0
        for at, bit in enumerate(rest):
            mask = mask | (((t >> (len(rest) - 1 - at)) & 1) << bit)
        return mask

    def body(place_ref, blocks_ref, out_ref):
        low = place_ref[0] & 7
        for first in range(2):
            for second in range(2):
                for third in range(2):
                    mask = first | (second << order[-2]) | (third << order[-1])
                    out_ref[first, 0, 2 * second + third] = blocks_ref[low ^ mask]

    ordered = pl.pallas_call(
        body,
        grid_spec=pltpu.PrefetchScalarGridSpec(
            num_scalar_prefetch=1,
            grid=(count // 8,),
            in_specs=[
                pl.BlockSpec((8, share, tokens), lambda t, place_ref: ((place_ref[0] ^ mask_of(t)) >> 3, 0, 0))
            ],
            out_specs=pl.BlockSpec((2, 1, 4, share, tokens), lambda t, place_ref: (0, t, 0, 0, 0)),
        ),
        out_shape=jax.ShapeDtypeStruct((2, count // 8, 4, share, tokens), blocks.dtype),
        compiler_params=pltpu.CompilerParams(vmem_limit_bytes=60 << 20),
        cost_estimate=FLOOR,
        name="order_blocks",
    )(place[None], blocks)
    return ordered.reshape(1, count * share, tokens)


def join(pairs, deps=()):
    operands = []
    shapes = []
    finals = []
    cuts = []
    scratch = []
    for own, received, bit, at in pairs:
        lead = own.shape[:-2]
        rows, columns = own.shape[-2:]
        outer = 1
        for size in lead[:at]:
            outer *= size
        inner = 1
        for size in lead[at:]:
            inner *= size
        operands += [bit[None], own.reshape(outer, inner, rows, columns), received.reshape(outer, inner, rows, columns)]
        shapes.append(jax.ShapeDtypeStruct((outer, 2, inner, rows, columns), own.dtype))
        finals.append(lead[:at] + (2,) + lead[at:] + (rows, columns))
        scratch.append(pltpu.VMEM((2, outer, inner, rows, columns), own.dtype))
        if outer > 1:
            step = max(1, outer // 4)
            cuts.append([(pl.ds(i, step), slice(None)) for i in range(0, outer, step)])
        else:
            step = max(1, inner // 4)
            cuts.append([(slice(None), pl.ds(i, step)) for i in range(0, inner, step)])
    total = 2 * sum(len(c) for c in cuts)

    def body(*refs):
        number = len(pairs)
        outs = refs[3 * number : 4 * number]
        held = refs[4 * number : 5 * number]
        in_sems, out_sems = refs[5 * number :]
        ins = []
        writes = []
        for p in range(number):
            mine = refs[3 * p][0]
            for o, n in cuts[p]:
                for s, target in enumerate((mine, 1 - mine)):
                    k = len(ins)
                    ins.append(pltpu.make_async_copy(refs[3 * p + 1 + s].at[o, n], held[p].at[s, o, n], in_sems.at[k]))
                    writes.append(pltpu.make_async_copy(held[p].at[s, o, n], outs[p].at[o, target, n], out_sems.at[k]))
        for copy in ins:
            copy.start()
        for copy, write in zip(ins, writes):
            copy.wait()
            write.start()
        for write in writes:
            write.wait()

    smem = pl.BlockSpec(memory_space=pltpu.SMEM)
    joined = run(
        body,
        operands,
        [smem, ANYWHERE, ANYWHERE] * len(pairs),
        shapes,
        [ANYWHERE] * len(pairs),
        scratch=scratch + [pltpu.SemaphoreType.DMA((total,)), pltpu.SemaphoreType.DMA((total,))],
        deps=deps,
    )
    return [j.reshape(f) for j, f in zip(joined, finals)]


class Gather:
    def __init__(self, values, orders, place, count):
        self.values = list(values)
        self.orders = orders
        self.have = [[], []]
        self.place = place
        self.count = count
        self.step = 0
        self.send()

    def send(self):
        if self.step < len(self.orders[0]):
            self.received = [hop(v, o[self.step], self.count) for v, o in zip(self.values, self.orders)]

    def take(self, deps=()):
        pairs = []
        for i in range(2):
            bit = self.orders[i][self.step]
            at = sum(1 for other in self.have[i] if other > bit)
            pairs.append((self.values[i], self.received[i], (self.place >> bit) & 1, at))
            self.have[i].append(bit)
        self.values = join(pairs, deps)
        self.step += 1
        self.send()
        return self.values[0]

    def result(self):
        return [v.reshape(-1, v.shape[-1]) for v in self.values]


class Slot:
    def __init__(self, count):
        self.count = count
        self.pending = []

    def run(self, take, sends, *args, **kwargs):
        carried = [array for _, _, arrays in self.pending for array in arrays]
        kept = [d for d in kwargs.pop("deps", ()) if not any(d is c for c in carried)]
        outs = run(*args, carry=carried, deps=kept, **kwargs)
        if carried:
            outs, carried = outs
            fresh = []
            for owner, bits, arrays in self.pending:
                fresh.append((owner, bits, carried[: len(arrays)]))
                carried = carried[len(arrays) :]
            self.pending = fresh
        self.pending.append(take(outs))
        return sends(outs)

    def hold(self, array):
        self.pending.append((None, (), [array]))

    def start(self):
        held = []
        for owner, bits, arrays in self.pending:
            if owner is None:
                held += arrays
            else:
                owner.received = [hop(a, b, self.count) for a, b in zip(arrays, bits)]
        self.pending = []
        return held


class Scatter:
    def __init__(self, lefts, pick, rights, tile, orders):
        self.lefts, self.pick, self.rights, self.tile = lefts, pick, rights, tile
        self.orders = orders
        self.half = lefts.shape[1] // 2
        self.tokens = lefts.shape[2]
        self.step = 0
        self.starts = [sum(r[2] for r in rights[:i]) for i in range(len(rights))]
        self.tiles = sum(r[2] for r in rights)

    def within(self, part):
        start, tiles = self.starts[part], self.rights[part][2]
        return lambda t: jnp.clip(t - start, 0, tiles - 1)

    def specs(self, rows_at):
        tile, tokens, pick = self.tile, self.tokens, self.pick
        specs = [pl.BlockSpec((1, self.half, tokens), lambda t: (pick(t), rows_at, 0))]
        for part, (_, first, _) in enumerate(self.rights):
            at = self.within(part)
            specs.append(pl.BlockSpec((tokens, tile), lambda t, at=at, first=first: (0, first + at(t))))
        return specs

    def each(self, act):
        t = pl.program_id(0)
        for part, (_, _, tiles) in enumerate(self.rights):
            start = self.starts[part]
            pl.when((t >= start) & (t < start + tiles))(lambda part=part: act(part))

    def bits(self, number):
        return [order[self.step] for order in self.orders[:number]]

    def first(self, slot, deps=()):
        number = len(self.rights)

        def body(left_ref, *refs):
            def act(part):
                refs[number][...] = jnp.dot(left_ref[0], refs[part][...], preferred_element_type=F32).astype(LOW)

            self.each(act)

        bits = self.bits(1)
        self.step = 1
        return slot.run(
            lambda sent: (self, bits, [sent]),
            lambda sent: sent,
            body,
            [self.lefts, *[r[0] for r in self.rights]],
            self.specs(1),
            jax.ShapeDtypeStruct((self.half, self.tiles * self.tile), LOW),
            pl.BlockSpec((self.half, self.tile), lambda t: (0, t)),
            grid=(self.tiles,),
            deps=deps,
        )

    def keep(self, outs):
        self.kept = [outs[i] for i in range(1, len(outs), 2)]
        return self.kept[0]

    def second(self, slot, deps=()):
        tile, quarter, number = self.tile, self.half // 2, len(self.rights)

        def body(left_ref, *refs):
            got_ref = refs[number]
            outs = refs[number + 1 :]

            def act(part):
                total = jnp.dot(left_ref[0], refs[part][...], preferred_element_type=F32) + got_ref[...].astype(F32)
                total = total.astype(LOW)
                outs[2 * part][...] = total[quarter:]
                outs[2 * part + 1][...] = total[:quarter]

            self.each(act)

        shapes = []
        specs = []
        for part, (_, _, tiles) in enumerate(self.rights):
            at = self.within(part)
            shapes += [jax.ShapeDtypeStruct((quarter, tiles * tile), LOW)] * 2
            specs += [pl.BlockSpec((quarter, tile), lambda t, at=at: (0, at(t)))] * 2
        bits = self.bits(number)
        self.step = 2
        return slot.run(
            lambda outs: (self, bits, [outs[i] for i in range(0, len(outs), 2)]),
            self.keep,
            body,
            [self.lefts, *[r[0] for r in self.rights], self.received[0]],
            self.specs(0) + [pl.BlockSpec((self.half, tile), lambda t: (0, t))],
            shapes,
            specs,
            grid=(self.tiles,),
            deps=deps,
        )

    def add(self, slot, deps=()):
        number = len(self.kept)
        joined = len(self.kept[0].shape) == 3
        joining = not joined and self.step >= 3
        rows, columns = self.kept[0].shape[-2:]
        parts = self.kept[0].shape[0] if joined else number
        half = rows // 2
        cut = columns
        while cut % 256 == 0 and parts * rows * cut > 700 * 1024:
            cut //= 2

        def body(*refs):
            ins, outs = refs[: 2 * number], refs[2 * number :]
            for p in range(number):
                total = (ins[2 * p][...].astype(F32) + ins[2 * p + 1][...].astype(F32)).astype(LOW)
                if joined:
                    outs[0][...] = total[:, half:]
                    outs[1][...] = total[:, :half]
                elif joining:
                    outs[0][p] = total[half:]
                    outs[1][p] = total[:half]
                else:
                    outs[2 * p][...] = total[half:]
                    outs[2 * p + 1][...] = total[:half]

        operands = [a for pair in zip(self.kept, self.received) for a in pair]
        flat = lambda size: pl.BlockSpec((size, cut), lambda t: (0, t))
        deep = lambda size: pl.BlockSpec((parts, size, cut), lambda t: (0, 0, t))
        if joined or joining:
            shapes = [jax.ShapeDtypeStruct((parts, half, columns), LOW)] * 2
            specs = [deep(half)] * 2
        else:
            shapes = [jax.ShapeDtypeStruct((half, columns), LOW)] * (2 * number)
            specs = [flat(half)] * (2 * number)
        bits = self.bits(1 if joined or joining else number)
        self.step += 1
        return slot.run(
            lambda outs: (self, bits, [outs[i] for i in range(0, len(outs), 2)]),
            self.keep,
            body,
            operands,
            [deep(rows) if joined else flat(rows)] * len(operands),
            shapes,
            specs,
            grid=(columns // cut,),
            deps=deps,
        )


class Merged(Scatter):
    def __init__(self, slot, scatters, units, deps=()):
        first = scatters[0]
        self.orders = first.orders
        self.step = first.step
        number = len(first.kept)
        halves = [scatter.kept[0].shape[0] // 2 for scatter in scatters]
        columns = [scatter.kept[0].shape[1] for scatter in scatters]
        operands = []
        for scatter in scatters:
            for kept, received in zip(scatter.kept, scatter.received):
                operands += [kept, received]
        if units is None:
            shape = (number, halves[0], sum(columns))
        else:
            owners = halves[0] // units[0]
            shape = (number, owners * sum(units), columns[0])

        def body(*refs):
            ins, outs = refs[: len(operands)], refs[len(operands) :]
            for i in range(len(scatters)):
                half = halves[i]
                for p in range(number):
                    at = 2 * (i * number + p)
                    total = (ins[at][...].astype(F32) + ins[at + 1][...].astype(F32)).astype(LOW)
                    for out_ref, begin in zip(outs, (half, 0)):
                        if units is None:
                            left = sum(columns[:i])
                            out_ref[p, :, left : left + columns[i]] = total[begin : begin + half]
                            continue
                        for owner in range(owners):
                            top = owner * sum(units) + sum(units[:i])
                            source = begin + owner * units[i]
                            out_ref[p, top : top + units[i], :] = total[source : source + units[i]]

        bits = self.bits(1)
        self.step += 1
        out = jax.ShapeDtypeStruct(shape, LOW)
        slot.run(
            lambda outs: (self, bits, [outs[0]]),
            self.keep,
            body,
            operands,
            [pl.BlockSpec(a.shape, lambda t: (0, 0)) for a in operands],
            [out, out],
            [pl.BlockSpec(shape, lambda t: (0, 0, 0))] * 2,
            deps=deps,
        )


def finish(scatters, places, shapes, deps=()):
    operands = []
    for scatter in scatters:
        operands += [scatter.kept[0], scatter.received[0]]

    def body(*refs):
        ins, outs = refs[: len(operands)], refs[len(operands) :]
        totals = {}
        for which, part, from_rows, from_columns, out, rows, columns in places:
            if (which, part) not in totals:
                totals[which, part] = ins[2 * which][part].astype(F32) + ins[2 * which + 1][part].astype(F32)
            outs[out][rows, columns] = totals[which, part][from_rows, from_columns]

    return run(
        body,
        operands,
        [pl.BlockSpec(a.shape, lambda t: (0, 0, 0)) for a in operands],
        [jax.ShapeDtypeStruct(shape, F32) for shape in shapes],
        [pl.BlockSpec(shape, lambda t: (0, 0)) for shape in shapes],
        deps=deps,
    )


def head_sum(values, ones):
    high = values.astype(jnp.bfloat16)
    rest = (values - high.astype(jnp.float32)).astype(jnp.bfloat16)
    return jnp.dot(high, ones, preferred_element_type=jnp.float32) + jnp.dot(
        rest, ones, preferred_element_type=jnp.float32
    )


def swap_halves(values):
    lane = lax.broadcasted_iota(jnp.int32, values.shape, 1)
    return jnp.where(
        lane % HEAD_SIZE < HEAD_SIZE // 2,
        pltpu.roll(values, 2 * HEAD_SIZE - HEAD_SIZE // 2, 1),
        pltpu.roll(values, HEAD_SIZE // 2, 1),
    )


def lower_lanes(values):
    return lax.broadcasted_iota(jnp.int32, values.shape, 1) < HEAD_SIZE


def head_ones():
    row = lax.broadcasted_iota(jnp.int32, (2 * HEAD_SIZE, 2 * HEAD_SIZE), 0) // HEAD_SIZE
    column = lax.broadcasted_iota(jnp.int32, (2 * HEAD_SIZE, 2 * HEAD_SIZE), 1) // HEAD_SIZE
    return (row == column).astype(jnp.bfloat16)


def spread(pair, which):
    other = pltpu.roll(pair.astype(jnp.float32), HEAD_SIZE, 1)
    pair = pair.astype(jnp.float32)
    left, right = (pair, other) if which == 0 else (other, pair)
    low = lower_lanes(pair)
    zero = jnp.zeros_like(pair)
    return jnp.concatenate([jnp.where(low, left, zero), jnp.where(low, zero, right)], axis=0).astype(jnp.bfloat16)


def spread_ones(rows):
    row = lax.broadcasted_iota(jnp.int32, (2 * rows, 2 * HEAD_SIZE), 0) // rows
    column = lax.broadcasted_iota(jnp.int32, (2 * rows, 2 * HEAD_SIZE), 1) // HEAD_SIZE
    return (row == column).astype(jnp.bfloat16)


def attend_kernel(q_ref, k_ref, v_ref, cos_ref, sin_ref, qg_ref, kg_ref, bias_ref, qs_ref, kl_ref, vl_ref, att_ref):
    ones = head_ones()
    cosine = cos_ref[...]
    sine = sin_ref[...]
    bias = bias_ref[0]
    bias = jnp.concatenate([bias, bias], axis=1)
    rows = cosine.shape[0]
    tail = spread_ones(rows)

    def turn(values, gain):
        inverse = lax.rsqrt(head_sum(values * values, ones) * (1.0 / HEAD_SIZE) + EPS)
        normed = values * inverse * gain
        return normed * cosine + swap_halves(normed) * sine

    keys = turn(k_ref[...], kg_ref[...]).astype(jnp.bfloat16)
    kl_ref[...] = keys
    values = v_ref[...].astype(jnp.bfloat16)
    vl_ref[...] = values
    for which in range(2):
        lanes = slice(which * 2 * HEAD_SIZE, (which + 1) * 2 * HEAD_SIZE)
        queries = turn(q_ref[:, lanes], qg_ref[...]).astype(jnp.bfloat16) * (HEAD_SIZE**-0.5)
        queries = queries.astype(jnp.bfloat16)
        qs_ref[:, lanes] = queries
        scores = ntdot(queries, spread(keys, which)) + bias
        exponent = jnp.exp(scores).astype(jnp.bfloat16)
        both = jnp.concatenate([spread(values, which), tail], axis=1)
        mixed = jnp.dot(exponent, both, preferred_element_type=jnp.float32)
        att_ref[:, lanes] = (mixed[:, : 2 * HEAD_SIZE] / mixed[:, 2 * HEAD_SIZE :]).astype(jnp.bfloat16)


def attend(proj, cosine, sine, query_gain, key_gain, bias, deps=()):
    window = bias.shape[1]
    rows = proj.shape[0]
    pair = 2 * HEAD_SIZE
    pairs = KEY_VALUE_HEADS // 2
    k_at = QUERY_HEADS * HEAD_SIZE // pair
    gain = pl.BlockSpec((1, pair), lambda m, p: (0, 0))
    table = pl.BlockSpec((window, pair), lambda m, p: (m, 0))
    wide = pl.BlockSpec((window, 2 * pair), lambda m, p: (m, p))
    thin = pl.BlockSpec((window, pair), lambda m, p: (m, p))
    return run(
        attend_kernel,
        [proj, proj, proj, cosine, sine, query_gain, key_gain, bias],
        [
            wide,
            pl.BlockSpec((window, pair), lambda m, p: (m, k_at + p)),
            pl.BlockSpec((window, pair), lambda m, p: (m, k_at + pairs + p)),
            table,
            table,
            gain,
            gain,
            pl.BlockSpec((1, window, window), lambda m, p: (m, 0, 0)),
        ],
        [
            jax.ShapeDtypeStruct((rows, QUERY_HEADS * HEAD_SIZE), LOW),
            jax.ShapeDtypeStruct((rows, KEY_VALUE_HEADS * HEAD_SIZE), LOW),
            jax.ShapeDtypeStruct((rows, KEY_VALUE_HEADS * HEAD_SIZE), LOW),
            jax.ShapeDtypeStruct((rows, QUERY_HEADS * HEAD_SIZE), LOW),
        ],
        [wide, thin, thin, wide],
        grid=(MICRO, pairs),
        deps=deps,
    )


def attend_back_kernel(
    q_ref, k_ref, qs_ref, kl_ref, vl_ref, att_ref, da_ref, cos_ref, sin_ref, qg_ref, kg_ref, bias_ref,
    room_ref, grad_ref, ov_ref, gains_ref,
):
    pair = pl.program_id(1)
    ones = head_ones()
    cosine = cos_ref[...]
    sine = sin_ref[...]
    bias = bias_ref[0]
    bias = jnp.concatenate([bias, bias], axis=1)
    rows = cosine.shape[0]
    tail = spread_ones(rows)
    low = jnp.bfloat16

    def unturn(grad, values, gain):
        inverse = lax.rsqrt(head_sum(values * values, ones) * (1.0 / HEAD_SIZE) + EPS)
        back = grad * cosine - swap_halves(grad) * sine
        scaled = back * gain
        mean = head_sum(scaled * values, ones) * (1.0 / HEAD_SIZE)
        grad_values = inverse * scaled - values * (inverse * inverse * inverse) * mean
        return (grad_values.astype(low), jnp.sum(back * values * inverse, axis=0, keepdims=True))

    keys = kl_ref[...]
    values = vl_ref[...]
    query_sum = jnp.zeros((1, 2 * HEAD_SIZE), jnp.float32)
    key_grads = []
    value_grads = []
    for which in range(2):
        lanes = slice(which * 2 * HEAD_SIZE, (which + 1) * 2 * HEAD_SIZE)
        queries = qs_ref[:, lanes]
        grads = da_ref[:, lanes]
        wide_keys = spread(keys, which)
        exponent = jnp.exp(ntdot(queries, wide_keys) + bias)
        exponent_low = exponent.astype(low)
        inverse = 1.0 / jnp.dot(exponent_low, tail, preferred_element_type=jnp.float32)
        grads_wide = grads.astype(jnp.float32)
        inner = (-grads_wide * att_ref[:, lanes].astype(jnp.float32)).astype(low)
        shifted = ntdot(
            jnp.concatenate([grads, inner], axis=1), jnp.concatenate([spread(values, which), tail], axis=1)
        )
        score_grads = (exponent * shifted).astype(low)
        query_grad = jnp.dot(score_grads, wide_keys, preferred_element_type=jnp.float32) * (
            inverse * (HEAD_SIZE**-0.5)
        )
        grad_low, gain_rows = unturn(query_grad, q_ref[:, lanes], qg_ref[...])
        at = pl.multiple_of(pair * (4 * HEAD_SIZE) + which * 2 * HEAD_SIZE, 2 * HEAD_SIZE)
        grad_ref[:, pl.ds(at, 2 * HEAD_SIZE)] = grad_low
        query_sum = query_sum + gain_rows
        key_grads.append(tdot(score_grads, (queries.astype(jnp.float32) * inverse).astype(low)))
        value_grads.append(tdot(exponent_low, (grads_wide * inverse).astype(low)))

    def fold(parts):
        first = parts[0][:rows] + pltpu.roll(parts[0][rows:], HEAD_SIZE, 1)
        second = pltpu.roll(parts[1][:rows], HEAD_SIZE, 1) + parts[1][rows:]
        return jnp.where(lower_lanes(first), first, second)

    at = pl.multiple_of(pair * (2 * HEAD_SIZE), 2 * HEAD_SIZE)
    ov_ref[:, pl.ds(at, 2 * HEAD_SIZE)] = fold(value_grads).astype(low)
    grad_low, key_sum = unturn(fold(key_grads), k_ref[...], kg_ref[...])
    at = pl.multiple_of(QUERY_HEADS * HEAD_SIZE + pair * (2 * HEAD_SIZE), 2 * HEAD_SIZE)
    grad_ref[:, pl.ds(at, 2 * HEAD_SIZE)] = grad_low

    @pl.when((pl.program_id(0) == 0) & (pair == 0))
    def _():
        gains_ref[...] = jnp.zeros_like(gains_ref)

    gains_ref[0:1, :] += query_sum
    gains_ref[1:2, :] += key_sum


def attend_back(proj, saved, att_grads, grad_ov, cosine, sine, query_gain, key_gain, bias, deps=()):
    window = bias.shape[1]
    rows = proj.shape[0]
    pair = 2 * HEAD_SIZE
    pairs = KEY_VALUE_HEADS // 2
    q_width = QUERY_HEADS * HEAD_SIZE
    k_width = KEY_VALUE_HEADS * HEAD_SIZE
    k_at = q_width // pair
    gain = pl.BlockSpec((1, pair), lambda m, p: (0, 0))
    table = pl.BlockSpec((window, pair), lambda m, p: (m, 0))
    wide = pl.BlockSpec((window, 2 * pair), lambda m, p: (m, p))
    thin = pl.BlockSpec((window, pair), lambda m, p: (m, p))
    queries, keys, values, attended = saved
    return run(
        attend_back_kernel,
        [proj, proj, queries, keys, values, attended, att_grads, cosine, sine, query_gain, key_gain, bias, grad_ov],
        [
            wide,
            pl.BlockSpec((window, pair), lambda m, p: (m, k_at + p)),
            wide,
            thin,
            thin,
            wide,
            wide,
            table,
            table,
            gain,
            gain,
            pl.BlockSpec((1, window, window), lambda m, p: (m, 0, 0)),
            ANYWHERE,
        ],
        [
            jax.ShapeDtypeStruct((rows, q_width + k_width), LOW),
            jax.ShapeDtypeStruct(grad_ov.shape, LOW),
            jax.ShapeDtypeStruct((8, pair), jnp.float32),
        ],
        [
            pl.BlockSpec((window, q_width + k_width), lambda m, p: (m, 0)),
            pl.BlockSpec((window, k_width), lambda m, p: (m, q_width // k_width)),
            pl.BlockSpec((8, pair), lambda m, p: (0, 0)),
        ],
        grid=(MICRO, pairs),
        deps=deps,
        aliases={12: 1},
    )


def project(tokens, gain, query_key, value_out, deps=()):
    rows, width = tokens.shape
    qk_width = query_key.shape[1]
    v_width = KEY_VALUE_HEADS * HEAD_SIZE
    tile = WINDOW_TOKENS

    def body(x_ref, gain_ref, qk_ref, v_ref, n1_ref, proj_ref):
        normed, _ = norm_rows(x_ref[...].astype(F32), gain_ref[...])
        normed = normed.astype(LOW)
        n1_ref[...] = normed
        proj_ref[:, :qk_width] = jnp.dot(normed, qk_ref[...], preferred_element_type=F32)
        proj_ref[:, qk_width:] = jnp.dot(normed, v_ref[...], preferred_element_type=F32)

    return run(
        body,
        [tokens, gain, query_key, value_out],
        [
            pl.BlockSpec((tile, width), lambda i: (i, 0)),
            pl.BlockSpec((1, width), lambda i: (0, 0)),
            pl.BlockSpec((width, qk_width), lambda i: (0, 0)),
            pl.BlockSpec((width, v_width), lambda i: (0, width // v_width)),
        ],
        [jax.ShapeDtypeStruct((rows, width), LOW), jax.ShapeDtypeStruct((rows, qk_width + v_width), F32)],
        [
            pl.BlockSpec((tile, width), lambda i: (i, 0)),
            pl.BlockSpec((tile, qk_width + v_width), lambda i: (i, 0)),
        ],
        grid=(rows // tile,),
        deps=deps,
    )


def residual(tokens, attended, value_out, gain, deps=()):
    rows, width = tokens.shape
    tile = WINDOW_TOKENS

    def body(x_ref, att_ref, out_ref, gain_ref, h1_ref, n2_ref):
        h1 = x_ref[...].astype(F32) + jnp.dot(att_ref[...], out_ref[...], preferred_element_type=F32)
        h1_ref[...] = h1
        n2_ref[...] = norm_rows(h1, gain_ref[...])[0].astype(LOW)

    row = pl.BlockSpec((tile, width), lambda i: (i, 0))
    return run(
        body,
        [tokens, attended, value_out, gain],
        [row, row, pl.BlockSpec((width, width), lambda i: (0, 0)), pl.BlockSpec((1, width), lambda i: (0, 0))],
        [jax.ShapeDtypeStruct((rows, width), F32), jax.ShapeDtypeStruct((rows, width), LOW)],
        [row, row],
        grid=(rows // tile,),
        deps=deps,
    )


def ffn_shards(w_gate, w_up, w_down, devices):
    rows, hidden = w_gate.shape
    owned, width = w_down.shape
    unit = hidden // devices
    split = unit * 5 // 9
    bounds = [(0, split), (split, unit)]
    cuts = [(end - begin) * devices for begin, end in bounds]
    down_cuts = [(owned * begin // unit, owned * end // unit) for begin, end in bounds]
    depth = [(end - begin) * width // (2 * cut) for (begin, end), cut in zip(down_cuts, cuts)]

    def body(gate_ref, up_ref, down_ref, first_ref, second_ref):
        for (begin, end), cut, (top, bottom), deep, out_ref in zip(
            bounds, cuts, down_cuts, depth, (first_ref, second_ref)
        ):
            for source_ref, at in ((gate_ref, 0), (up_ref, cut)):
                source = source_ref[...].astype(F32)
                for i in range(devices):
                    size = end - begin
                    out_ref[:rows, at + i * size : at + (i + 1) * size] = source[
                        :, i * unit + begin : i * unit + end
                    ].astype(LOW)
            for q in range((bottom - top) // deep):
                out_ref[rows:, q * width : (q + 1) * width] = down_ref[top + q * deep : top + (q + 1) * deep, :]

    whole = lambda a: pl.BlockSpec(a.shape, lambda i: (0, 0))
    shapes = [jax.ShapeDtypeStruct((rows + deep, 2 * cut), LOW) for deep, cut in zip(depth, cuts)]
    return run(
        body, [w_gate, w_up, w_down], [whole(a) for a in (w_gate, w_up, w_down)], shapes, [whole(a) for a in shapes]
    )


def ffn_shards_plain(w_gate, w_up, w_down, devices):
    chunks, rows, hidden = w_gate.shape
    width = w_down.shape[2]
    unit = hidden // devices
    split = unit * 5 // 9
    outs = []
    for begin, end in ((0, split), (split, unit)):
        columns = [
            w.reshape(chunks, rows, devices, unit)[..., begin:end].reshape(chunks, rows, -1) for w in (w_gate, w_up)
        ]
        down = w_down.reshape(chunks, -1, unit, width)[:, :, begin:end].reshape(chunks, -1, width)
        pieces = 2 * columns[0].shape[2] // width
        down = down.reshape(chunks, pieces, -1, width).transpose(0, 2, 1, 3).reshape(chunks, -1, pieces * width)
        outs.append(jnp.concatenate([jnp.concatenate(columns, axis=2), down], axis=1))
    return outs


def gather_ffn(w_gate, w_up, w_down, count):
    gather = lambda values: lax.all_gather(values, "dp", axis=0, tiled=True)
    if count == CHUNKS:
        return [
            gather(shard).reshape(CHUNKS, shard.shape[0], shard.shape[1])
            for shard in ffn_shards(w_gate, w_up, w_down, count)
        ]
    cut = lambda values: gather(values).reshape(CHUNKS, -1, values.shape[1])
    return ffn_shards_plain(cut(w_gate), cut(w_up), cut(w_down), count)


def set_down(down_ref, held):
    chunks, rows, _ = down_ref.shape
    width = held.shape[1]
    pieces = held.shape[0] // (chunks * rows)
    for i in range(chunks):
        for q in range(pieces):
            at = (i * pieces + q) * rows
            held[at : at + rows, :] = down_ref[i, :, q * width : (q + 1) * width]


def ffn(normed, grads, weight, output, grad_normed, count, last, deps=()):
    rows, width = normed.shape
    share = width // CHUNKS
    hidden = weight.shape[2] // 2
    pieces = 2 * hidden // width
    rest = weight.shape[1] - share
    steps = 4
    tile = hidden // steps
    chunks = CHUNKS // steps
    begins = grad_normed is None

    def body(*refs):
        n2_ref, dy_ref, gate_ref, up_ref, down_ref, y_in_ref = refs[:6]
        hid_ref, dg_ref, du_ref, y_ref, dn_ref, total_y, total_n, held = refs[-8:]
        j = pl.program_id(0)

        @pl.when(j == 0)
        def _():
            total_y[...] = y_in_ref[...]
            total_n[...] = jnp.zeros_like(total_n) if begins else refs[6][...]

        set_down(down_ref, held)
        gate_weight = gate_ref[...].reshape(width, tile)
        up_weight = up_ref[...].reshape(width, tile)
        n2 = n2_ref[...]
        gate = jnp.dot(n2, gate_weight, preferred_element_type=F32)
        up = jnp.dot(n2, up_weight, preferred_element_type=F32)
        dhid = ntdot(dy_ref[...], held[...])
        sig = jax.nn.sigmoid(gate)
        silu = gate * sig
        hid = (silu * up).astype(LOW)
        dgate = (dhid * up * (sig + silu * (1.0 - sig))).astype(LOW)
        dup = (dhid * silu).astype(LOW)
        hid_ref[...] = hid.T
        dg_ref[...] = dgate
        du_ref[...] = dup
        total_y[...] += jnp.dot(hid, held[...], preferred_element_type=F32)
        total_n[...] += ntdot(dgate, gate_weight) + ntdot(dup, up_weight)

        @pl.when(j == pl.num_programs(0) - 1)
        def _():
            dn_ref[...] = total_n[...]
            if last:
                for m in range(MICRO):
                    part = total_y[m * WINDOW_TOKENS : (m + 1) * WINDOW_TOKENS].astype(LOW)
                    y_ref[:, m] = part.reshape(count, WINDOW_TOKENS // count, width)
            else:
                y_ref[...] = total_y[...]

    whole = pl.BlockSpec((rows, width), lambda j: (0, 0))
    cut = pl.BlockSpec((rows, tile), lambda j: (0, j))
    shape = jax.ShapeDtypeStruct((rows, hidden), LOW)
    sums = jax.ShapeDtypeStruct((rows, width), F32)
    dealt = (count, MICRO, WINDOW_TOKENS // count, width)
    return run(
        body,
        [normed, grads, weight, weight, weight, output] + ([] if begins else [grad_normed]),
        [
            whole,
            whole,
            pl.BlockSpec((CHUNKS, share, tile), lambda j: (0, 0, j)),
            pl.BlockSpec((CHUNKS, share, tile), lambda j: (0, 0, j + steps)),
            pl.BlockSpec((chunks, rest, pieces * width), lambda j: (j, share // rest, 0)),
            whole,
        ]
        + ([] if begins else [whole]),
        [
            jax.ShapeDtypeStruct((hidden, rows), LOW),
            shape,
            shape,
            jax.ShapeDtypeStruct(dealt, LOW) if last else sums,
            sums,
        ],
        [
            pl.BlockSpec((tile, rows), lambda j: (j, 0)),
            cut,
            cut,
            pl.BlockSpec(dealt, lambda j: (0, 0, 0, 0)) if last else whole,
            whole,
        ],
        grid=(steps,),
        scratch=[
            pltpu.VMEM((rows, width), F32),
            pltpu.VMEM((rows, width), F32),
            pltpu.VMEM((tile, width), LOW),
        ],
        deps=deps,
    )


def residual_back(grad_normed, resid, grads, gain, value_out, deps=()):
    rows, width = resid.shape
    v_width = KEY_VALUE_HEADS * HEAD_SIZE
    tile = WINDOW_TOKENS

    def body(dn_ref, h1_ref, dy_ref, gain_ref, out_ref, dh_ref, da_ref, datt_ref, sum_ref):
        h1 = h1_ref[...]
        _, inverse = norm_rows(h1, gain_ref[...])
        part, gain_rows = norm_back(dn_ref[...], h1, inverse, gain_ref[...])
        dh1 = dy_ref[...].astype(F32) + part
        low = dh1.astype(LOW)
        dh_ref[...] = dh1
        da_ref[...] = low
        datt_ref[...] = ntdot(low, out_ref[...]).astype(LOW)

        @pl.when(pl.program_id(0) == 0)
        def _():
            sum_ref[...] = jnp.zeros_like(sum_ref)

        sum_ref[...] += jnp.sum(gain_rows, axis=0, keepdims=True)

    row = pl.BlockSpec((tile, width), lambda i: (i, 0))
    one = pl.BlockSpec((1, width), lambda i: (0, 0))
    return run(
        body,
        [grad_normed, resid, grads, gain, value_out],
        [row, row, row, one, pl.BlockSpec((width, width), lambda i: (0, 0))],
        [
            jax.ShapeDtypeStruct((rows, width), F32),
            jax.ShapeDtypeStruct((rows, width + v_width), LOW),
            jax.ShapeDtypeStruct((rows, width), LOW),
            jax.ShapeDtypeStruct((1, width), F32),
        ],
        [row, row, row, one],
        grid=(rows // tile,),
        deps=deps,
    )


def input_back(grad_qk, grad_ov, query_key, value_out, tokens, gain, grad_resid, count, deps=()):
    rows, width = tokens.shape
    qk_width = query_key.shape[1]
    v_width = KEY_VALUE_HEADS * HEAD_SIZE
    tile = WINDOW_TOKENS
    share = tile // count

    def body(qk_ref, v_ref, wqk_ref, wv_ref, x_ref, gain_ref, dh_ref, dx_ref, sum_ref):
        grad = ntdot(qk_ref[...], wqk_ref[...]) + ntdot(v_ref[...], wv_ref[...])
        x = x_ref[...].astype(F32)
        _, inverse = norm_rows(x, gain_ref[...])
        part, gain_rows = norm_back(grad, x, inverse, gain_ref[...])
        dx_ref[:, 0] = (dh_ref[...] + part).astype(LOW).reshape(count, share, width)

        @pl.when(pl.program_id(0) == 0)
        def _():
            sum_ref[...] = jnp.zeros_like(sum_ref)

        sum_ref[...] += jnp.sum(gain_rows, axis=0, keepdims=True)

    row = pl.BlockSpec((tile, width), lambda i: (i, 0))
    one = pl.BlockSpec((1, width), lambda i: (0, 0))
    return run(
        body,
        [grad_qk, grad_ov, query_key, value_out, tokens, gain, grad_resid],
        [
            pl.BlockSpec((tile, qk_width), lambda i: (i, 0)),
            pl.BlockSpec((tile, v_width), lambda i: (i, width // v_width)),
            pl.BlockSpec((width, qk_width), lambda i: (0, 0)),
            pl.BlockSpec((width, v_width), lambda i: (0, width // v_width)),
            row,
            one,
            row,
        ],
        [jax.ShapeDtypeStruct((count, MICRO, share, width), LOW), jax.ShapeDtypeStruct((1, width), F32)],
        [pl.BlockSpec((count, 1, share, width), lambda i: (0, i, 0, 0)), one],
        grid=(rows // tile,),
        deps=deps,
    )


def deal_rows(deal, values, deps=()):
    def body(deal_ref, values_ref, out_ref):
        out_ref[...] = jnp.dot(deal_ref[...], values_ref[...], preferred_element_type=F32).astype(LOW)

    whole = lambda a: pl.BlockSpec(a.shape, lambda i: (0, 0))
    return run(
        body,
        [deal, values],
        [whole(deal), whole(values)],
        jax.ShapeDtypeStruct(values.shape, LOW),
        whole(values),
        deps=deps,
    )


def deal_back(deal, values, width, deps=()):
    def body(deal_ref, values_ref, out_ref):
        out_ref[...] = tdot(deal_ref[...], values_ref[...]).astype(LOW)

    whole = lambda a: pl.BlockSpec(a.shape, lambda i: (0, 0))
    part = pl.BlockSpec((values.shape[0], width), lambda i: (0, 0))
    return run(
        body,
        [deal, values],
        [whole(deal), part],
        jax.ShapeDtypeStruct((values.shape[0], width), LOW),
        part,
        deps=deps,
    )


def per_device(
    tokens,
    cotangent,
    route,
    lengths,
    attn_gain,
    w_query,
    key_weight,
    value_weight,
    query_gain,
    key_norm_gain,
    w_out,
    ffn_gain,
    w_gate,
    w_up,
    w_down,
):
    count = lax.axis_size("dp")
    levels = count.bit_length() - 1
    place = lax.axis_index("dp")
    window = WINDOW_TOKENS
    share = window // count
    width = tokens.shape[1]
    share_width = width // count
    q_width = QUERY_HEADS * HEAD_SIZE
    k_width = KEY_VALUE_HEADS * HEAD_SIZE
    rows = MICRO * window
    half = width // 2
    downward = list(range(levels - 1, -1, -1))
    crossed = list(range(levels - 1, 2, -1)) + [1, 2, 0]
    plain = list(range(levels))
    turned = [0, 2, 1] + list(range(3, levels))
    inward = [0] + list(range(3, levels)) + [1, 2]

    gains = jnp.pad(jnp.stack([attn_gain, ffn_gain], axis=1), ((0, 0), (0, 126)))
    ffn_one, ffn_two = gather_ffn(w_gate, w_up, w_down, count)
    attn = Gather(
        [jnp.concatenate([w_query, key_weight], axis=1), jnp.concatenate([w_out, value_weight, gains], axis=1)],
        [downward, crossed],
        place,
        count,
    )

    orders = route[0].reshape(MICRO, count, share).transpose(1, 0, 2).reshape(rows)
    deal = (orders[:, None] == jnp.arange(rows, dtype=jnp.int32)[None, :]).astype(LOW)

    def exchange(values):
        return lax.all_to_all(values, "dp", split_axis=0, concat_axis=0, tiled=True)

    def to_windows(sent):
        got = exchange(sent).reshape(count, MICRO, share, width)
        return got.transpose(1, 0, 2, 3).reshape(rows, width)

    def returned(values):
        return exchange(values.reshape(rows, values.shape[-1]))

    q_gain = jnp.tile(query_gain.astype(F32), 2)[None, :]
    k_gain = jnp.tile(key_norm_gain.astype(F32), 2)[None, :]
    layouts = [layout(lengths[m], window) for m in range(MICRO)]
    cosine_half, sine_half = tables(jnp.concatenate([l[0] for l in layouts]), HEAD_SIZE // 2)
    cosine = jnp.tile(cosine_half, (1, 4))
    sine = jnp.tile(jnp.concatenate([-sine_half, sine_half], axis=1), (1, 2))
    bias = jnp.where(jnp.stack([l[1] for l in layouts]), 0.0, NEGATIVE).astype(F32)
    select_plain = owner_select(place, plain, count, width)
    select_turned = owner_select(place, turned, count, width)

    tables_ready = [cosine, sine, bias, select_plain, select_turned]
    token = deal
    for step in range(levels):
        token = attn.take([token] + (tables_ready if step == 1 else []))
        if step == levels - 3:
            window_tokens = to_windows(deal_rows(deal, tokens, [token]))
    window_grads = to_windows(deal_rows(deal, cotangent, [token]))
    query_key, out_value = attn.result()
    gain_rows = out_value[:, width + k_width :].astype(F32)
    attn_gain_all = gain_rows[:, 0][None, :]
    ffn_gain_all = gain_rows[:, 1][None, :]

    normed_low, proj = project(window_tokens, attn_gain_all, query_key, out_value)
    queries, keys, values, attended = attend(proj, cosine, sine, q_gain, k_gain, bias)
    resid, ffn_low = residual(window_tokens, attended, out_value, ffn_gain_all)
    lefts_ffn = select_rows([select_plain, select_turned], [ffn_low, ffn_low])
    orders_pair = [plain, turned]
    slot = Slot(count)

    def ffn_sums(hidden_t, grad_gate_low, grad_up_low):
        tile = grad_gate_low.shape[1] // 2
        both = Scatter(
            lefts_ffn, lambda t: t // 2, [(grad_gate_low, 0, 2), (grad_up_low, 0, 2)], tile, orders_pair
        )
        lefts = order_blocks(hidden_t.reshape(count, -1, rows), place, inward)
        return both, Scatter(lefts, lambda t: 0, [(window_grads, 0, 2)], half, [inward])

    hid_one, dg_one, du_one, partial_output, dn_one = ffn(
        ffn_low, window_grads, ffn_one, resid, None, count, False, [lefts_ffn]
    )
    sum_one, down_one = ffn_sums(hid_one, dg_one, du_one)
    token = sum_one.first(slot, [])
    token = down_one.first(slot, [token])
    slot.start()
    lefts_attn = select_rows(
        [select_plain, select_turned, select_turned], [normed_low, attended, normed_low], [token]
    )
    token = sum_one.second(slot, [lefts_attn])
    token = down_one.second(slot, [token])
    slot.start()
    hid_two, dg_two, du_two, output, dn_two = ffn(
        ffn_low, window_grads, ffn_two, partial_output, dn_one, count, True, [token]
    )
    sum_two, down_two = ffn_sums(hid_two, dg_two, du_two)
    token = sum_two.first(slot, [dn_two])
    slot.hold(output)
    token = down_two.first(slot, [token])
    token = sum_one.add(slot, [token])
    token = down_one.add(slot, [token])
    (output,) = slot.start()
    returned_output = returned(output)
    grad_resid, grad_ov, grad_att, ffn_sum = residual_back(dn_two, resid, window_grads, ffn_gain_all, out_value, [token])
    grad_qk, grad_ov, head_gains = attend_back(
        proj, (queries, keys, values, attended), grad_att, grad_ov, cosine, sine, q_gain, k_gain, bias
    )
    sum_attn = Scatter(
        lefts_attn,
        lambda t: jnp.where(t < 3, 0, jnp.where(t < 5, 1, 2)),
        [(grad_qk, 0, 3), (grad_ov, 0, 3)],
        half,
        orders_pair,
    )
    token = sum_two.second(slot, [grad_qk])
    token = down_two.second(slot, [token, *sum_one.received, *down_one.received])
    slot.start()
    token = sum_attn.first(slot, [token])
    token = sum_one.add(slot, [token])
    slot.start()
    input_grad, attn_sum = input_back(
        grad_qk, grad_ov, query_key, out_value, window_tokens, attn_gain_all, grad_resid, count, [token]
    )
    small = jnp.concatenate(
        [
            attn_sum.reshape(count, share_width),
            ffn_sum.reshape(count, share_width),
            jnp.broadcast_to((head_gains[:2, :HEAD_SIZE] + head_gains[:2, HEAD_SIZE:]).reshape(1, -1), (count, 2 * HEAD_SIZE)),
        ],
        axis=1,
    )
    small_high = small.astype(LOW)
    small_rest = (small - small_high.astype(F32)).astype(LOW)
    beside = MICRO * share * 128
    small = jnp.concatenate([small_high, small_rest], axis=1)
    small = jnp.pad(small, ((0, 0), (0, beside - small.shape[1]))).reshape(count, MICRO, share, 128)
    input_grad = jnp.concatenate([input_grad, small], axis=3)
    slot.hold(input_grad)
    token = sum_attn.second(slot, [input_grad])
    token = sum_two.add(slot, [token, *sum_one.received])
    token = down_two.add(slot, [token])
    (input_grad,) = slot.start()
    returned_grads = returned(input_grad)
    output_rows = deal_back(deal, returned_output, width, [token])
    token = output_rows
    if sum_one.step < levels:
        token = sum_one.add(slot, [token])
    token = sum_two.add(slot, [token])
    token = sum_attn.add(slot, [token])
    owned = w_down.shape[0]
    down_split = owned * 5 // 9
    down_all = Merged(slot, [down_one, down_two], [down_split, owned - down_split], [token])
    token = down_all.kept[0]
    slot.start()
    grad_rows = deal_back(deal, returned_grads, width, [token])
    token = grad_rows
    while sum_attn.step < levels:
        for scatter in (sum_one, sum_two, down_all, sum_attn):
            if scatter.step < levels:
                token = scatter.add(slot, [token])
        slot.start()
    every = slice(None)
    unit = w_gate.shape[1] // count
    split = unit * 5 // 9
    places = []
    for which, begin, size in ((0, 0, split), (1, split, unit - split)):
        for part in range(2):
            for i in range(count):
                source = slice(i * size, (i + 1) * size)
                target = slice(i * unit + begin, i * unit + begin + size)
                places.append((which, part, every, source, part, every, target))
    places.append((2, 0, every, every, 2, every, every))
    grad_gate, grad_up, grad_down = finish(
        [sum_one, sum_two, down_all], places, [w_gate.shape, w_up.shape, w_down.shape], [token]
    )
    columns = lambda first, size: slice(first, first + size)
    grad_query, grad_key, grad_value, grad_out = finish(
        [sum_attn],
        [
            (0, 0, every, columns(0, q_width), 0, every, every),
            (0, 0, every, columns(q_width, k_width), 1, every, every),
            (0, 1, every, columns(width, k_width), 2, every, every),
            (0, 1, every, columns(0, width), 3, every, every),
        ],
        [w_query.shape, key_weight.shape, value_weight.shape, w_out.shape],
        [grad_gate],
    )
    small = jnp.sum(returned_grads[:, width:].reshape(count, -1).astype(F32), axis=0)
    small_size = 2 * share_width + 2 * HEAD_SIZE
    small = small[:small_size] + small[small_size : 2 * small_size]
    head_sums = small[2 * share_width : 2 * share_width + 2 * HEAD_SIZE]
    return (
        output_rows,
        grad_rows,
        small[:share_width],
        grad_query,
        grad_key,
        grad_value,
        head_sums[:HEAD_SIZE],
        head_sums[HEAD_SIZE:],
        grad_out,
        small[share_width : 2 * share_width],
        grad_gate,
        grad_up,
        grad_down,
    )


def solution(mesh):
    in_specs = (
        P("dp", None),
        P("dp", None),
        P("dp", None),
        P("dp", None),
        P("dp"),
        P("dp", None),
        P("dp", None),
        P("dp", None),
        P(),
        P(),
        P("dp", None),
        P("dp"),
        P("dp", None),
        P("dp", None),
        P("dp", None),
    )
    out_specs = (
        P("dp", None),
        P("dp", None),
        P("dp"),
        P("dp", None),
        P("dp", None),
        P("dp", None),
        P(),
        P(),
        P("dp", None),
        P("dp"),
        P("dp", None),
        P("dp", None),
        P("dp", None),
    )
    return jax.shard_map(
        per_device, mesh=mesh, in_specs=in_specs, out_specs=out_specs, check_vma=False
    )
```

time: 879 us -> 584 us (0.66)
  matrix products: 235 us -> 0 us
  Pallas kernels: 49.4 us -> 259 us
  waiting for transfers between devices: 361 us -> 189 us
  local copies, waits for them, and re-layouts: 83.1 us -> 29.1 us
  other arithmetic: 70.8 us -> 17 us
  starting transfers between devices: 52.7 us -> 66.9 us
    dot_general x144 -> x0, matrix products: 235 us -> none  [the longest x16 44.4 us: product_scatter(): dot = lambda left: jnp.dot(left, right, preferred_element_type=jnp.float32)]
    pallas_call x2 -> x47, Pallas kernels: 49.4 us -> 259 us  [the longest x45 252 us: run(): pl.pallas_call(wrapped, grid=grid, in_specs=list(in_specs) + [ANYWHERE] *...]
    all_gather x3 -> x2, waiting for transfers between devices: 98.7 us -> 23.4 us  [gather_ffn(): gather = lambda values: lax.all_gather(values, 'dp', axis=0, tiled=True)]
    all_to_all x4, waiting for transfers between devices: 69.6 us -> 4.52 us  [exchange(): return lax.all_to_all(values, 'dp', split_axis=0, concat_axis=0, tiled=True)]
    ppermute x30 -> x39, waiting for transfers between devices: 192 us -> 161 us  [hop(): return lax.ppermute(values, 'dp', [(i, i ^ 1 << bit) for i in range(count)])]
    ppermute x30 -> x39, starting transfers between devices: 34.4 us -> 51 us  [hop(): return lax.ppermute(values, 'dp', [(i, i ^ 1 << bit) for i in range(count)])]
    concatenate x9 -> x3, other arithmetic: 19.6 us -> 3.89 us  [the longest x1 2.36 us: per_device(): input_grad = jnp.concatenate([input_grad, small], axis=3)]
    mul x12 -> x2, local copies, waits for them, and re-layouts: 13.9 us -> 0.15 us  [owner_select(): (place ^ jnp.repeat(position_masks(order, count), share)) * share]
  transfers between devices with their start and end apart: 37 -> 45, of which waited for: 19 -> 17; matrix products, arithmetic and copies ran while one was open for 20% -> 5% of each run, Pallas kernels for 2% -> 41%
where the time goes in v2:
time: 584 us; the launch traced here: 577 us
  Pallas kernels  259 us (44%)
  waiting for transfers between devices  189 us (32%)
  starting transfers between devices  66.9 us (11%)
  local copies, waits for them, and re-layouts  29.1 us (5%)
  other arithmetic  17 us (3%)
  between operations  14.8 us (3%)
    pallas_call x45, Pallas kernels, run(): pl.pallas_call(wrapped, grid=grid, in_specs=list(in_specs) + [ANYWHERE] *...  252 us
    ppermute x39, waiting for transfers between devices, hop(): return lax.ppermute(values, 'dp', [(i, i ^ 1 << bit) for i in range(count)])  161 us
    ppermute x39, starting transfers between devices, hop(): return lax.ppermute(values, 'dp', [(i, i ^ 1 << bit) for i in range(count)])  51 us
    all_gather x2, waiting for transfers between devices, gather_ffn(): gather = lambda values: lax.all_gather(values, 'dp', axis=0, tiled=True)  23.4 us
    unnamed x83, local copies, waits for them, and re-layouts  19.6 us
    all_to_all x4, starting transfers between devices, exchange(): return lax.all_to_all(values, 'dp', split_axis=0, concat_axis=0, tiled=True)  15.8 us
  transfers between devices with their start and end apart: 45, of which 17 were waited for; matrix products, arithmetic and copies ran while one was open for 5% of the time, Pallas kernels for 41%

profile of v2, /device:TPU:0, one launch (start us, length us, event | category | flops | bytes accessed | tf_op | source)
XLA Modules:
  0.0 576.8 jit_solution(13149296680086455016)
XLA Ops:
  7.2 2.4 ffn_shards.1
  12.1 4.0 collective-permute-start
  24.4 2.3 fusion.1.refs_11_.refs_1_.refs_2_
  33.9 7.7 %collective-permute-done.2 = bf16[2,32,1536]{2,1,0:T(8,128)(2,1)S(1)} collective-permute-done((bf16[2,32,1536]{2,1,0:T(8,128)(2,1)}, bf16[2,32,1536]{2,1,0:T(8,128)(2,1)S(1)}, u32[]{:S(2)}, u32[]{:S(2)}) %collective-permute-start.2) | collective-permute-done | bytes 196640 | tf_op jit(solution)/shard_map/ppermute | solution.py:108
  41.6 4.3 collective-permute-done.3
  51.5 12.2 %collective-permute-done.4 = bf16[2,2,32,1536]{3,2,1,0:T(8,128)(2,1)S(1)} collective-permute-done((bf16[2,2,32,1536]{3,2,1,0:T(8,128)(2,1)}, bf16[2,2,32,1536]{3,2,1,0:T(8,128)(2,1)S(1)}, u32[]{:S(2)}, u32[]{:S(2)}) %collective-permute-start.4) | collective-permute-done | bytes 393248 | tf_op jit(solution)/shard_map/ppermute | solution.py:108
  63.7 6.6 %collective-permute-done.5 = bf16[2,2,32,1664]{3,2,1,0:T(8,128)(2,1)S(1)} collective-permute-done((bf16[2,2,32,1664]{3,2,1,0:T(8,128)(2,1)}, bf16[2,2,32,1664]{3,2,1,0:T(8,128)(2,1)S(1)}, u32[]{:S(2)}, u32[]{:S(2)}) %collective-permute-start.5) | collective-permute-done | bytes 426016 | tf_op jit(solution)/shard_map/ppermute | solution.py:108
  71.1 2.4 join.7
  76.5 3.1 deal_rows.2
  79.5 3.4 all-to-all-start
  82.9 26.6 %collective-permute-done.6 = bf16[2,2,2,32,1536]{4,3,2,1,0:T(8,128)(2,1)S(1)} collective-permute-done((bf16[2,2,2,32,1536]{4,3,2,1,0:T(8,128)(2,1)}, bf16[2,2,2,32,1536]{4,3,2,1,0:T(8,128)(2,1)S(1)}, u32[]{:S(2)}, u32[]{:S(2)}) %collective-permute-start.6) | collective-permute-done | bytes 786464 | tf_op jit(solution)/shard_map/ppermute | solution.py:108
  110.8 3.3 join.8
  114.7 5.9 %collective-permute-done.8 = bf16[2,2,2,2,32,1536]{5,4,3,2,1,0:T(8,128)(2,1)} collective-permute-done((bf16[2,2,2,2,32,1536]{5,4,3,2,1,0:T(8,128)(2,1)}, bf16[2,2,2,2,32,1536]{5,4,3,2,1,0:T(8,128)(2,1)}, u32[]{:S(2)}, u32[]{:S(2)}) %collective-permute-start.8) | collective-permute-done | bytes 1572896 | tf_op jit(solution)/shard_map/ppermute | solution.py:108
  121.8 5.6 join.9
  127.4 3.1 deal_rows.3
  130.5 2.3 all-to-all-done
  132.9 4.8 all-to-all-start.1
  142.0 6.7 %project.1 = (bf16[512,1024]{1,0:T(8,128)(2,1)}, f32[512,2048]{1,0:T(8,128)}) custom-call(bf16[512,1024]{1,0:T(8,128)(2,1)} %bitcast.121, f32[1,1024]{1,0:T(1,128)} %bitcast.168, bf16[1024,1536]{1,0:T(8,128)(2,1)} %bitcast.115, bf16[1024,1664]{1,0:T(8,128)(2,1)} %bitcast.109), custom_call_target="tpu_custom_call" | custom-call | bytes 65536 | tf_op jit(solution)/shard_map/project/pallas_call | solution.py:91
  148.6 11.7 %attend_kernel.1 = (bf16[512,1024]{1,0:T(8,128)(2,1)}, bf16[512,512]{1,0:T(8,128)(2,1)}, bf16[512,512]{1,0:T(8,128)(2,1)}, bf16[512,1024]{1,0:T(8,128)(2,1)}) custom-call(f32[512,2048]{1,0:T(8,128)} %get-tuple-element.154.refs_0_.refs_1_.refs_2_, f32[512,2048]{1,0:T(8,128)} %get-tuple-element.154.refs_0_.refs_1_.refs_2_, ...), custom_call_target="tpu_custom_call" | custom-call | bytes 65536 | tf_op jit(solution)/shard_map/attend_kernel/pallas_call | solution.py:91
  160.3 4.7 residual.1
  165.0 6.7 %select_rows.2.refs_6_.refs_0_ = bf16[2,1024,512]{2,1,0:T(8,128)(2,1)} custom-call(bf16[1024,1024]{1,0:T(8,128)(2,1)} %fusion.refs_10_.refs_0_, bf16[1024,1024]{1,0:T(8,128)(2,1)} %fusion.1.refs_11_.refs_1_.refs_2_, bf16[512,1024]{1,0:T(8,128)(2,1)} %get-tuple-element.156.refs_2_.refs_3_.refs_0_, bf16[512,1024]{1,0:T(8,128)(2,1)} %get-tuple-element.156.refs_2_.refs_3_.refs_0_), custom_call_target="tpu_custom_call" | custom-call | bytes 65536 | tf_op jit(solution)/shard_map/select_rows/pallas_call | solution.py:91
  174.9 27.5 %ffn.2 = (bf16[2560,512]{1,0:T(8,128)(2,1)}, bf16[512,2560]{1,0:T(8,128)(2,1)}, bf16[512,2560]{1,0:T(8,128)(2,1)}, f32[512,1024]{1,0:T(8,128)}, f32[512,1024]{1,0:T(8,128)}) custom-call(bf16[512,1024]{1,0:T(8,128)(2,1)} %get-tuple-element.156.refs_2_.refs_3_.refs_0_, bf16[512,1024]{1,0:T(8,128)(2,1)} %bitcast.101, bf16[32,48,5120]{2,1,0:T(8,128)(2,1)} %bitcast.95, ...), custom_call_target="tpu_custom_call" | custom-call | bytes 65536 | tf_op jit(solution)/shard_map/ffn/pallas_call | solution.py:91
  202.4 4.0 order_blocks.2
  206.4 7.4 %scatter_first.5.refs_2_ = bf16[512,5120]{1,0:T(8,128)(2,1)} custom-call(bf16[2,1024,512]{2,1,0:T(8,128)(2,1)} %select_rows.2.refs_6_.refs_0_, bf16[512,2560]{1,0:T(8,128)(2,1)} %get-tuple-element.160.refs_1_, bf16[512,2560]{1,0:T(8,128)(2,1)} %get-tuple-element.161.refs_2_), custom_call_target="tpu_custom_call" | custom-call | bytes 65536 | tf_op jit(solution)/shard_map/scatter_first/pallas_call | solution.py:91
  213.8 4.5 scatter_first.6
  218.9 9.2 %select_rows.3.refs_4_.refs_0_ = bf16[3,1024,512]{2,1,0:T(8,128)(2,1)} custom-call(bf16[1024,1024]{1,0:T(8,128)(2,1)} %fusion.refs_10_.refs_0_, bf16[1024,1024]{1,0:T(8,128)(2,1)} %fusion.1.refs_11_.refs_1_.refs_2_, bf16[1024,1024]{1,0:T(8,128)(2,1)} %fusion.1.refs_11_.refs_1_.refs_2_, bf16[512,1024]{1,0:T(8,128)(2,1)} %get-tuple-element.164.refs_3_.refs_5_, ...), custom_call_target="tpu_custom_call" | custom-call | bytes 65536 | tf_op jit(solution)/shard_map/select_rows/pallas_call | solution.py:91
  228.1 5.3 collective-permute-done.11.refs_3_
  233.4 8.6 %scatter_second.5 = (bf16[256,2560]{1,0:T(8,128)(2,1)}, bf16[256,2560]{1,0:T(8,128)(2,1)}, bf16[256,2560]{1,0:T(8,128)(2,1)}, bf16[256,2560]{1,0:T(8,128)(2,1)}) custom-call(bf16[2,1024,512]{2,1,0:T(8,128)(2,1)} %select_rows.2.refs_6_.refs_0_, bf16[512,2560]{1,0:T(8,128)(2,1)} %get-tuple-element.160.refs_1_, bf16[512,2560]{1,0:T(8,128)(2,1)} %get-tuple-element.161.refs_2_, ...), custom_call_target="tpu_custom_call" | custom-call | bytes 65536 | tf_op jit(solution)/shard_map/scatter_second/pallas_call | solution.py:91
  243.5 4.8 scatter_second.6
  251.8 23.4 %all-gather.5.cloned.1.call-done = bf16[1536,4096]{1,0:T(8,128)(2,1)} async-done(((bf16[48,4096]{1,0:T(8,128)(2,1)}), bf16[1536,4096]{1,0:T(8,128)(2,1)}) %all-gather.5.cloned.1.call-update) | async-done | bytes 12582928 | tf_op jit(solution)/shard_map/all_gather | solution.py:851
  275.2 21.3 %ffn.3 = (bf16[2048,512]{1,0:T(8,128)(2,1)}, bf16[512,2048]{1,0:T(8,128)(2,1)}, bf16[512,2048]{1,0:T(8,128)(2,1)}, bf16[32,2,8,1024]{3,2,1,0:T(8,128)(2,1)}, f32[512,1024]{1,0:T(8,128)}) custom-call(bf16[512,1024]{1,0:T(8,128)(2,1)} %get-tuple-element.156.refs_2_.refs_3_.refs_0_, bf16[512,1024]{1,0:T(8,128)(2,1)} %bitcast.104, ...), custom_call_target="tpu_custom_call" | custom-call | bytes 65536 | tf_op jit(solution)/shard_map/ffn/pallas_call | solution.py:91
  296.5 3.8 order_blocks.3
  300.3 6.6 %scatter_first.7.refs_2_ = bf16[512,4096]{1,0:T(8,128)(2,1)} custom-call(bf16[2,1024,512]{2,1,0:T(8,128)(2,1)} %select_rows.2.refs_6_.refs_0_, bf16[512,2048]{1,0:T(8,128)(2,1)} %get-tuple-element.177.refs_1_, bf16[512,2048]{1,0:T(8,128)(2,1)} %get-tuple-element.178.refs_2_, f32[512,1024]{1,0:T(8,128)} %get-tuple-element.179.refs_3_.refs_0_), custom_call_target="tpu_custom_call" | custom-call | bytes 65536 | tf_op jit(solution)/shard_map/scatter_first/pallas_call | solution.py:91
  307.0 3.8 scatter_first.8
  311.9 3.8 scatter_add.12
  316.9 2.9 scatter_add.13
  320.3 3.2 collective-permute-start.17
  323.8 8.7 %collective-permute-start.19 = (bf16[320,1024]{1,0:T(8,128)(2,1)}, bf16[320,1024]{1,0:T(8,128)(2,1)S(1)}, u32[]{:S(2)}, u32[]{:S(2)}) collective-permute-start(bf16[320,1024]{1,0:T(8,128)(2,1)} %get-tuple-element.203), channel_id=1, source_target_pairs={{0,16},{1,17},{2,18},{3,19},{4,20},{5,21},{6,22},{7,23},{8,24},{9,... | collective-permute-start | bytes 1966088 | tf_op jit(solution)/shard_map/ppermute | solution.py:108
  332.5 6.9 %residual_back.1 = (f32[512,1024]{1,0:T(8,128)}, bf16[512,1536]{1,0:T(8,128)(2,1)}, bf16[512,1024]{1,0:T(8,128)(2,1)}, f32[1,1024]{1,0:T(1,128)}) custom-call(f32[512,1024]{1,0:T(8,128)} %get-tuple-element.179.refs_3_.refs_0_, f32[512,1024]{1,0:T(8,128)} %get-tuple-element.158.refs_5_.refs_1_, bf16[512,1024]{1,0:T(8,128)(2,1)} %bitcast.106, ...), custom_call_target="tpu_custom_call" | custom-call | bytes 65536 | tf_op jit(solution)/shard_map/residual_back/pallas_call | solution.py:91
  339.4 18.2 %attend_back_kernel.1 = (bf16[512,1536]{1,0:T(8,128)(2,1)}, bf16[512,1536]{1,0:T(8,128)(2,1)}, f32[8,128]{1,0:T(8,128)}) custom-call(f32[512,2048]{1,0:T(8,128)} %get-tuple-element.154.refs_0_.refs_1_.refs_2_, f32[512,2048]{1,0:T(8,128)} %get-tuple-element.154.refs_0_.refs_1_.refs_2_, ...), custom_call_target="tpu_custom_call", output_to_operand_aliasing={{1}: (12, {})} | custom-call | bytes 65536 | tf_op jit(solution)/shard_map/attend_back_kernel/pallas_call | solution.py:91
  357.6 7.6 %scatter_second.7 = (bf16[256,2048]{1,0:T(8,128)(2,1)}, bf16[256,2048]{1,0:T(8,128)(2,1)}, bf16[256,2048]{1,0:T(8,128)(2,1)}, bf16[256,2048]{1,0:T(8,128)(2,1)}) custom-call(bf16[2,1024,512]{2,1,0:T(8,128)(2,1)} %select_rows.2.refs_6_.refs_0_, bf16[512,2048]{1,0:T(8,128)(2,1)} %get-tuple-element.177.refs_1_, bf16[512,2048]{1,0:T(8,128)(2,1)} %get-tuple-element.178.refs_2_, ...), custom_call_target="tpu_custom_call" | custom-call | bytes 65536 | tf_op jit(solution)/shard_map/scatter_second/pallas_call | solution.py:91
  367.2 4.2 scatter_second.8
  371.4 6.9 %scatter_first.9.refs_4_ = bf16[512,3072]{1,0:T(8,128)(2,1)} custom-call(bf16[3,1024,512]{2,1,0:T(8,128)(2,1)} %select_rows.3.refs_4_.refs_0_, bf16[512,1536]{1,0:T(8,128)(2,1)} %get-tuple-element.199.refs_4_.refs_1_.refs_0_, bf16[512,1536]{1,0:T(8,128)(2,1)} %get-tuple-element.211.refs_2_.refs_1_, bf16[512,1024]{1,0:T(8,128)(2,1)} %get-tuple-element.206.refs_3_.refs_0_), custom_call_target="tpu_custom_call" | custom-call | bytes 65536 | tf_op jit(solution)/shard_map/scatter_first/pallas_call | solution.py:91
  378.3 3.0 scatter_add.14
  381.4 2.8 all-to-all-start.2
  390.3 7.2 %input_back.1 = (bf16[32,2,8,1024]{3,2,1,0:T(8,128)(2,1)}, f32[1,1024]{1,0:T(1,128)}) custom-call(bf16[512,1536]{1,0:T(8,128)(2,1)} %get-tuple-element.199.refs_4_.refs_1_.refs_0_, bf16[512,1536]{1,0:T(8,128)(2,1)} %get-tuple-element.211.refs_2_.refs_1_, bf16[1024,1536]{1,0:T(8,128)(2,1)} %bitcast.116, bf16[1024,1664]{1,0:T(8,128)(2,1)} %bitcast.112, ...), custom_call_target="tpu_custom_call" | custom-call | bytes 65536 | tf_op jit(solution)/shard_map/input_back/pallas_call | solution.py:91
  399.7 2.4 pad_maximum_fusion.refs_4_
  402.1 7.7 %scatter_second.9 = (bf16[256,1536]{1,0:T(8,128)(2,1)}, bf16[256,1536]{1,0:T(8,128)(2,1)}, bf16[256,1536]{1,0:T(8,128)(2,1)}, bf16[256,1536]{1,0:T(8,128)(2,1)}, bf16[32,2,8,1152]{3,2,1,0:T(8,128)(2,1)}) custom-call(bf16[3,1024,512]{2,1,0:T(8,128)(2,1)} %select_rows.3.refs_4_.refs_0_, ...), custom_call_target="tpu_custom_call", output_to_operand_aliasing={{4}: (4, {})} | custom-call | bytes 65536 | tf_op jit(solution)/shard_map/scatter_second/pallas_call | solution.py:91
  409.8 30.5 %collective-permute-done.24.refs_5_.refs_1_ = bf16[2,64,2560]{2,1,0:T(8,128)(2,1)S(1)} collective-permute-done((bf16[2,64,2560]{2,1,0:T(8,128)(2,1)}, bf16[2,64,2560]{2,1,0:T(8,128)(2,1)S(1)}, u32[]{:S(2)}, u32[]{:S(2)}) %collective-permute-start.24) | collective-permute-done | bytes 655392 | tf_op jit(solution)/shard_map/ppermute | solution.py:108
  441.2 3.3 scatter_add.15
  445.4 2.6 scatter_add.16
  448.1 4.9 all-to-all-start.3
  457.1 2.8 collective-permute-start.25
  459.9 3.1 deal_back.2.refs_2_
  465.3 31.5 %collective-permute-done.28.refs_1_ = bf16[128,2048]{1,0:T(8,128)(2,1)} collective-permute-done((bf16[128,2048]{1,0:T(8,128)(2,1)S(1)}, bf16[128,2048]{1,0:T(8,128)(2,1)}, u32[]{:S(2)}, u32[]{:S(2)}) %collective-permute-start.28) | collective-permute-done | bytes 524320 | tf_op jit(solution)/shard_map/ppermute | solution.py:108
  496.7 2.7 scatter_add.18
  499.5 2.9 scatter_add.19
  505.3 2.8 merged___init__.1
  514.7 3.1 deal_back.3.refs_2_
  518.8 11.2 %collective-permute-done.33.refs_1_ = bf16[2,64,2048]{2,1,0:T(8,128)(2,1)S(1)} collective-permute-done((bf16[2,64,2048]{2,1,0:T(8,128)(2,1)}, bf16[2,64,2048]{2,1,0:T(8,128)(2,1)S(1)}, u32[]{:S(2)}, u32[]{:S(2)}) %collective-permute-start.33) | collective-permute-done | bytes 524320 | tf_op jit(solution)/shard_map/ppermute | solution.py:108
  536.7 2.4 scatter_add.22
  543.7 10.7 %collective-permute-done.34.refs_1_ = bf16[2,64,1536]{2,1,0:T(8,128)(2,1)S(1)} collective-permute-done((bf16[2,64,1536]{2,1,0:T(8,128)(2,1)}, bf16[2,64,1536]{2,1,0:T(8,128)(2,1)S(1)}, u32[]{:S(2)}, u32[]{:S(2)}) %collective-permute-start.34) | collective-permute-done | bytes 393248 | tf_op jit(solution)/shard_map/ppermute | solution.py:108
  558.5 3.0 finish.2
  561.5 5.8 collective-permute-done.35.refs_1_
  (221 shorter events, 93.1 us)
Async XLA Ops:
  7.2 11.8 %copy-start.36 = (s32[1,512]{1,0:T(1,128)S(1)}, s32[1,512]{1,0:T(1,128)}, u32[]{:S(2)}) copy-start(s32[1,512]{1,0:T(1,128)} %param.17) | copy-start | bytes 6148
  7.2 12.7 %copy-start.34 = (s32[2,4]{1,0:T(2,128)S(1)}, s32[2,4]{1,0:T(2,128)}, u32[]{:S(2)}) copy-start(s32[2,4]{1,0:T(2,128)} %param.18) | copy-start | bytes 100
  7.2 167.7 %all-gather.3.cloned.1.call-start = ((), (), s32[]{:S(2)}) async-start(), calls=%async_computation.4 | async-start | bytes 16220160 | tf_op jit(solution)/shard_map/all_gather | solution.py:851
  9.7 265.5 %all-gather.5.cloned.1.call-start = ((), (), s32[]{:S(2)}) async-start(), calls=%async_computation.5 | async-start | bytes 12976128 | tf_op jit(solution)/shard_map/all_gather | solution.py:851
  12.1 14.6 %copy-start.27 = (bf16[32,1536]{1,0:T(8,128)(2,1)}, bf16[32,1536]{1,0:T(8,128)(2,1)S(1)}, u32[]{:S(2)}) copy-start(bf16[32,1536]{1,0:T(8,128)(2,1)S(1)} %constant_dynamic-update-slice_fusion) | copy-start | bytes 294916
  12.1 15.6 %collective-permute-start = (bf16[32,1536]{1,0:T(8,128)(2,1)S(1)}, bf16[32,1536]{1,0:T(8,128)(2,1)S(1)}, u32[]{:S(2)}, u32[]{:S(2)}) collective-permute-start(bf16[32,1536]{1,0:T(8,128)(2,1)S(1)} %constant_dynamic-update-slice_fusion), channel_id=1, source_target_pairs={{0,16},{1,17},{2,18},{3,19},{4,20},{5,21},{6,22},{7,23},{8,24},{9,... | collective-permute-start | bytes 294920 | tf_op jit(solution)/shard_map/ppermute | solution.py:108
  18.4 9.3 %collective-permute-start.1 = (bf16[32,1664]{1,0:T(8,128)(2,1)S(1)}, bf16[32,1664]{1,0:T(8,128)(2,1)S(1)}, u32[]{:S(2)}, u32[]{:S(2)}) collective-permute-start(bf16[32,1664]{1,0:T(8,128)(2,1)S(1)} %get-tuple-element.277), channel_id=1, source_target_pairs={{0,16},{1,17},{2,18},{3,19},{4,20},{5,21},{6,22},{7,23},{8,24},{9,... | collective-permute-start | bytes 319496 | tf_op jit(solution)/shard_map/ppermute | solution.py:108
  30.1 11.5 %collective-permute-start.2 = (bf16[2,32,1536]{2,1,0:T(8,128)(2,1)}, bf16[2,32,1536]{2,1,0:T(8,128)(2,1)S(1)}, u32[]{:S(2)}, u32[]{:S(2)}) collective-permute-start(bf16[2,32,1536]{2,1,0:T(8,128)(2,1)} %bitcast.152), channel_id=1, source_target_pairs={{0,8},{1,9},{2,10},{3,11},{4,12},{5,13},{6,14},{7,15},{8,0},{9,1},... | collective-permute-start | bytes 589832 | tf_op jit(solution)/shard_map/ppermute | solution.py:108
  32.0 13.9 %collective-permute-start.3 = (bf16[2,32,1664]{2,1,0:T(8,128)(2,1)}, bf16[2,32,1664]{2,1,0:T(8,128)(2,1)S(1)}, u32[]{:S(2)}, u32[]{:S(2)}) collective-permute-start(bf16[2,32,1664]{2,1,0:T(8,128)(2,1)} %bitcast.161), channel_id=1, source_target_pairs={{0,8},{1,9},{2,10},{3,11},{4,12},{5,13},{6,14},{7,15},{8,0},{9,1},... | collective-permute-start | bytes 638984 | tf_op jit(solution)/shard_map/ppermute | solution.py:108
  41.6 4.3 copy-start.31
  48.6 21.7 %collective-permute-start.5 = (bf16[2,2,32,1664]{3,2,1,0:T(8,128)(2,1)}, bf16[2,2,32,1664]{3,2,1,0:T(8,128)(2,1)S(1)}, u32[]{:S(2)}, u32[]{:S(2)}) collective-permute-start(bf16[2,2,32,1664]{3,2,1,0:T(8,128)(2,1)} %bitcast.156), channel_id=1, source_target_pairs={{0,2},{1,3},{2,0},{3,1},{4,6},{5,7},{6,4},{7,5},{8,10},{9,11},{10,... | collective-permute-start | bytes 1277960 | tf_op jit(solution)/shard_map/ppermute | solution.py:108
  50.1 13.6 %collective-permute-start.4 = (bf16[2,2,32,1536]{3,2,1,0:T(8,128)(2,1)}, bf16[2,2,32,1536]{3,2,1,0:T(8,128)(2,1)S(1)}, u32[]{:S(2)}, u32[]{:S(2)}) collective-permute-start(bf16[2,2,32,1536]{3,2,1,0:T(8,128)(2,1)} %bitcast.143), channel_id=1, source_target_pairs={{0,4},{1,5},{2,6},{3,7},{4,0},{5,1},{6,2},{7,3},{8,12},{9,13},{10,... | collective-permute-start | bytes 1179656 | tf_op jit(solution)/shard_map/ppermute | solution.py:108
  63.7 6.6 %copy-start.23 = (bf16[2,2,32,1536]{3,2,1,0:T(8,128)(2,1)}, bf16[2,2,32,1536]{3,2,1,0:T(8,128)(2,1)S(1)}, u32[]{:S(2)}) copy-start(bf16[2,2,32,1536]{3,2,1,0:T(8,128)(2,1)S(1)} %collective-permute-done.4) | copy-start | bytes 1179652
  73.5 36.3 %collective-permute-start.7 = (bf16[2,2,2,32,1664]{4,3,2,1,0:T(8,128)(2,1)}, bf16[2,2,2,32,1664]{4,3,2,1,0:T(8,128)(2,1)S(1)}, u32[]{:S(2)}, u32[]{:S(2)}) collective-permute-start(bf16[2,2,2,32,1664]{4,3,2,1,0:T(8,128)(2,1)} %bitcast.148), channel_id=1, source_target_pairs={{0,4},{1,5},{2,6},{3,7},{4,0},{5,1},{6,2},{7,3},{8,12},{9,13},{10,... | collective-permute-start | bytes 2555912 | tf_op jit(solution)/shard_map/ppermute | solution.py:108
  74.9 34.6 %collective-permute-start.6 = (bf16[2,2,2,32,1536]{4,3,2,1,0:T(8,128)(2,1)}, bf16[2,2,2,32,1536]{4,3,2,1,0:T(8,128)(2,1)S(1)}, u32[]{:S(2)}, u32[]{:S(2)}) collective-permute-start(bf16[2,2,2,32,1536]{4,3,2,1,0:T(8,128)(2,1)} %bitcast.124), channel_id=1, source_target_pairs={{0,2},{1,3},{2,0},{3,1},{4,6},{5,7},{6,4},{7,5},{8,10},{9,11},{10,... | collective-permute-start | bytes 2359304 | tf_op jit(solution)/shard_map/ppermute | solution.py:108
  79.5 53.3 %all-to-all-start = ((bf16[32,16,1024]{2,1,0:T(8,128)(2,1)}), bf16[32,16,1024]{2,1,0:T(8,128)(2,1)S(1)}, u32[]{:S(2)}, u32[]{:S(2)}) async-start(bf16[32,16,1024]{2,1,0:T(8,128)(2,1)} %bitcast.135), calls=%async_computation | async-start | bytes 2097152 | tf_op jit(solution)/shard_map/all_to_all | solution.py:1119
  114.1 6.5 %collective-permute-start.9 = (bf16[2,2,2,2,32,1664]{5,4,3,2,1,0:T(8,128)(2,1)}, bf16[2,2,2,2,32,1664]{5,4,3,2,1,0:T(8,128)(2,1)S(1)}, u32[]{:S(2)}, u32[]{:S(2)}) collective-permute-start(bf16[2,2,2,2,32,1664]{5,4,3,2,1,0:T(8,128)(2,1)} %bitcast.140), channel_id=1, source_target_pairs={{0,1},{1,0},{2,3},{3,2},{4,5},{5,4},{6,7},{7,6},{8,9},{9,8},{10,11... | collective-permute-start | bytes 5111816 | tf_op jit(solution)/shard_map/ppermute | solution.py:108
  114.2 6.4 %collective-permute-start.8 = (bf16[2,2,2,2,32,1536]{5,4,3,2,1,0:T(8,128)(2,1)}, bf16[2,2,2,2,32,1536]{5,4,3,2,1,0:T(8,128)(2,1)}, u32[]{:S(2)}, u32[]{:S(2)}) collective-permute-start(bf16[2,2,2,2,32,1536]{5,4,3,2,1,0:T(8,128)(2,1)} %bitcast.128), channel_id=1, source_target_pairs={{0,1},{1,0},{2,3},{3,2},{4,5},{5,4},{6,7},{7,6},{8,9},{9,8},{10,11... | collective-permute-start | bytes 4718600 | tf_op jit(solution)/shard_map/ppermute | solution.py:108
  120.6 1.2 copy-start.9
  130.5 7.1 %copy-start.38 = (bf16[64]{0:T(256)(128)(2,1)S(1)}, bf16[64]{0:T(256)(128)(2,1)}, u32[]{:S(2)}) copy-start(bf16[64]{0:T(256)(128)(2,1)} %param.23) | copy-start | bytes 388
  130.5 7.7 %copy-start.39 = (bf16[64]{0:T(256)(128)(2,1)S(1)}, bf16[64]{0:T(256)(128)(2,1)}, u32[]{:S(2)}) copy-start(bf16[64]{0:T(256)(128)(2,1)} %param.24) | copy-start | bytes 388
  132.9 41.0 %all-to-all-start.1 = ((bf16[32,16,1024]{2,1,0:T(8,128)(2,1)}), bf16[32,16,1024]{2,1,0:T(8,128)(2,1)S(1)}, u32[]{:S(2)}, u32[]{:S(2)}) async-start(bf16[32,16,1024]{2,1,0:T(8,128)(2,1)} %bitcast.137), calls=%async_computation.1 | async-start | bytes 2097152 | tf_op jit(solution)/shard_map/all_to_all | solution.py:1119
  218.3 15.1 %collective-permute-start.11 = (bf16[512,5120]{1,0:T(8,128)(2,1)}, bf16[512,5120]{1,0:T(8,128)(2,1)}, u32[]{:S(2)}, u32[]{:S(2)}) collective-permute-start(bf16[512,5120]{1,0:T(8,128)(2,1)} %get-tuple-element.163), channel_id=1, source_target_pairs={{0,1},{1,0},{2,3},{3,2},{4,5},{5,4},{6,7},{7,6},{8,9},{9,8},{10,11... | collective-permute-start | bytes 15728648 | tf_op jit(solution)/shard_map/ppermute | solution.py:108
  218.6 23.5 %collective-permute-start.10 = (bf16[1280,1024]{1,0:T(8,128)(2,1)}, bf16[1280,1024]{1,0:T(8,128)(2,1)S(1)}, u32[]{:S(2)}, u32[]{:S(2)}) collective-permute-start(bf16[1280,1024]{1,0:T(8,128)(2,1)} %get-tuple-element.162.refs_6_), channel_id=1, source_target_pairs={{0,1},{1,0},{2,3},{3,2},{4,5},{5,4},{6,7},{7,6},{8,9},{9,8},{10,11... | collective-permute-start | bytes 7864328 | tf_op jit(solution)/shard_map/ppermute | solution.py:108
  242.0 1.5 copy-start.4
  248.3 62.5 %collective-permute-start.13 = (bf16[256,2560]{1,0:T(8,128)(2,1)}, bf16[256,2560]{1,0:T(8,128)(2,1)S(1)}, u32[]{:S(2)}, u32[]{:S(2)}) collective-permute-start(bf16[256,2560]{1,0:T(8,128)(2,1)} %get-tuple-element.170), channel_id=1, source_target_pairs={{0,2},{1,3},{2,0},{3,1},{4,6},{5,7},{6,4},{7,5},{8,10},{9,11},{10,... | collective-permute-start | bytes 3932168 | tf_op jit(solution)/shard_map/ppermute | solution.py:108
  250.2 60.6 %collective-permute-start.14 = (bf16[256,2560]{1,0:T(8,128)(2,1)}, bf16[256,2560]{1,0:T(8,128)(2,1)}, u32[]{:S(2)}, u32[]{:S(2)}) collective-permute-start(bf16[256,2560]{1,0:T(8,128)(2,1)} %get-tuple-element.172), channel_id=1, source_target_pairs={{0,4},{1,5},{2,6},{3,7},{4,0},{5,1},{6,2},{7,3},{8,12},{9,13},{10,... | collective-permute-start | bytes 3932168 | tf_op jit(solution)/shard_map/ppermute | solution.py:108
  251.8 63.9 %collective-permute-start.12 = (bf16[640,1024]{1,0:T(8,128)(2,1)}, bf16[640,1024]{1,0:T(8,128)(2,1)S(1)}, u32[]{:S(2)}, u32[]{:S(2)}) collective-permute-start(bf16[640,1024]{1,0:T(8,128)(2,1)} %get-tuple-element.169), channel_id=1, source_target_pairs={{0,8},{1,9},{2,10},{3,11},{4,12},{5,13},{6,14},{7,15},{8,0},{9,1},... | collective-permute-start | bytes 3932168 | tf_op jit(solution)/shard_map/ppermute | solution.py:108
  310.8 1.1 copy-start.11
  315.8 1.1 copy-start.10
  319.8 37.8 %collective-permute-start.16 = (bf16[512,4096]{1,0:T(8,128)(2,1)}, bf16[512,4096]{1,0:T(8,128)(2,1)}, u32[]{:S(2)}, u32[]{:S(2)}) collective-permute-start(bf16[512,4096]{1,0:T(8,128)(2,1)} %get-tuple-element.192), channel_id=1, source_target_pairs={{0,1},{1,0},{2,3},{3,2},{4,5},{5,4},{6,7},{7,6},{8,9},{9,8},{10,11... | collective-permute-start | bytes 12582920 | tf_op jit(solution)/shard_map/ppermute | solution.py:108
  319.8 45.5 %collective-permute-start.15 = (bf16[1024,1024]{1,0:T(8,128)(2,1)}, bf16[1024,1024]{1,0:T(8,128)(2,1)S(1)}, u32[]{:S(2)}, u32[]{:S(2)}) collective-permute-start(bf16[1024,1024]{1,0:T(8,128)(2,1)} %get-tuple-element.191), channel_id=1, source_target_pairs={{0,1},{1,0},{2,3},{3,2},{4,5},{5,4},{6,7},{7,6},{8,9},{9,8},{10,11... | collective-permute-start | bytes 6291464 | tf_op jit(solution)/shard_map/ppermute | solution.py:108
  320.3 44.9 %collective-permute-start.17 = (bf16[128,2560]{1,0:T(8,128)(2,1)}, bf16[128,2560]{1,0:T(8,128)(2,1)S(1)}, u32[]{:S(2)}, u32[]{:S(2)}) collective-permute-start(bf16[128,2560]{1,0:T(8,128)(2,1)} %get-tuple-element.201), channel_id=1, source_target_pairs={{0,4},{1,5},{2,6},{3,7},{4,0},{5,1},{6,2},{7,3},{8,12},{9,13},{10,... | collective-permute-start | bytes 1966088 | tf_op jit(solution)/shard_map/ppermute | solution.py:108
  323.5 41.7 %collective-permute-start.18 = (bf16[128,2560]{1,0:T(8,128)(2,1)}, bf16[128,2560]{1,0:T(8,128)(2,1)S(1)}, u32[]{:S(2)}, u32[]{:S(2)}) collective-permute-start(bf16[128,2560]{1,0:T(8,128)(2,1)} %get-tuple-element.202), channel_id=1, source_target_pairs={{0,2},{1,3},{2,0},{3,1},{4,6},{5,7},{6,4},{7,5},{8,10},{9,11},{10,... | collective-permute-start | bytes 1966088 | tf_op jit(solution)/shard_map/ppermute | solution.py:108
  323.8 41.4 %collective-permute-start.19 = (bf16[320,1024]{1,0:T(8,128)(2,1)}, bf16[320,1024]{1,0:T(8,128)(2,1)S(1)}, u32[]{:S(2)}, u32[]{:S(2)}) collective-permute-start(bf16[320,1024]{1,0:T(8,128)(2,1)} %get-tuple-element.203), channel_id=1, source_target_pairs={{0,16},{1,17},{2,18},{3,19},{4,20},{5,21},{6,22},{7,23},{8,24},{9,... | collective-permute-start | bytes 1966088 | tf_op jit(solution)/shard_map/ppermute | solution.py:108
  365.2 1.2 copy-start.5
  365.3 1.9 copy-start.8
  381.3 3.4 copy-start.35
  381.3 5.8 %copy-start.13 = (bf16[256,2048]{1,0:T(8,128)(2,1)S(1)}, bf16[256,2048]{1,0:T(8,128)(2,1)}, u32[]{:S(2)}) copy-start(bf16[256,2048]{1,0:T(8,128)(2,1)} %get-tuple-element.208) | copy-start | bytes 3145732
  381.3 8.8 %copy-start.37 = (f32[8,128]{1,0:T(8,128)S(1)}, f32[8,128]{1,0:T(8,128)}, u32[]{:S(2)}) copy-start(f32[8,128]{1,0:T(8,128)} %get-tuple-element.219) | copy-start | bytes 12292
  381.3 20.8 %collective-permute-start.23 = (bf16[512,3072]{1,0:T(8,128)(2,1)}, bf16[512,3072]{1,0:T(8,128)(2,1)}, u32[]{:S(2)}, u32[]{:S(2)}) collective-permute-start(bf16[512,3072]{1,0:T(8,128)(2,1)} %get-tuple-element.213), channel_id=1, source_target_pairs={{0,1},{1,0},{2,3},{3,2},{4,5},{5,4},{6,7},{7,6},{8,9},{9,8},{10,11... | collective-permute-start | bytes 9437192 | tf_op jit(solution)/shard_map/ppermute | solution.py:108
  381.4 66.7 %all-to-all-start.2 = ((bf16[32,16,1024]{2,1,0:T(8,128)(2,1)}), bf16[32,16,1024]{2,1,0:T(8,128)(2,1)S(1)}, u32[]{:S(2)}, u32[]{:S(2)}) async-start(bf16[32,16,1024]{2,1,0:T(8,128)(2,1)} %bitcast.68), calls=%async_computation.2 | async-start | bytes 2097152 | tf_op jit(solution)/shard_map/all_to_all | solution.py:1119
  385.4 59.0 %collective-permute-start.20 = (bf16[512,1024]{1,0:T(8,128)(2,1)}, bf16[512,1024]{1,0:T(8,128)(2,1)S(1)}, u32[]{:S(2)}, u32[]{:S(2)}) collective-permute-start(bf16[512,1024]{1,0:T(8,128)(2,1)} %get-tuple-element.207), channel_id=1, source_target_pairs={{0,8},{1,9},{2,10},{3,11},{4,12},{5,13},{6,14},{7,15},{8,0},{9,1},... | collective-permute-start | bytes 3145736 | tf_op jit(solution)/shard_map/ppermute | solution.py:108
  387.1 53.2 %collective-permute-start.21 = (bf16[256,2048]{1,0:T(8,128)(2,1)S(1)}, bf16[256,2048]{1,0:T(8,128)(2,1)}, u32[]{:S(2)}, u32[]{:S(2)}) collective-permute-start(bf16[256,2048]{1,0:T(8,128)(2,1)S(1)} %copy-done.13), channel_id=1, source_target_pairs={{0,2},{1,3},{2,0},{3,1},{4,6},{5,7},{6,4},{7,5},{8,10},{9,11},{10,... | collective-permute-start | bytes 3145736 | tf_op jit(solution)/shard_map/ppermute | solution.py:108
  388.6 51.7 %collective-permute-start.22 = (bf16[256,2048]{1,0:T(8,128)(2,1)}, bf16[256,2048]{1,0:T(8,128)(2,1)}, u32[]{:S(2)}, u32[]{:S(2)}) collective-permute-start(bf16[256,2048]{1,0:T(8,128)(2,1)} %get-tuple-element.210), channel_id=1, source_target_pairs={{0,4},{1,5},{2,6},{3,7},{4,0},{5,1},{6,2},{7,3},{8,12},{9,13},{10,... | collective-permute-start | bytes 3145736 | tf_op jit(solution)/shard_map/ppermute | solution.py:108
  399.0 41.4 %collective-permute-start.24 = (bf16[2,64,2560]{2,1,0:T(8,128)(2,1)}, bf16[2,64,2560]{2,1,0:T(8,128)(2,1)S(1)}, u32[]{:S(2)}, u32[]{:S(2)}) collective-permute-start(bf16[2,64,2560]{2,1,0:T(8,128)(2,1)} %get-tuple-element.221), channel_id=1, source_target_pairs={{0,8},{1,9},{2,10},{3,11},{4,12},{5,13},{6,14},{7,15},{8,0},{9,1},... | collective-permute-start | bytes 1966088 | tf_op jit(solution)/shard_map/ppermute | solution.py:108
  448.1 4.9 copy-start.2
  448.1 8.3 %copy-start.18 = (bf16[128,2048]{1,0:T(8,128)(2,1)S(1)}, bf16[128,2048]{1,0:T(8,128)(2,1)}, u32[]{:S(2)}) copy-start(bf16[128,2048]{1,0:T(8,128)(2,1)} %get-tuple-element.237) | copy-start | bytes 1572868
  448.1 11.8 %copy-start.1 = (bf16[32,16,1024]{2,1,0:T(8,128)(2,1)}, bf16[32,16,1024]{2,1,0:T(8,128)(2,1)S(1)}, u32[]{:S(2)}) copy-start(bf16[32,16,1024]{2,1,0:T(8,128)(2,1)S(1)} %all-to-all-done.2) | copy-start | bytes 3145732
  448.1 65.6 %all-to-all-start.3 = ((bf16[32,16,1152]{2,1,0:T(8,128)(2,1)}), bf16[32,16,1152]{2,1,0:T(8,128)(2,1)S(1)}, u32[]{:S(2)}, u32[]{:S(2)}) async-start(bf16[32,16,1152]{2,1,0:T(8,128)(2,1)} %bitcast.113), calls=%async_computation.3 | async-start | bytes 2359296 | tf_op jit(solution)/shard_map/all_to_all | solution.py:1119
  453.0 46.5 %collective-permute-start.26 = (bf16[256,1536]{1,0:T(8,128)(2,1)S(1)}, bf16[256,1536]{1,0:T(8,128)(2,1)}, u32[]{:S(2)}, u32[]{:S(2)}) collective-permute-start(bf16[256,1536]{1,0:T(8,128)(2,1)S(1)} %copy-done.2), channel_id=1, source_target_pairs={{0,2},{1,3},{2,0},{3,1},{4,6},{5,7},{6,4},{7,5},{8,10},{9,11},{10,... | collective-permute-start | bytes 2359304 | tf_op jit(solution)/shard_map/ppermute | solution.py:108
  455.0 44.5 %collective-permute-start.27 = (bf16[256,1536]{1,0:T(8,128)(2,1)}, bf16[256,1536]{1,0:T(8,128)(2,1)}, u32[]{:S(2)}, u32[]{:S(2)}) collective-permute-start(bf16[256,1536]{1,0:T(8,128)(2,1)} %get-tuple-element.236), channel_id=1, source_target_pairs={{0,4},{1,5},{2,6},{3,7},{4,0},{5,1},{6,2},{7,3},{8,12},{9,13},{10,... | collective-permute-start | bytes 2359304 | tf_op jit(solution)/shard_map/ppermute | solution.py:108
  456.4 40.3 %collective-permute-start.28 = (bf16[128,2048]{1,0:T(8,128)(2,1)S(1)}, bf16[128,2048]{1,0:T(8,128)(2,1)}, u32[]{:S(2)}, u32[]{:S(2)}) collective-permute-start(bf16[128,2048]{1,0:T(8,128)(2,1)S(1)} %copy-done.18), channel_id=1, source_target_pairs={{0,4},{1,5},{2,6},{3,7},{4,0},{5,1},{6,2},{7,3},{8,12},{9,13},{10,... | collective-permute-start | bytes 1572872 | tf_op jit(solution)/shard_map/ppermute | solution.py:108
  457.0 39.8 %collective-permute-start.29 = (bf16[128,2048]{1,0:T(8,128)(2,1)}, bf16[128,2048]{1,0:T(8,128)(2,1)}, u32[]{:S(2)}, u32[]{:S(2)}) collective-permute-start(bf16[128,2048]{1,0:T(8,128)(2,1)} %get-tuple-element.239), channel_id=1, source_target_pairs={{0,2},{1,3},{2,0},{3,1},{4,6},{5,7},{6,4},{7,5},{8,10},{9,11},{10,... | collective-permute-start | bytes 1572872 | tf_op jit(solution)/shard_map/ppermute | solution.py:108
  457.1 47.4 %collective-permute-start.25 = (bf16[256,1024]{1,0:T(8,128)(2,1)}, bf16[256,1024]{1,0:T(8,128)(2,1)S(1)}, u32[]{:S(2)}, u32[]{:S(2)}) collective-permute-start(bf16[256,1024]{1,0:T(8,128)(2,1)} %get-tuple-element.233), channel_id=1, source_target_pairs={{0,16},{1,17},{2,18},{3,19},{4,20},{5,21},{6,22},{7,23},{8,24},{9,... | collective-permute-start | bytes 1572872 | tf_op jit(solution)/shard_map/ppermute | solution.py:108
  508.1 24.7 %collective-permute-start.32 = (bf16[1,288,1024]{2,1,0:T(8,128)(2,1)}, bf16[1,288,1024]{2,1,0:T(8,128)(2,1)S(1)}, u32[]{:S(2)}, u32[]{:S(2)}) collective-permute-start(bf16[1,288,1024]{2,1,0:T(8,128)(2,1)} %get-tuple-element.254), channel_id=1, source_target_pairs={{0,2},{1,3},{2,0},{3,1},{4,6},{5,7},{6,4},{7,5},{8,10},{9,11},{10,... | collective-permute-start | bytes 1769480 | tf_op jit(solution)/shard_map/ppermute | solution.py:108
  509.6 20.4 %collective-permute-start.33 = (bf16[2,64,2048]{2,1,0:T(8,128)(2,1)}, bf16[2,64,2048]{2,1,0:T(8,128)(2,1)S(1)}, u32[]{:S(2)}, u32[]{:S(2)}) collective-permute-start(bf16[2,64,2048]{2,1,0:T(8,128)(2,1)} %get-tuple-element.255), channel_id=1, source_target_pairs={{0,8},{1,9},{2,10},{3,11},{4,12},{5,13},{6,14},{7,15},{8,0},{9,1},... | collective-permute-start | bytes 1572872 | tf_op jit(solution)/shard_map/ppermute | solution.py:108
  509.6 26.2 %collective-permute-start.30 = (bf16[128,1536]{1,0:T(8,128)(2,1)}, bf16[128,1536]{1,0:T(8,128)(2,1)S(1)}, u32[]{:S(2)}, u32[]{:S(2)}) collective-permute-start(bf16[128,1536]{1,0:T(8,128)(2,1)} %get-tuple-element.251), channel_id=1, source_target_pairs={{0,4},{1,5},{2,6},{3,7},{4,0},{5,1},{6,2},{7,3},{8,12},{9,13},{10,... | collective-permute-start | bytes 1179656 | tf_op jit(solution)/shard_map/ppermute | solution.py:108
  511.1 24.8 %collective-permute-start.31 = (bf16[128,1536]{1,0:T(8,128)(2,1)}, bf16[128,1536]{1,0:T(8,128)(2,1)S(1)}, u32[]{:S(2)}, u32[]{:S(2)}) collective-permute-start(bf16[128,1536]{1,0:T(8,128)(2,1)} %get-tuple-element.253), channel_id=1, source_target_pairs={{0,2},{1,3},{2,0},{3,1},{4,6},{5,7},{6,4},{7,5},{8,10},{9,11},{10,... | collective-permute-start | bytes 1179656 | tf_op jit(solution)/shard_map/ppermute | solution.py:108
  511.6 46.0 %collective-permute-start.36 = (bf16[2,32,2560]{2,1,0:T(8,128)(2,1)}, bf16[2,32,2560]{2,1,0:T(8,128)(2,1)S(1)}, u32[]{:S(2)}, u32[]{:S(2)}) collective-permute-start(bf16[2,32,2560]{2,1,0:T(8,128)(2,1)} %get-tuple-element.265), channel_id=1, source_target_pairs={{0,16},{1,17},{2,18},{3,19},{4,20},{5,21},{6,22},{7,23},{8,24},{9,... | collective-permute-start | bytes 983048 | tf_op jit(solution)/shard_map/ppermute | solution.py:108
  539.1 15.3 %collective-permute-start.34 = (bf16[2,64,1536]{2,1,0:T(8,128)(2,1)}, bf16[2,64,1536]{2,1,0:T(8,128)(2,1)S(1)}, u32[]{:S(2)}, u32[]{:S(2)}) collective-permute-start(bf16[2,64,1536]{2,1,0:T(8,128)(2,1)} %get-tuple-element.262), channel_id=1, source_target_pairs={{0,8},{1,9},{2,10},{3,11},{4,12},{5,13},{6,14},{7,15},{8,0},{9,1},... | collective-permute-start | bytes 1179656 | tf_op jit(solution)/shard_map/ppermute | solution.py:108
  539.1 18.6 %collective-permute-start.37 = (bf16[2,32,2048]{2,1,0:T(8,128)(2,1)}, bf16[2,32,2048]{2,1,0:T(8,128)(2,1)S(1)}, u32[]{:S(2)}, u32[]{:S(2)}) collective-permute-start(bf16[2,32,2048]{2,1,0:T(8,128)(2,1)} %get-tuple-element.266), channel_id=1, source_target_pairs={{0,16},{1,17},{2,18},{3,19},{4,20},{5,21},{6,22},{7,23},{8,24},{9,... | collective-permute-start | bytes 786440 | tf_op jit(solution)/shard_map/ppermute | solution.py:108
  541.2 16.5 %collective-permute-start.38 = (bf16[1,144,1024]{2,1,0:T(8,128)(2,1)}, bf16[1,144,1024]{2,1,0:T(8,128)(2,1)S(1)}, u32[]{:S(2)}, u32[]{:S(2)}) collective-permute-start(bf16[1,144,1024]{2,1,0:T(8,128)(2,1)} %get-tuple-element.267), channel_id=1, source_target_pairs={{0,4},{1,5},{2,6},{3,7},{4,0},{5,1},{6,2},{7,3},{8,12},{9,13},{10,... | collective-permute-start | bytes 884744 | tf_op jit(solution)/shard_map/ppermute | solution.py:108
  557.0 10.3 %collective-permute-start.35 = (bf16[2,32,1536]{2,1,0:T(8,128)(2,1)}, bf16[2,32,1536]{2,1,0:T(8,128)(2,1)S(1)}, u32[]{:S(2)}, u32[]{:S(2)}) collective-permute-start(bf16[2,32,1536]{2,1,0:T(8,128)(2,1)} %get-tuple-element.264), channel_id=1, source_target_pairs={{0,16},{1,17},{2,18},{3,19},{4,20},{5,21},{6,22},{7,23},{8,24},{9,... | collective-permute-start | bytes 589832 | tf_op jit(solution)/shard_map/ppermute | solution.py:108
  (21 other events, 17.2 us)
Sparse Core Ops, SparseCore 0:
  10.9 157.4 all-gather.2
  171.3 103.9 all-gather.4
